TPU v7x, 128 devices: a whole 4x4x4 slice. The times are simulated.
128 devices in a mesh: inst: 16 (over x, z), tp: 8 (over y, core).
Axes of the slice: x: 4, y: 4, z: 4, core: 2. Of those that a mesh axis runs over, the one named last changes fastest.
Arguments:
- queries: bfloat16 [4, 256, 64, 128], P(None, 'inst', 'tp'), may hold values from -6 to 6
- new_keys: bfloat16 [4, 256, 8, 128], P(None, 'inst', 'tp'), may hold values from -12 to 12
- new_values: bfloat16 [4, 256, 8, 128], P(None, 'inst', 'tp'), may hold values from -16 to 16
- key_pool: bfloat16 [2048, 8, 256, 128], P('inst', 'tp'), may hold values from -6 to 6
- value_pool: bfloat16 [2048, 8, 256, 128], P('inst', 'tp'), may hold values from -6 to 6
- block_table: int32 [2048], P('inst'), may hold values from 0 to 2047, as said below
- context_len: int32 [256], P('inst'), may hold values from 1 to 2048, 327680 in all
- out_weight: bfloat16 [8192, 8192], P('tp'), may hold values from -1 to 1
Outputs:
- projected: bfloat16 [4, 256, 8192], P(None, 'inst', 'tp')
Inputs may be any that keep to these rules, and one draw needn't show every extreme that they name: `block_table`: a permutation of the slots: each slot holds exactly one block of one request; slot s lies with instance s // 128; every instance holds exactly 8 slots with blocks of the requests of each instance. `context_len`: at least one request has a full cache of 8 blocks.
All inputs are finite; a program needn't handle non-finite values.
Results may differ from a plain program's by a relative error of at most 0.0051.
Values may be sent and summed in bfloat16 or wider, within the bound.
No kernel may reach another device: no remote copies, remote signals or barrier semaphores. Data moves between devices by JAX's collectives and lax.ppermute only.
A program may use at most 128 MiB of HBM per device.

v0:
```python
import jax
import jax.numpy as jnp
from jax import lax
from jax.sharding import PartitionSpec as P

NEG = -1e30


def combine_rows(selector, peak, total, summed):
    row_peak = jnp.max(jnp.where(selector[:, :, None, None, None], peak[None], NEG), axis=1)
    target = jnp.argmax(selector, axis=0)
    factor = jnp.exp(peak - jnp.take(row_peak, target, axis=0))
    sel_f = selector.astype(jnp.float32)
    pool = peak.shape[0]
    row_total = jnp.dot(
        sel_f, (total * factor).reshape(pool, -1), precision=lax.Precision.HIGHEST
    ).reshape(row_peak.shape)
    row_out = jnp.dot(
        sel_f, (summed * factor[..., None]).reshape(pool, -1), precision=lax.Precision.HIGHEST
    )
    return (row_peak, row_total, row_out.reshape(row_peak.shape + (summed.shape[-1],)))


def on_device(
    queries, new_keys, new_values, key_pool, value_pool, block_table, context_len, out_weight
):
    drafts, req_dev, heads_loc, head = queries.shape
    pool, kv_loc, block, _ = key_pool.shape
    group = heads_loc // kv_loc
    blocks_each = block_table.shape[0] // req_dev
    n_inst = lax.axis_size("inst")
    total_req = req_dev * n_inst
    lender = lax.axis_index("inst")
    scale = head ** (-0.5)
    all_rows = lax.all_gather(queries, "inst", axis=1, tiled=True)
    tables, lengths = (
        lax.all_gather(block_table, "inst", axis=0, tiled=True),
        lax.all_gather(context_len, "inst", axis=0, tiled=True),
    )
    mine = lender * pool + jnp.arange(pool, dtype=jnp.int32)
    entries = jnp.arange(tables.shape[0], dtype=jnp.int32)
    entry = jnp.sum(jnp.where(tables[None, :] == mine[:, None], entries[None, :], 0), axis=1)
    owner = entry // blocks_each
    blockno = entry % blocks_each
    requests = jnp.arange(total_req, dtype=jnp.int32)
    member = owner[None, :] == requests[:, None]
    limit = jnp.sum(jnp.where(member, lengths[:, None], 0), axis=0)
    slot_rows = jnp.take(all_rows, owner, axis=1).reshape(drafts, pool, kv_loc, group, head)
    scores = (
        jnp.einsum("dskgh,skth->skgdt", slot_rows, key_pool, preferred_element_type=jnp.float32)
        * scale
    )
    places = blockno[:, None] * block + jnp.arange(block, dtype=jnp.int32)[None, :]
    valid = (places < limit[:, None])[:, None, None, None, :]
    peak = jnp.max(jnp.where(valid, scores, NEG), axis=-1)
    weights = jnp.exp(jnp.where(valid, scores - peak[..., None], NEG))
    total = jnp.sum(weights, axis=-1)
    summed = jnp.einsum(
        "skgdt,skth->skgdh",
        weights.astype(jnp.bfloat16),
        value_pool,
        preferred_element_type=jnp.float32,
    )
    own_rows = queries.reshape(drafts, req_dev, kv_loc, group, head)
    fresh = (
        jnp.einsum("drkgh,erkh->rkgde", own_rows, new_keys, preferred_element_type=jnp.float32)
        * scale
    )
    causal = (
        jnp.arange(drafts, dtype=jnp.int32)[None, :] <= jnp.arange(drafts, dtype=jnp.int32)[:, None]
    )
    fresh_peak = jnp.max(jnp.where(causal, fresh, NEG), axis=-1)
    fresh_weights = jnp.exp(jnp.where(causal, fresh - fresh_peak[..., None], NEG))
    fresh_total = jnp.sum(fresh_weights, axis=-1)
    fresh_out = jnp.einsum(
        "rkgde,erkh->rkgdh",
        fresh_weights.astype(jnp.bfloat16),
        new_values,
        preferred_element_type=jnp.float32,
    )
    req_peak, req_total, req_out = combine_rows(member, peak, total, summed)
    got_peak, got_total, got_out = (
        lax.all_to_all(
            req_peak.reshape(n_inst, req_dev, kv_loc, group, drafts),
            "inst",
            split_axis=0,
            concat_axis=0,
            tiled=True,
        ),
        lax.all_to_all(
            req_total.reshape(n_inst, req_dev, kv_loc, group, drafts),
            "inst",
            split_axis=0,
            concat_axis=0,
            tiled=True,
        ),
        lax.all_to_all(
            req_out.reshape(n_inst, req_dev, kv_loc, group, drafts, head),
            "inst",
            split_axis=0,
            concat_axis=0,
            tiled=True,
        ),
    )
    top = jnp.maximum(jnp.max(got_peak, axis=0), fresh_peak)
    shift = jnp.exp(got_peak - top[None])
    fresh_shift = jnp.exp(fresh_peak - top)
    denom = jnp.sum(got_total * shift, axis=0) + fresh_total * fresh_shift
    numer = jnp.sum(got_out * shift[..., None], axis=0) + fresh_out * fresh_shift[..., None]
    attended = (numer / denom[..., None]).astype(jnp.bfloat16)
    flat = attended.transpose(3, 0, 1, 2, 4).reshape(drafts * req_dev, heads_loc * head)
    partial_value = jnp.dot(flat, out_weight, preferred_element_type=jnp.float32).reshape(
        drafts, req_dev, -1
    )
    return lax.psum_scatter(partial_value, "tp", scatter_dimension=2, tiled=True).astype(
        jnp.bfloat16
    )


def solution(mesh):
    return jax.shard_map(
        on_device,
        mesh=mesh,
        in_specs=(
            P(None, "inst", "tp", None),
            P(None, "inst", "tp", None),
            P(None, "inst", "tp", None),
            P("inst", "tp", None, None),
            P("inst", "tp", None, None),
            P("inst"),
            P("inst"),
            P("tp", None),
        ),
        out_specs=P(None, "inst", "tp"),
        check_vma=False,
    )
```

profile of v0, /device:TPU:1, one launch (start us, length us, event | category | flops | bytes accessed | tf_op | source)
XLA Modules:
  0.0 215.9 jit_solution(3017901389024089836)
XLA Ops:
  6.5 0.0 copy-start
  6.5 0.0 all-gather.3.cloned.1.call-start
  6.5 0.7 all-gather.3.cloned.1.call-update
  7.3 1.2 dynamic-slice
  9.2 0.9 dynamic-update-slice
  10.0 14.5 %all-reduce = s32[256]{0:T(256)S(1)} all-reduce(s32[256]{0:T(256)S(1)} %dynamic-update-slice), channel_id=1, replica_groups=mesh['inst'=16,'tp'=8] {'inst'}, use_global_device_ids=true, to_apply=%add | all-reduce | flops 256 | bytes 2048
  24.6 15.0 %all-gather = s32[16,1,128]{2,1,0:T(1,128)S(1)} all-gather(s32[1,1,128]{2,1,0:T(1,128)} %bitcast.155), channel_id=1, replica_groups=mesh['inst'=16,'tp'=8] {'inst'}, dimensions={0}, use_global_device_ids=true | all-gather | bytes 8704 | tf_op jit(solution)/shard_map/all_gather | solution.py:37
  39.6 0.3 select_reduce_fusion.1
  39.9 0.6 iota_reduce_fusion
  40.5 0.1 select_reduce_fusion.3
  40.7 0.1 add_compare_fusion
  40.8 16.2 %all-gather.3.cloned.1.call-done = bf16[4,256,8,128]{3,2,1,0:T(8,128)(2,1)} async-done(((bf16[4,16,8,128]{3,2,1,0:T(8,128)(2,1)}), bf16[4,256,8,128]{3,2,1,0:T(8,128)(2,1)}) %all-gather.3.cloned.1.call-update) | async-done | bytes 2097168 | tf_op jit(solution)/shard_map/all_gather | solution.py:35
  57.0 2.5 %gather_fusion = bf16[128,4,8,128]{3,2,1,0:T(8,128)(2,1)S(1)} fusion(bf16[4,256,8,128]{3,2,1,0:T(8,128)(2,1)} %all-gather.3.cloned.1.call-done, s32[1024]{0:T(1024)S(1)} %pad_clamp_fusion.1), kind=kCustom, calls=%fused_computation | custom fusion | bytes 2097664 | tf_op jit(solution)/shard_map/jit(_take)/gather | solution.py:48
  59.6 8.2 %fusion.6 = (f32[128,8,4]{1,2,0:T(4,128)S(1)}, f32[128,4,8,256]{3,2,1,0:T(8,128)}) fusion(pred[128,256]{1,0:T(8,128)(4,1)S(1)} %add_compare_fusion, bf16[128,1,256,128]{3,2,1,0:T(8,128)(2,1)} %param.11, bf16[128,4,8,128]{3,2,1,0:T(8,128)(2,1)S(1)} %gather_fusion, pred[128]{0:T(512)(128)(4,1)S(1)} %get-tuple-element.9), kind=kOutput, calls=%fused_computation.11 | convolution fusion | flops 272101376 | bytes 13680768 | tf_op jit(solution)/shard_map/dskgh,skth->skgdt/dot_general | solution.py:50
  67.7 0.1 copy.91
  67.8 0.1 copy.75
  67.9 3.4 %fusion.9 = f32[128,8,4]{1,2,0:T(4,128)S(1)} fusion(f32[128,4,8,256]{3,2,1,0:T(8,128)} %get-tuple-element.12, f32[128,8,4]{1,2,0:T(4,128)S(1)} %get-tuple-element.11, pred[128,256]{1,0:T(8,128)(4,1)S(1)} %add_compare_fusion), kind=kLoop, calls=%fused_computation.15 | loop fusion | flops 4190208 | bytes 4259840 | tf_op jit(solution)/shard_map/reduce_sum | solution.py:57
  71.3 0.1 copy.90
  71.4 1.6 select_reduce_fusion
  73.0 0.8 gather_fusion.1
  73.7 0.1 copy.92
  73.8 0.2 subtract_exponential_fusion.1
  74.1 0.7 fusion.56
  74.8 0.8 reshape.398
  75.6 4.7 %all-to-all-start.2 = ((f32[16,1,512]{2,1,0:T(1,128)}), f32[16,1,512]{2,1,0:T(1,128)S(1)}, u32[]{:S(2)}, u32[]{:S(2)}) async-start(f32[16,1,512]{2,1,0:T(1,128)} %reshape.398), calls=%async_computation.2 | async-start | bytes 65536 | tf_op jit(solution)/shard_map/all_to_all | solution.py:90
  80.2 8.2 %fusion.18 = f32[128,8,4,128]{3,1,2,0:T(8,128)} fusion(bf16[128,1,256,128]{3,2,1,0:T(8,128)(2,1)} %param.12, f32[128,4,8,256]{3,2,1,0:T(8,128)} %get-tuple-element.12, f32[128,8,4]{1,2,0:T(4,128)S(1)} %get-tuple-element.11, pred[128,256]{1,0:T(8,128)(4,1)S(1)} %add_compare_fusion, f32[128,8,4]{1,2,0:T(4,128)S(1)} %subtract_exponential_fusion.1), kind=kOutput, calls=%fused_computation.24 | convolution fusion | flops 273154048 | bytes 14745600 | tf_op jit(solution)/shard_map/skgdt,skth->skgdh/dot_general | solution.py:58
  88.4 2.0 copy.76
  90.5 0.2 copy.79
  90.6 0.8 reshape.396
  91.4 0.0 all-to-all-done.2
  91.4 6.7 %all-to-all-start.1 = ((f32[16,1,512]{2,1,0:T(1,128)}), f32[16,1,512]{2,1,0:T(1,128)S(1)}, u32[]{:S(2)}, u32[]{:S(2)}) async-start(f32[16,1,512]{2,1,0:T(1,128)} %reshape.396), calls=%async_computation.1 | async-start | bytes 65536 | tf_op jit(solution)/shard_map/all_to_all | solution.py:83
  98.1 3.8 %convolution_bitcast_fusion = f32[16,16,1,8,4,128]{5,1,4,3,2,0:T(8,128)} fusion(f32[128,8,4,128]{0,3,2,1:T(8,128)S(1)} %copy.76, s32[16,16]{1,0:T(8,128)S(1)} %multiply_add_fusion.1, s32[128]{0:T(128)S(1)} %get-tuple-element.10), kind=kOutput, calls=%fused_computation.17 | convolution fusion | flops 1610645504 | bytes 6292992 | tf_op jit(solution)/shard_map/dot_general | solution.py:18
  101.9 0.0 copy-start.1
  101.9 0.0 copy-start.2
  101.9 2.6 %all-to-all-done.1 = f32[16,1,512]{2,1,0:T(1,128)S(1)} async-done(((f32[16,1,512]{2,1,0:T(1,128)}), f32[16,1,512]{2,1,0:T(1,128)S(1)}, u32[]{:S(2)}, u32[]{:S(2)}) %all-to-all-start.1) | async-done | bytes 32800 | tf_op jit(solution)/shard_map/all_to_all | solution.py:83
  104.6 4.7 %all-to-all-start = ((f32[16,16,1,8,4,128]{5,1,4,3,2,0:T(8,128)}), f32[16,16,1,8,4,128]{5,1,4,3,2,0:T(8,128)}, u32[]{:S(2)}, u32[]{:S(2)}) async-start(f32[16,16,1,8,4,128]{5,1,4,3,2,0:T(8,128)} %convolution_bitcast_fusion), calls=%async_computation | async-start | bytes 8388608 | tf_op jit(solution)/shard_map/all_to_all | solution.py:97
  109.3 0.0 reduce-scatter.2.cloned.1.call-start
  109.4 0.0 copy-done.1
  109.4 0.0 copy-done.2
  109.4 0.7 select_reduce_fusion.2
  110.1 0.1 copy.83
  110.2 0.2 fusion.35
  110.4 0.1 copy.96
  110.4 0.5 broadcast.317
  111.0 0.7 reduce.28
  111.7 0.1 reshape.399
  111.8 0.7 reduce.27
  112.6 0.1 reshape.397
  112.8 0.1 copy.84
  112.9 0.1 bitcast_reduce_fusion.1
  112.9 0.1 copy.97
  113.0 0.1 copy.88
  113.1 42.4 %all-to-all-done = f32[16,16,1,8,4,128]{5,1,4,3,2,0:T(8,128)} async-done(((f32[16,16,1,8,4,128]{5,1,4,3,2,0:T(8,128)}), f32[16,16,1,8,4,128]{5,1,4,3,2,0:T(8,128)}, u32[]{:S(2)}, u32[]{:S(2)}) %all-to-all-start) | async-done | bytes 4194336 | tf_op jit(solution)/shard_map/all_to_all | solution.py:97
  155.5 2.9 %bitcast_reduce_fusion = f32[16,8,4,128]{3,0,2,1:T(8,128)S(1)} fusion(f32[16,16,1,8,4,128]{5,1,4,3,2,0:T(8,128)} %all-to-all-done, f32[16,16,8,4]{1,3,2,0:T(4,128)S(1)} %copy.84), kind=kLoop, calls=%fused_computation.8 | loop fusion | flops 2031616 | bytes 4489216 | tf_op jit(solution)/shard_map/reduce_sum | solution.py:109
  158.4 0.0 copy-done
  158.4 0.4 fusion.26
  158.9 10.2 %fusion = f32[4,16,8192]{2,1,0:T(8,128)} fusion(bf16[1024,8192]{1,0:T(8,128)(2,1)} %param.15, bf16[4,16,1024]{2,0,1:T(4,128)(2,1)S(1)} %dot_general.41), kind=kOutput, calls=%fused_computation.2 | convolution fusion | flops 1073741824 | bytes 19005440 | tf_op jit(solution)/shard_map/dot_general | solution.py:112
  169.0 0.0 reduce-scatter.2.cloned.1.call-update
  169.0 38.4 %reduce-scatter.2.cloned.1.call-done = f32[4,16,1024]{2,1,0:T(8,128)} async-done(((f32[4,16,8192]{2,1,0:T(8,128)}), f32[4,16,1024]{2,1,0:T(8,128)}) %reduce-scatter.2.cloned.1.call-update) | async-done | bytes 262160 | tf_op jit(solution)/shard_map/reduce_scatter | solution.py:115
  207.5 1.6 convert_element_type.20
  (18 shorter events, 0.3 us)
Async XLA Ops:
  6.5 151.8 %copy-start = (bf16[4,16,1,128]{3,1,2,0:T(8,128)(2,1)S(1)}, bf16[4,16,1,128]{3,1,2,0:T(8,128)(2,1)}, u32[]{:S(2)}) copy-start(bf16[4,16,1,128]{3,1,2,0:T(8,128)(2,1)} %param.10) | copy-start | bytes 49156
  6.5 50.5 %all-gather.3.cloned.1.call-start = ((), (), s32[]{:S(2)}) async-start(), calls=%async_computation.4 | async-start | bytes 2228224 | tf_op jit(solution)/shard_map/all_gather | solution.py:35
  75.6 15.9 %all-to-all-start.2 = ((f32[16,1,512]{2,1,0:T(1,128)}), f32[16,1,512]{2,1,0:T(1,128)S(1)}, u32[]{:S(2)}, u32[]{:S(2)}) async-start(f32[16,1,512]{2,1,0:T(1,128)} %reshape.398), calls=%async_computation.2 | async-start | bytes 65536 | tf_op jit(solution)/shard_map/all_to_all | solution.py:90
  91.4 13.1 %all-to-all-start.1 = ((f32[16,1,512]{2,1,0:T(1,128)}), f32[16,1,512]{2,1,0:T(1,128)S(1)}, u32[]{:S(2)}, u32[]{:S(2)}) async-start(f32[16,1,512]{2,1,0:T(1,128)} %reshape.396), calls=%async_computation.1 | async-start | bytes 65536 | tf_op jit(solution)/shard_map/all_to_all | solution.py:83
  101.9 7.4 %copy-start.1 = (bf16[4,16,8,128]{3,2,1,0:T(8,128)(2,1)S(1)}, bf16[4,16,8,128]{3,2,1,0:T(8,128)(2,1)}, u32[]{:S(2)}) copy-start(bf16[4,16,8,128]{3,2,1,0:T(8,128)(2,1)} %param.8) | copy-start | bytes 393220
  101.9 7.4 %copy-start.2 = (bf16[4,16,1,128]{3,1,2,0:T(8,128)(2,1)S(1)}, bf16[4,16,1,128]{3,1,2,0:T(8,128)(2,1)}, u32[]{:S(2)}) copy-start(bf16[4,16,1,128]{3,1,2,0:T(8,128)(2,1)} %param.9) | copy-start | bytes 49156
  104.6 50.9 %all-to-all-start = ((f32[16,16,1,8,4,128]{5,1,4,3,2,0:T(8,128)}), f32[16,16,1,8,4,128]{5,1,4,3,2,0:T(8,128)}, u32[]{:S(2)}, u32[]{:S(2)}) async-start(f32[16,16,1,8,4,128]{5,1,4,3,2,0:T(8,128)} %convolution_bitcast_fusion), calls=%async_computation | async-start | bytes 8388608 | tf_op jit(solution)/shard_map/all_to_all | solution.py:97
  109.3 98.2 %reduce-scatter.2.cloned.1.call-start = ((), (), s32[]{:S(2)}) async-start(), calls=%async_computation.5 | async-start | bytes 2359296 | tf_op jit(solution)/shard_map/reduce_scatter | solution.py:115
Sparse Core Ops, SparseCore 0:
  9.6 47.4 all-gather.2
  169.2 38.2 reduce-scatter.1
where the time goes:
time: 219 us; the launch traced here: 216 us
  waiting for transfers between devices  100 us (46%)
  matrix products  32.2 us (15%)
  blocking collectives  29.6 us (14%)
  starting transfers between devices  16.1 us (7%)
  between operations  14.3 us (7%)
  other arithmetic  12.7 us (6%)
  local copies, waits for them, and re-layouts  10.7 us (5%)
    all_to_all x1, waiting for transfers between devices, on_device(): lax.all_to_all(req_out.reshape(n_inst, req_dev, kv_loc, group, drafts, he...  42.4 us
    reduce_scatter x1, waiting for transfers between devices, on_device(): lax.psum_scatter(partial_value, 'tp', scatter_dimension=2, tiled=True)  38.4 us
    all_gather x1, waiting for transfers between devices, on_device(): all_rows = lax.all_gather(queries, 'inst', axis=1, tiled=True)  16.2 us
    all_gather x1, blocking collectives, on_device(): lax.all_gather(block_table, 'inst', axis=0, tiled=True)  15 us
    unnamed x1, blocking collectives  14.5 us
    dot_general x1, matrix products, on_device(): jnp.dot(flat, out_weight, preferred_element_type=jnp.float32)  10.2 us
    dot_general x1, matrix products, on_device(): jnp.einsum('skgdt,skth->skgdh', weights.astype(jnp.bfloat16), value_pool,...  8.2 us
    dot_general x1, matrix products, on_device(): jnp.einsum('dskgh,skth->skgdt', slot_rows, key_pool, preferred_element_ty...  8.15 us
  transfers between devices with their start and end apart: 5, of which 4 were waited for; matrix products, arithmetic and copies ran while one was open for 10% of the time, Pallas kernels for 0%

commit v1 on v0

v1 whole, which is shorter than its diff:
```python
import functools

import jax
import jax.numpy as jnp
from jax import lax
from jax.experimental import pallas as pl
from jax.experimental.pallas import tpu as pltpu
from jax.sharding import PartitionSpec as P

NEG = -1e30
F32 = jnp.float32
BF16 = jnp.bfloat16
META = 16


def prepare_kernel(table_ref, length_ref, q_ref, out_ref, place_ref, meta_ref, count_ref):
    lenders = out_ref.shape[0]
    rows = q_ref.shape[1]
    entries = table_ref.shape[0]
    pool = entries
    blocks = entries // q_ref.shape[0]
    each = entries // lenders
    block = 256

    def clear(i, _):
        count_ref[i] = 0
        return 0

    lax.fori_loop(0, lenders, clear, 0)

    def one(e, _):
        slot = table_ref[e]
        lender = slot // pool
        j = count_ref[lender]
        count_ref[lender] = j + 1
        place_ref[e] = lender * each + j
        r = e // blocks
        limit = jnp.clip(length_ref[r] - (e % blocks) * block, 0, block)
        out_ref[lender, pl.ds(pl.multiple_of(j * rows, rows), rows), :] = q_ref[r]
        lanes = (1, meta_ref.shape[2])
        meta_ref[lender, pl.ds(j, 1), :] = jnp.full(lanes, (slot % pool).astype(F32), F32)
        meta_ref[lender, pl.ds(each + j, 1), :] = jnp.full(lanes, limit.astype(F32), F32)
        return 0

    lax.fori_loop(0, entries, one, 0, unroll=8)
    out_ref[:, each * rows :, :] = meta_ref[...].astype(BF16)


def prepare(table, lengths, q):
    requests, rows, head = q.shape
    entries = table.shape[0]
    lenders = lax.axis_size("inst")
    each = entries // lenders
    return pl.pallas_call(
        prepare_kernel,
        in_specs=[
            pl.BlockSpec(memory_space=pltpu.SMEM),
            pl.BlockSpec(memory_space=pltpu.SMEM),
            pl.BlockSpec(memory_space=pltpu.VMEM),
        ],
        out_specs=[
            pl.BlockSpec(memory_space=pltpu.VMEM),
            pl.BlockSpec(memory_space=pltpu.SMEM),
        ],
        out_shape=[
            jax.ShapeDtypeStruct((lenders, each * rows + META, head), BF16),
            jax.ShapeDtypeStruct((entries,), jnp.int32),
        ],
        scratch_shapes=[
            pltpu.VMEM((lenders, META, head), F32),
            pltpu.SMEM((lenders,), jnp.int32),
        ],
        name="prepare",
    )(table, lengths, q)


def attend_kernel(rows, info_ref, q_ref, k_ref, v_ref, out_ref, stat_ref):
    step = pl.program_id(0)
    chunk = k_ref.shape[0]
    block, head = k_ref.shape[1:]
    lenders = out_ref.shape[0]
    each = (out_ref.shape[1] - META) // rows
    scale = head ** (-0.5)
    lane = lax.broadcasted_iota(jnp.int32, (rows, block), 1)
    column = lax.broadcasted_iota(jnp.int32, (rows, head), 1)

    entry = [info_ref[0, step * chunk + i] for i in range(chunk)]
    limit = [info_ref[1, step * chunk + i] for i in range(chunk)]
    at = [
        (entry[i] // each, pl.ds(pl.multiple_of((entry[i] % each) * rows, rows), rows))
        for i in range(chunk)
    ]
    scores = [
        lax.dot_general(
            q_ref[at[i][0], at[i][1], :],
            k_ref[i],
            (((1,), (1,)), ((), ())),
            preferred_element_type=F32,
        )
        for i in range(chunk)
    ]
    stat = stat_ref[...]
    for i in range(chunk):
        s = jnp.where(lane < limit[i], scores[i] * scale, NEG)
        peak = jnp.max(s, axis=1, keepdims=True)
        weight = jnp.exp(s - peak)
        total = jnp.sum(weight, axis=1, keepdims=True)
        summed = jnp.dot(weight.astype(BF16), v_ref[i], preferred_element_type=F32)
        out_ref[at[i][0], at[i][1], :] = (summed * (1.0 / total)).astype(BF16)
        lse = jnp.where(limit[i] > 0, peak + jnp.log(total), NEG)
        stat = jnp.where(column == entry[i], lse, stat)
    stat_ref[...] = stat

    @pl.when(step == pl.num_programs(0) - 1)
    def _():
        x = stat_ref[...]
        hi = x.astype(BF16).astype(F32)
        rest = x - hi
        mid = rest.astype(BF16).astype(F32)
        low = rest - mid
        stack = jnp.concatenate([hi, mid, low, jnp.zeros((head - 3 * rows, head), F32)], axis=0)
        turned = stack.T
        for i in range(lenders):
            part = jnp.concatenate(
                [turned[i * each : (i + 1) * each], jnp.zeros((META - each, head), F32)], axis=0
            )
            out_ref[i, each * rows :, :] = part.astype(BF16)


def attend(info, q, keys, values, rows, chunk):
    pool, block, head = keys.shape
    whole = pl.BlockSpec(q.shape, lambda i, info: (0, 0, 0))
    part = pl.BlockSpec((chunk, block, head), lambda i, info: (i, 0, 0))
    return pl.pallas_call(
        functools.partial(attend_kernel, rows),
        grid_spec=pltpu.PrefetchScalarGridSpec(
            num_scalar_prefetch=1,
            grid=(pool // chunk,),
            in_specs=[whole, part, part],
            out_specs=whole,
            scratch_shapes=[pltpu.VMEM((rows, pool), F32)],
        ),
        out_shape=jax.ShapeDtypeStruct(q.shape, BF16),
        compiler_params=pltpu.CompilerParams(vmem_limit_bytes=32 * 1024 * 1024),
        name="attend",
    )(info, q, keys, values)


def draft_kernel(drafts, q_ref, k_ref, v_ref, out_ref, lse_ref):
    requests, rows, head = q_ref.shape
    group = rows // drafts
    tall = requests * rows
    wide = k_ref.shape[0]
    q = q_ref[...].reshape(tall, head)
    s = lax.dot_general(q, k_ref[...], (((1,), (1,)), ((), ())), preferred_element_type=F32)
    s = s * head ** (-0.5)
    row = lax.broadcasted_iota(jnp.int32, (tall, wide), 0)
    col = lax.broadcasted_iota(jnp.int32, (tall, wide), 1)
    valid = (row // rows == col % requests) & (col // requests <= (row % rows) // group)
    s = jnp.where(valid, s, NEG)
    peak = jnp.max(s, axis=1, keepdims=True)
    weight = jnp.exp(s - peak)
    total = jnp.sum(weight, axis=1, keepdims=True)
    summed = jnp.dot(weight.astype(BF16), v_ref[...], preferred_element_type=F32)
    out_ref[...] = (summed * (1.0 / total)).reshape(requests, rows, head)
    lse = peak + jnp.log(total)
    row = lax.broadcasted_iota(jnp.int32, (tall, head), 0)
    lane = lax.broadcasted_iota(jnp.int32, (tall, head), 1)
    picked = jnp.where(row % rows == lane, lse, 0.0)
    lse_ref[...] = jnp.sum(picked.reshape(requests, rows, head), axis=1)


def draft_block(q, keys, values, drafts):
    requests, rows, head = q.shape
    vmem = pl.BlockSpec(memory_space=pltpu.VMEM)
    return pl.pallas_call(
        functools.partial(draft_kernel, drafts),
        in_specs=[vmem] * 3,
        out_specs=[vmem] * 2,
        out_shape=[
            jax.ShapeDtypeStruct((requests, rows, head), F32),
            jax.ShapeDtypeStruct((requests, head), F32),
        ],
        cost_estimate=pl.CostEstimate(flops=10**7, bytes_accessed=10**6, transcendentals=10**5),
        name="draft",
    )(q, keys, values)


def combine_kernel(
    drafts, place_ref, core_ref, got_ref, fresh_ref, fresh_lse_ref, w_ref,
    send_ref, att_ref, arrived_ref, own_ref, rows_ref,
):
    requests, rows, head = fresh_ref.shape
    lenders = got_ref.shape[0]
    entries = place_ref.shape[0]
    each = entries // lenders
    blocks = entries // requests
    group = rows // drafts

    @pl.when(pl.program_id(0) == 0)
    def _():
        for i in range(lenders):
            arrived_ref[i * each : (i + 1) * each, :] = got_ref[i, each * rows :, :].astype(F32)[
                :each
            ]
        for e in range(entries):
            own_ref[e : e + 1, :] = arrived_ref[pl.ds(place_ref[e], 1), :]
        x = own_ref[...]
        lse = x + pltpu.roll(x, head - rows, 1) + pltpu.roll(x, head - 2 * rows, 1)
        lse = lse.reshape(requests, blocks, head)
        fresh = fresh_lse_ref[...]
        top = jnp.maximum(jnp.max(lse, axis=1), fresh)
        weight = jnp.exp(lse - top[:, None])
        fresh_weight = jnp.exp(fresh - top)
        part = 1.0 / (jnp.sum(weight, axis=1) + fresh_weight)
        weight = (weight * part[:, None]).reshape(entries, head).T
        fresh_weight = (fresh_weight * part)
        fresh_weight = jnp.concatenate(
            [fresh_weight, jnp.zeros((head - requests, head), F32)], axis=0
        ).T
        for r in range(requests):
            acc = fresh_ref[r] * fresh_weight[:rows, r : r + 1]
            for b in range(blocks):
                e = r * blocks + b
                place = place_ref[e]
                block_out = got_ref[
                    place // each, pl.ds(pl.multiple_of((place % each) * rows, rows), rows), :
                ]
                acc += block_out.astype(F32) * weight[:rows, e : e + 1]
            for d in range(drafts):
                rows_ref[pl.ds((d * requests + r) * group, group), :] = acc[
                    d * group : (d + 1) * group
                ]
        att_ref[...] = jnp.concatenate(
            [rows_ref[pl.ds(g, drafts * requests, stride=group), :] for g in range(group)], axis=1
        ).astype(BF16)

    send_ref[0] = jnp.dot(att_ref[...], w_ref[...], preferred_element_type=F32).astype(BF16)


def combine(place, core, got, fresh, fresh_lse, w, drafts, tp):
    requests, rows, head = fresh.shape
    deep, wide = w.shape
    tile = wide // tp
    tall = drafts * requests

    def whole(x):
        return pl.BlockSpec(x.shape, lambda i, place, core: (0,) * x.ndim)

    return pl.pallas_call(
        functools.partial(combine_kernel, drafts),
        grid_spec=pltpu.PrefetchScalarGridSpec(
            num_scalar_prefetch=2,
            grid=(tp // 2,),
            in_specs=[
                whole(got),
                whole(fresh),
                whole(fresh_lse),
                pl.BlockSpec((deep, tile), lambda i, place, core: (0, 2 * i + 1 - core[0])),
            ],
            out_specs=[
                pl.BlockSpec((1, tall, tile), lambda i, place, core: (i, 0, 0)),
                pl.BlockSpec((tall, deep), lambda i, place, core: (0, 0)),
            ],
            scratch_shapes=[
                pltpu.VMEM((place.shape[0], head), F32),
                pltpu.VMEM((place.shape[0], head), F32),
                pltpu.VMEM((requests * rows, head), F32),
            ],
        ),
        out_shape=[
            jax.ShapeDtypeStruct((tp // 2, tall, tile), BF16),
            jax.ShapeDtypeStruct((tall, deep), BF16),
        ],
        compiler_params=pltpu.CompilerParams(vmem_limit_bytes=32 * 1024 * 1024),
        name="combine",
    )(place, core, got, fresh, fresh_lse, w)


def keep_kernel(core_ref, att_ref, w_ref, keep_ref):
    keep_ref[0] = jnp.dot(att_ref[...], w_ref[...], preferred_element_type=F32)


def keep_half(core, att, w, tp):
    deep, wide = w.shape
    tile = wide // tp
    tall = att.shape[0]
    return pl.pallas_call(
        keep_kernel,
        grid_spec=pltpu.PrefetchScalarGridSpec(
            num_scalar_prefetch=1,
            grid=(tp // 2,),
            in_specs=[
                pl.BlockSpec((tall, deep), lambda i, core: (0, 0)),
                pl.BlockSpec((deep, tile), lambda i, core: (0, 2 * i + core[0])),
            ],
            out_specs=pl.BlockSpec((1, tall, tile), lambda i, core: (i, 0, 0)),
        ),
        out_shape=jax.ShapeDtypeStruct((tp // 2, tall, tile), F32),
        compiler_params=pltpu.CompilerParams(vmem_limit_bytes=32 * 1024 * 1024),
        cost_estimate=pl.CostEstimate(
            flops=tall * deep * wide, bytes_accessed=deep * wide, transcendentals=0
        ),
        name="keep_half",
    )(core, att, w)


def on_device(
    queries, new_keys, new_values, key_pool, value_pool, block_table, context_len, out_weight
):
    drafts, requests, heads, head = queries.shape
    pool, _, block, _ = key_pool.shape
    tp = lax.axis_size("tp")
    rows = drafts * heads
    q = queries.transpose(1, 0, 2, 3).reshape(requests, rows, head)
    payload, place = prepare(block_table, context_len, q)
    asked = lax.all_to_all(payload, "inst", 0, 0, tiled=True)
    fresh, fresh_lse = draft_block(
        q, new_keys.reshape(-1, head), new_values.reshape(-1, head), drafts
    )

    each = pool // asked.shape[0]
    meta = asked[:, each * rows :, 0].astype(jnp.int32)
    slot = meta[:, :each].reshape(pool)
    limit = meta[:, each : 2 * each].reshape(pool)
    hit = slot[None, :] == jnp.arange(pool, dtype=jnp.int32)[:, None]
    numbers = jnp.stack([jnp.arange(pool, dtype=jnp.int32), limit])
    info = jnp.sum(jnp.where(hit[None], numbers[:, None, :], 0), axis=2)
    answer = attend(
        info, asked, key_pool.reshape(pool, block, head), value_pool.reshape(pool, block, head), rows, 16
    )
    got = lax.all_to_all(answer, "inst", 0, 0, tiled=True)

    core = (lax.axis_index("tp") % 2).astype(jnp.int32).reshape(1)
    send, att = combine(place, core, got, fresh, fresh_lse, out_weight, drafts, tp)
    other = lax.ppermute(send, "tp", [(i, i ^ 1) for i in range(tp)])
    keep = keep_half(core, att, out_weight, tp)
    pair = (keep + other.astype(F32)).astype(BF16)
    groups = [list(range(c, tp, 2)) for c in range(2)]
    parts = lax.all_to_all(pair, "tp", 0, 0, axis_index_groups=groups, tiled=True)
    result = jnp.sum(parts.astype(F32), axis=0).astype(BF16)
    return result.reshape(drafts, requests, -1)


def solution(mesh):
    return jax.shard_map(
        on_device,
        mesh=mesh,
        in_specs=(
            P(None, "inst", "tp", None),
            P(None, "inst", "tp", None),
            P(None, "inst", "tp", None),
            P("inst", "tp", None, None),
            P("inst", "tp", None, None),
            P("inst"),
            P("inst"),
            P("tp", None),
        ),
        out_specs=P(None, "inst", "tp"),
        check_vma=False,
    )
```

time: 219 us -> 104 us (0.47); the launches traced: 216 us -> 103 us
  waiting for transfers between devices: 100 us -> 13.3 us
  matrix products: 32.2 us -> 0 us
  Pallas kernels: 0 us -> 21.1 us
  between operations: 14.3 us -> 0.11 us
  other arithmetic: 12.7 us -> 1.38 us
  local copies, waits for them, and re-layouts: 10.7 us -> 21.8 us
  starting transfers between devices: 16.1 us -> 7.26 us
  blocking collectives: 29.6 us -> 38.4 us
    reduce_scatter x1 -> x0, waiting for transfers between devices: 38.4 us -> none  [on_device(): lax.psum_scatter(partial_value, 'tp', scatter_dimension=2, tiled=True)]
    all_to_all x0 -> x2, blocking collectives: none -> 38.4 us  [the longest x1 25.1 us: on_device(): asked = lax.all_to_all(payload, 'inst', 0, 0, tiled=True)]
    dot_general x7 -> x0, matrix products: 32.2 us -> none  [the longest x1 10.2 us: on_device(): jnp.dot(flat, out_weight, preferred_element_type=jnp.float32)]
    all_to_all x3 -> x1, waiting for transfers between devices: 45 us -> 13.3 us  [on_device(): got = lax.all_to_all(answer, 'inst', 0, 0, tiled=True)]
    pallas_call x0 -> x5, Pallas kernels: none -> 21.1 us  [the longest x1 7.47 us: attend(): pl.pallas_call(functools.partial(attend_kernel, rows), grid_spec=pltpu.Pr...]
    unnamed x13 -> x16, local copies, waits for them, and re-layouts: 3.89 us -> 20.9 us
    all_gather x1 -> x0, waiting for transfers between devices: 16.2 us -> none  [on_device(): all_rows = lax.all_gather(queries, 'inst', axis=1, tiled=True)]
    all_gather x1 -> x0, blocking collectives: 15 us -> none  [on_device(): lax.all_gather(block_table, 'inst', axis=0, tiled=True)]
  transfers between devices with their start and end apart: 5 -> 2, of which waited for: 4 -> 1; matrix products, arithmetic and copies ran while one was open for 10% -> 0% of each run, Pallas kernels for 0% -> 4%
where the time goes in v1:
time: 104 us; the launch traced here: 103 us
  blocking collectives  38.4 us (37%)
  local copies, waits for them, and re-layouts  21.8 us (21%)
  Pallas kernels  21.1 us (20%)
  waiting for transfers between devices  13.3 us (13%)
  starting transfers between devices  7.26 us (7%)
  other arithmetic  1.38 us (1%)
    all_to_all x1, blocking collectives, on_device(): asked = lax.all_to_all(payload, 'inst', 0, 0, tiled=True)  25.1 us
    unnamed x16, local copies, waits for them, and re-layouts  20.9 us
    all_to_all x1, waiting for transfers between devices, on_device(): got = lax.all_to_all(answer, 'inst', 0, 0, tiled=True)  13.3 us
    all_to_all x1, blocking collectives, on_device(): lax.all_to_all(pair, 'tp', 0, 0, axis_index_groups=groups, tiled=True)  13.3 us
    pallas_call x1, Pallas kernels, attend(): pl.pallas_call(functools.partial(attend_kernel, rows), grid_spec=pltpu.Pr...  7.47 us
    pallas_call x1, Pallas kernels, combine(): pl.pallas_call(functools.partial(combine_kernel, drafts), grid_spec=pltpu...  4.56 us
    pallas_call x1, Pallas kernels, prepare(): pl.pallas_call(prepare_kernel, in_specs=[pl.BlockSpec(memory_space=pltpu....  4.51 us
    all_to_all x1, starting transfers between devices, on_device(): got = lax.all_to_all(answer, 'inst', 0, 0, tiled=True)  3.83 us
  transfers between devices with their start and end apart: 2, of which 1 were waited for; matrix products, arithmetic and copies ran while one was open for 0% of the time, Pallas kernels for 4%

profile of v1, /device:TPU:1, one launch (start us, length us, event | category | flops | bytes accessed | tf_op | source)
XLA Modules:
  0.0 103.4 jit_solution(16280065635130057075)
XLA Ops:
  0.0 0.0 copy-start
  0.0 0.9 copy-done
  0.9 0.7 copy_bitcast_fusion.q_ref
  1.6 4.5 %prepare.1 = (bf16[16,272,128]{2,1,0:T(8,128)(2,1)}, s32[128]{0:T(128)}) custom-call(s32[128]{0:T(128)} %table_ref.1, s32[16]{0:T(128)} %length_ref.1, bf16[16,32,128]{2,1,0:T(8,128)(2,1)} %copy_bitcast_fusion.q_ref), custom_call_target="tpu_custom_call" | custom-call | tf_op jit(solution)/shard_map/prepare/pallas_call | solution.py:54
  6.1 25.1 %all_to_all.15.q_ref = bf16[16,272,128]{2,1,0:T(8,128)(2,1)S(1)} all-to-all(bf16[16,272,128]{2,1,0:T(8,128)(2,1)} %get-tuple-element.12), channel_id=1, replica_groups=mesh['inst'=16,'tp'=8] {'inst'}, dimensions={0} | all-to-all | bytes 2228224 | tf_op jit(solution)/shard_map/all_to_all | solution.py:317
  31.2 0.3 convert_reduce_fusion
  31.6 0.1 fusion
  31.6 0.1 stack_reshape.3
  31.7 0.1 eq.21
  31.9 0.1 select_reduce_fusion.info_ref
  32.0 0.0 copy-start.3
  32.0 3.4 %copy-done.3 = bf16[128,1,256,128]{3,2,1,0:T(8,128)(2,1)S(1)} copy-done((bf16[128,1,256,128]{3,2,1,0:T(8,128)(2,1)S(1)}, bf16[128,1,256,128]{3,2,1,0:T(8,128)(2,1)}, u32[]{:S(2)}) %copy-start.3) | copy-done | bytes 8388632
  35.4 0.0 copy-start.4
  35.4 3.4 %copy-done.4 = bf16[128,1,256,128]{3,2,1,0:T(8,128)(2,1)S(1)} copy-done((bf16[128,1,256,128]{3,2,1,0:T(8,128)(2,1)S(1)}, bf16[128,1,256,128]{3,2,1,0:T(8,128)(2,1)}, u32[]{:S(2)}) %copy-start.4) | copy-done | bytes 8388632
  38.8 7.5 %attend.1 = bf16[16,272,128]{2,1,0:T(8,128)(2,1)} custom-call(s32[2,128]{1,0:T(2,128)S(1)} %select_reduce_fusion.info_ref, bf16[16,272,128]{2,1,0:T(8,128)(2,1)S(1)} %all_to_all.15.q_ref, bf16[128,256,128]{2,1,0:T(8,128)(2,1)S(1)} %bitcast.11, bf16[128,256,128]{2,1,0:T(8,128)(2,1)S(1)} %bitcast.12), custom_call_target="tpu_custom_call" | custom-call | tf_op jit(solution)/shard_map/attend/pallas_call | solution.py:134
  46.2 0.0 copy-start.7
  46.2 3.8 %all-to-all-start.1 = ((bf16[16,272,128]{2,1,0:T(8,128)(2,1)}), bf16[16,272,128]{2,1,0:T(8,128)(2,1)S(1)}, u32[]{:S(2)}, u32[]{:S(2)}) async-start(bf16[16,272,128]{2,1,0:T(8,128)(2,1)} %attend.1), calls=%async_computation.1 | async-start | bytes 2228224 | tf_op jit(solution)/shard_map/all_to_all | solution.py:332
  50.1 2.1 %draft.1 = (f32[16,32,128]{2,1,0:T(8,128)}, f32[16,128]{1,0:T(8,128)}) custom-call(bf16[16,32,128]{2,1,0:T(8,128)(2,1)} %copy_bitcast_fusion.q_ref, bf16[64,128]{1,0:T(8,128)(2,1)} %bitcast.13, bf16[64,128]{1,0:T(8,128)(2,1)} %bitcast.14), custom_call_target="tpu_custom_call" | custom-call | flops 10000000 | bytes 1000000 | tf_op jit(solution)/shard_map/draft/pallas_call | solution.py:176
  52.1 13.3 %all-to-all-done.1.got_ref = bf16[16,272,128]{2,1,0:T(8,128)(2,1)S(1)} async-done(((bf16[16,272,128]{2,1,0:T(8,128)(2,1)}), bf16[16,272,128]{2,1,0:T(8,128)(2,1)S(1)}, u32[]{:S(2)}, u32[]{:S(2)}) %all-to-all-start.1) | async-done | bytes 1114144 | tf_op jit(solution)/shard_map/all_to_all | solution.py:332
  65.4 0.0 copy-done.7
  65.4 0.0 copy-start.1
  65.4 5.8 %copy-done.1 = bf16[1024,8192]{1,0:T(8,128)(2,1)S(1)} copy-done((bf16[1024,8192]{1,0:T(8,128)(2,1)S(1)}, bf16[1024,8192]{1,0:T(8,128)(2,1)}, u32[]{:S(2)}) %copy-start.1) | copy-done | bytes 16777240
  71.2 0.0 copy-start.5
  71.2 0.9 copy-done.5
  72.2 0.0 copy-start.6
  72.2 0.7 copy-done.6
  72.9 4.6 %combine.1 = (bf16[4,64,1024]{2,1,0:T(8,128)(2,1)S(1)}, bf16[64,1024]{1,0:T(8,128)(2,1)S(1)}) custom-call(s32[128]{0:T(128)S(1)} %copy-done.7, s32[1]{0:T(128)} %bitcast.core_ref, bf16[16,272,128]{2,1,0:T(8,128)(2,1)S(1)} %all-to-all-done.1.got_ref, f32[16,32,128]{2,1,0:T(8,128)S(1)} %copy-done.5, f32[16,128]{1,0:T(8,128)S(1)} %copy-done.6, ...), custom_call_target="tpu_custom_call" | custom-call | tf_op jit(solution)/shard_map/combine/pallas_call | solution.py:250
  77.4 3.4 %collective-permute-start = (bf16[4,64,1024]{2,1,0:T(8,128)(2,1)S(1)}, bf16[4,64,1024]{2,1,0:T(8,128)(2,1)S(1)}, u32[]{:S(2)}, u32[]{:S(2)}) collective-permute-start(bf16[4,64,1024]{2,1,0:T(8,128)(2,1)S(1)} %get-tuple-element.16), channel_id=1, source_target_pairs={{0,1},{1,0},{2,3},{3,2},{4,5},{5,4},{6,7},{7,6},{8,9},{9,8},{10,11... | collective-permute-start | bytes 1572872 | tf_op jit(solution)/shard_map/ppermute | solution.py:336
  80.9 0.0 copy-start.2
  80.9 5.8 %copy-done.2 = bf16[1024,8192]{1,0:T(8,128)(2,1)S(1)} copy-done((bf16[1024,8192]{1,0:T(8,128)(2,1)S(1)}, bf16[1024,8192]{1,0:T(8,128)(2,1)}, u32[]{:S(2)}) %copy-start.2) | copy-done | bytes 16777240
  86.6 2.5 %keep_half.1 = f32[4,64,1024]{2,1,0:T(8,128)S(1)} custom-call(s32[1]{0:T(128)} %bitcast.core_ref, bf16[64,1024]{1,0:T(8,128)(2,1)S(1)} %get-tuple-element.15.att_ref, bf16[1024,8192]{1,0:T(8,128)(2,1)S(1)} %copy-done.2), custom_call_target="tpu_custom_call" | custom-call | flops 536870912 | bytes 8388608 | tf_op jit(solution)/shard_map/keep_half/pallas_call | solution.py:288
  89.2 0.0 collective-permute-done
  89.2 0.2 add_convert_fusion
  89.3 13.3 %all_to_all.16 = bf16[4,64,1024]{2,1,0:T(8,128)(2,1)S(1)} all-to-all(bf16[4,64,1024]{2,1,0:T(8,128)(2,1)S(1)} %add_convert_fusion), channel_id=1, replica_groups={{0,2,4,6},{1,3,5,7},{8,10,12,14},{9,11,13,15},{16,18,20,22},{17,19,21,2..., dimensions={0} | all-to-all | bytes 1048576 | tf_op jit(solution)/shard_map/all_to_all | solution.py:340
  102.6 0.7 reduce_sum.22
  (3 shorter events, 0.0 us)
Async XLA Ops:
  0.0 0.9 copy-start
  32.0 3.4 %copy-start.3 = (bf16[128,1,256,128]{3,2,1,0:T(8,128)(2,1)S(1)}, bf16[128,1,256,128]{3,2,1,0:T(8,128)(2,1)}, u32[]{:S(2)}) copy-start(bf16[128,1,256,128]{3,2,1,0:T(8,128)(2,1)} %param.11) | copy-start | bytes 25165828
  35.4 3.4 %copy-start.4 = (bf16[128,1,256,128]{3,2,1,0:T(8,128)(2,1)S(1)}, bf16[128,1,256,128]{3,2,1,0:T(8,128)(2,1)}, u32[]{:S(2)}) copy-start(bf16[128,1,256,128]{3,2,1,0:T(8,128)(2,1)} %param.12) | copy-start | bytes 25165828
  46.2 19.2 %copy-start.7 = (s32[128]{0:T(128)S(1)}, s32[128]{0:T(128)}, u32[]{:S(2)}) copy-start(s32[128]{0:T(128)} %get-tuple-element.11.place_ref) | copy-start | bytes 1540
  46.2 19.2 %all-to-all-start.1 = ((bf16[16,272,128]{2,1,0:T(8,128)(2,1)}), bf16[16,272,128]{2,1,0:T(8,128)(2,1)S(1)}, u32[]{:S(2)}, u32[]{:S(2)}) async-start(bf16[16,272,128]{2,1,0:T(8,128)(2,1)} %attend.1), calls=%async_computation.1 | async-start | bytes 2228224 | tf_op jit(solution)/shard_map/all_to_all | solution.py:332
  65.4 5.8 %copy-start.1 = (bf16[1024,8192]{1,0:T(8,128)(2,1)S(1)}, bf16[1024,8192]{1,0:T(8,128)(2,1)}, u32[]{:S(2)}) copy-start(bf16[1024,8192]{1,0:T(8,128)(2,1)} %w_ref.3) | copy-start | bytes 50331652
  71.2 0.9 copy-start.5
  72.2 0.7 copy-start.6
  77.4 11.7 %collective-permute-start = (bf16[4,64,1024]{2,1,0:T(8,128)(2,1)S(1)}, bf16[4,64,1024]{2,1,0:T(8,128)(2,1)S(1)}, u32[]{:S(2)}, u32[]{:S(2)}) collective-permute-start(bf16[4,64,1024]{2,1,0:T(8,128)(2,1)S(1)} %get-tuple-element.16), channel_id=1, source_target_pairs={{0,1},{1,0},{2,3},{3,2},{4,5},{5,4},{6,7},{7,6},{8,9},{9,8},{10,11... | collective-permute-start | bytes 1572872 | tf_op jit(solution)/shard_map/ppermute | solution.py:336
  80.9 5.8 %copy-start.2 = (bf16[1024,8192]{1,0:T(8,128)(2,1)S(1)}, bf16[1024,8192]{1,0:T(8,128)(2,1)}, u32[]{:S(2)}) copy-start(bf16[1024,8192]{1,0:T(8,128)(2,1)} %w_ref.3) | copy-start | bytes 50331652

commit v2 on v0

v2 whole, which is shorter than its diff:
```python
import functools

import jax
import jax.numpy as jnp
from jax import lax
from jax.experimental import pallas as pl
from jax.experimental.pallas import tpu as pltpu
from jax.sharding import PartitionSpec as P

NEG = -1e30
F32 = jnp.float32
BF16 = jnp.bfloat16
META = 16


def in_hbm(x):
    return pltpu.with_memory_space_constraint(x, pltpu.HBM)


def draft_block(drafts, q, k_ref, v_ref, out_ref, stat_ref):
    requests, rows, head = q.shape
    group = rows // drafts
    tall = requests * rows
    wide = k_ref.shape[0]
    s = lax.dot_general(
        k_ref[...], q.reshape(tall, head), (((1,), (1,)), ((), ())), preferred_element_type=F32
    )
    key = lax.broadcasted_iota(jnp.int32, (wide, tall), 0)
    row = lax.broadcasted_iota(jnp.int32, (wide, tall), 1)
    request_bits, rows_bits, group_bits = (n.bit_length() - 1 for n in (requests, rows, group))
    own = lax.shift_right_logical(row, rows_bits) == (key & (requests - 1))
    drafted = lax.shift_right_logical(row & (rows - 1), group_bits)
    valid = own & (lax.shift_right_logical(key, request_bits) <= drafted)
    s = jnp.where(valid, s * head ** (-0.5), NEG)
    peak = jnp.max(s, axis=0, keepdims=True)
    weight = jnp.exp(s - peak)
    total = jnp.sum(weight, axis=0, keepdims=True)
    out_ref[...] = lax.dot_general(
        weight.astype(BF16), v_ref[...], (((0,), (0,)), ((), ())), preferred_element_type=F32
    ).reshape(requests, rows, head)
    for r in range(requests):
        start = r * rows // head * head
        for n, x in enumerate((peak, total)):
            piece = x[:, start : start + head]
            if r * rows > start:
                piece = pltpu.roll(piece, head - (r * rows - start), 1)
            stat_ref[n, r : r + 1, :] = piece


def prepare_kernel(
    shifts, table_hbm, length_hbm, queries_hbm, k_hbm, v_hbm,
    out_ref, place_ref, fresh_ref, stat_ref,
    table_ref, length_ref, queries_ref, k_ref, v_ref, q_ref, meta_ref, count_ref, sems,
):
    pairs = (
        (table_hbm, table_ref), (length_hbm, length_ref), (queries_hbm, queries_ref),
        (k_hbm, k_ref), (v_hbm, v_ref),
    )
    copies = [pltpu.make_async_copy(a, b, sems.at[i]) for i, (a, b) in enumerate(pairs)]
    for copy in copies:
        copy.start()
    drafts, requests, group, head = queries_ref.shape
    lenders = out_ref.shape[0]
    rows = drafts * group
    entries = table_ref.shape[0]
    each = entries // lenders
    pool_bits, blocks_bits, block_bits = shifts

    for i in range(lenders):
        count_ref[i] = 0
    for copy in copies:
        copy.wait()
    for r in range(requests):
        q_ref[r] = jnp.concatenate([queries_ref[d, r] for d in range(drafts)], axis=0)

    def one(e, _):
        slot = table_ref[e]
        lender = lax.shift_right_logical(slot, pool_bits)
        j = count_ref[lender]
        count_ref[lender] = j + 1
        place_ref[e] = lender * each + j
        r = lax.shift_right_logical(e, blocks_bits)
        start = lax.shift_left(e & ((1 << blocks_bits) - 1), block_bits)
        limit = jnp.clip(length_ref[r] - start, 0, 1 << block_bits)
        out_ref[lender, pl.ds(pl.multiple_of(j * rows, rows), rows), :] = q_ref[r]
        lanes = (1, head)
        inner = slot & ((1 << pool_bits) - 1)
        meta_ref[lender, pl.ds(j, 1), :] = jnp.full(lanes, inner.astype(F32), F32)
        meta_ref[lender, pl.ds(each + j, 1), :] = jnp.full(lanes, limit.astype(F32), F32)
        return 0

    lax.fori_loop(0, entries, one, 0, unroll=8)
    out_ref[:, each * rows :, :] = meta_ref[...].astype(BF16)
    draft_block(drafts, q_ref[...], k_ref, v_ref, fresh_ref, stat_ref)


def prepare(table, lengths, queries, new_keys, new_values, block):
    drafts, requests, group, head = queries.shape
    rows = drafts * group
    entries = table.shape[0]
    lenders = lax.axis_size("inst")
    each = entries // lenders
    shifts = tuple(n.bit_length() - 1 for n in (entries, entries // requests, block))
    vmem, smem = pl.BlockSpec(memory_space=pltpu.VMEM), pl.BlockSpec(memory_space=pltpu.SMEM)
    return pl.pallas_call(
        functools.partial(prepare_kernel, shifts),
        in_specs=[pl.BlockSpec(memory_space=pltpu.HBM)] * 5,
        out_specs=[vmem, smem, vmem, vmem],
        out_shape=[
            jax.ShapeDtypeStruct((lenders, each * rows + META, head), BF16),
            jax.ShapeDtypeStruct((entries,), jnp.int32),
            jax.ShapeDtypeStruct((requests, rows, head), F32),
            jax.ShapeDtypeStruct((2, requests, head), F32),
        ],
        scratch_shapes=[
            pltpu.SMEM(table.shape, jnp.int32),
            pltpu.SMEM(lengths.shape, jnp.int32),
            pltpu.VMEM(queries.shape, BF16),
            pltpu.VMEM(new_keys.shape, BF16),
            pltpu.VMEM(new_values.shape, BF16),
            pltpu.VMEM((requests, rows, head), BF16),
            pltpu.VMEM((lenders, META, head), F32),
            pltpu.SMEM((lenders,), jnp.int32),
            pltpu.SemaphoreType.DMA((5,)),
        ],
        compiler_params=pltpu.CompilerParams(vmem_limit_bytes=8 * 1024 * 1024),
        cost_estimate=pl.CostEstimate(
            flops=0, bytes_accessed=64 * 1024 * 1024, transcendentals=0
        ),
        name="prepare",
    )(*(in_hbm(x) for x in (table, lengths, queries, new_keys, new_values)))


def attend_kernel(rows, chunk, info_ref, q_ref, k_ref, v_ref, out_ref, stat_ref):
    block, head = k_ref.shape[1:]
    lenders = out_ref.shape[0]
    each = (out_ref.shape[1] - META) // rows
    scale = head ** (-0.5)
    lane = lax.broadcasted_iota(jnp.int32, (rows, block), 1)
    column = lax.broadcasted_iota(jnp.int32, (rows, head), 1)
    near = chunk // each

    def some(step, _):
        of = [(step * near + i // each, i % each) for i in range(chunk)]
        slot = [info_ref[n, j] for n, j in of]
        limit = [info_ref[n, each + j] for n, j in of]
        scores = [
            lax.dot_general(
                q_ref[n, j * rows : (j + 1) * rows, :],
                k_ref[slot[i]],
                (((1,), (1,)), ((), ())),
                preferred_element_type=F32,
            )
            for i, (n, j) in enumerate(of)
        ]
        stat = stat_ref[...]
        for i, (n, j) in enumerate(of):
            s = jnp.where(lane < limit[i], scores[i] * scale, NEG)
            peak = jnp.max(s, axis=1, keepdims=True)
            weight = jnp.exp(s - peak)
            total = jnp.sum(weight, axis=1, keepdims=True)
            summed = jnp.dot(weight.astype(BF16), v_ref[slot[i]], preferred_element_type=F32)
            out_ref[n, j * rows : (j + 1) * rows, :] = (summed * (1.0 / total)).astype(BF16)
            lse = jnp.where(limit[i] > 0, peak + jnp.log(total), NEG)
            stat = jnp.where(column == step * chunk + i, lse, stat)
        stat_ref[...] = stat
        return 0

    lax.fori_loop(0, lenders * each // chunk, some, 0)
    x = stat_ref[...]
    hi = x.astype(BF16).astype(F32)
    rest = x - hi
    mid = rest.astype(BF16).astype(F32)
    low = rest - mid
    stack = jnp.concatenate([hi, mid, low, jnp.zeros((head - 3 * rows, head), F32)], axis=0)
    turned = stack.T
    for i in range(lenders):
        part = jnp.concatenate(
            [turned[i * each : (i + 1) * each], jnp.zeros((META - each, head), F32)], axis=0
        )
        out_ref[i, each * rows :, :] = part.astype(BF16)


def attend(info, q, keys, values, rows, chunk):
    pool, block, head = keys.shape
    vmem, smem = pl.BlockSpec(memory_space=pltpu.VMEM), pl.BlockSpec(memory_space=pltpu.SMEM)
    return pl.pallas_call(
        functools.partial(attend_kernel, rows, chunk),
        in_specs=[smem, vmem, vmem, vmem],
        out_specs=vmem,
        out_shape=jax.ShapeDtypeStruct(q.shape, BF16),
        scratch_shapes=[pltpu.VMEM((rows, pool), F32)],
        compiler_params=pltpu.CompilerParams(vmem_limit_bytes=16 * 1024 * 1024),
        name="attend",
    )(info, q, keys, values)


def combine_kernel(
    drafts, place_ref, got_ref, fresh_ref, stat_ref, w_ref,
    send_ref, att_ref, arrived_ref, own_ref, rows_ref,
):
    requests, rows, head = fresh_ref.shape
    lenders = got_ref.shape[0]
    entries = place_ref.shape[0]
    each = entries // lenders
    each_bits = each.bit_length() - 1
    blocks = entries // requests
    group = rows // drafts

    for i in range(lenders):
        arrived_ref[i * each : (i + 1) * each, :] = got_ref[i, each * rows :, :].astype(F32)[:each]
    for e in range(entries):
        own_ref[e : e + 1, :] = arrived_ref[pl.ds(place_ref[e], 1), :]
    x = own_ref[...]
    lse = x + pltpu.roll(x, head - rows, 1) + pltpu.roll(x, head - 2 * rows, 1)
    lse = lse.reshape(requests, blocks, head)
    fresh_peak = stat_ref[0]
    top = jnp.maximum(jnp.max(lse, axis=1), fresh_peak)
    weight = jnp.exp(lse - top[:, None])
    fresh_weight = jnp.exp(fresh_peak - top)
    part = 1.0 / (jnp.sum(weight, axis=1) + stat_ref[1] * fresh_weight)
    weight = (weight * part[:, None]).reshape(entries, head).T
    fresh_weight = fresh_weight * part
    fresh_weight = jnp.concatenate(
        [fresh_weight, jnp.zeros((head - requests, head), F32)], axis=0
    ).T
    for r in range(requests):
        acc = fresh_ref[r] * fresh_weight[:rows, r : r + 1]
        for b in range(blocks):
            e = r * blocks + b
            place = place_ref[e]
            lender = lax.shift_right_logical(place, each_bits)
            start = pl.multiple_of((place & (each - 1)) * rows, rows)
            block_out = got_ref[lender, pl.ds(start, rows), :]
            acc += block_out.astype(F32) * weight[:rows, e : e + 1]
        for d in range(drafts):
            rows_ref[pl.ds((d * requests + r) * group, group), :] = acc[
                d * group : (d + 1) * group
            ]
    att = jnp.concatenate(
        [rows_ref[pl.ds(g, drafts * requests, stride=group), :] for g in range(group)], axis=1
    ).astype(BF16)
    att_ref[...] = att
    tile = send_ref.shape[2]
    place_tp = lax.axis_index("tp")
    core = place_tp & 1
    ring = send_ref.shape[0]
    for i in range(send_ref.shape[0]):
        to = ((place_tp >> 1) + i) & (ring - 1)
        here = pl.ds(pl.multiple_of((2 * to + 1 - core) * tile, tile), tile)
        send_ref[i] = jnp.dot(att, w_ref[:, here], preferred_element_type=F32).astype(BF16)


def combine(place, got, fresh, stat, w, drafts, tp):
    requests, rows, head = fresh.shape
    deep, wide = w.shape
    tile = wide // tp
    tall = drafts * requests
    vmem, smem = pl.BlockSpec(memory_space=pltpu.VMEM), pl.BlockSpec(memory_space=pltpu.SMEM)
    return pl.pallas_call(
        functools.partial(combine_kernel, drafts),
        in_specs=[smem, vmem, vmem, vmem, vmem],
        out_specs=[vmem, vmem],
        out_shape=[
            jax.ShapeDtypeStruct((tp // 2, tall, tile), BF16),
            jax.ShapeDtypeStruct((tall, deep), BF16),
        ],
        scratch_shapes=[
            pltpu.VMEM((place.shape[0], head), F32),
            pltpu.VMEM((place.shape[0], head), F32),
            pltpu.VMEM((requests * rows, head), F32),
        ],
        compiler_params=pltpu.CompilerParams(vmem_limit_bytes=16 * 1024 * 1024),
        name="combine",
    )(place, got, fresh, stat, w)


def keep_kernel(att_ref, w_ref, keep_ref):
    tile = keep_ref.shape[2]
    place_tp = lax.axis_index("tp")
    core = place_tp & 1
    ring = keep_ref.shape[0]
    for i in range(ring):
        to = ((place_tp >> 1) + i) & (ring - 1)
        here = pl.ds(pl.multiple_of((2 * to + core) * tile, tile), tile)
        keep_ref[i] = jnp.dot(att_ref[...], w_ref[:, here], preferred_element_type=F32)


def keep_half(att, w, tp):
    deep, wide = w.shape
    tile = wide // tp
    tall = att.shape[0]
    vmem, smem = pl.BlockSpec(memory_space=pltpu.VMEM), pl.BlockSpec(memory_space=pltpu.SMEM)
    return pl.pallas_call(
        keep_kernel,
        in_specs=[vmem, vmem],
        out_specs=vmem,
        out_shape=jax.ShapeDtypeStruct((tp // 2, tall, tile), F32),
        compiler_params=pltpu.CompilerParams(vmem_limit_bytes=16 * 1024 * 1024),
        cost_estimate=pl.CostEstimate(
            flops=tall * deep * wide, bytes_accessed=deep * wide, transcendentals=0
        ),
        name="keep_half",
    )(att, w)


def on_device(
    queries, new_keys, new_values, key_pool, value_pool, block_table, context_len, out_weight
):
    drafts, requests, heads, head = queries.shape
    pool, _, block, _ = key_pool.shape
    tp = lax.axis_size("tp")
    rows = drafts * heads
    payload, place, fresh, stat = prepare(
        block_table, context_len, queries, new_keys.reshape(-1, head), new_values.reshape(-1, head), block
    )
    asked = lax.all_to_all(payload, "inst", 0, 0, tiled=True)
    each = pool // asked.shape[0]
    info = asked[:, each * rows :, 0].astype(jnp.int32)
    answer = attend(
        info, asked, key_pool.reshape(pool, block, head), value_pool.reshape(pool, block, head), rows, 32
    )
    got = lax.all_to_all(answer, "inst", 0, 0, tiled=True)

    send, att = combine(place, got, fresh, stat, out_weight, drafts, tp)
    other = lax.ppermute(send, "tp", [(i, i ^ 1) for i in range(tp)])
    keep = keep_half(att, out_weight, tp)
    ring = tp // 2
    parts = [
        lax.ppermute(
            (keep[n] + other[n].astype(F32)).astype(BF16),
            "tp",
            [(i, (i + 2 * n) % tp) for i in range(tp)],
        )
        for n in range(1, ring)
    ]
    total = keep[0] + other[0].astype(F32)
    for part in parts:
        total = total + part.astype(F32)
    result = total.astype(BF16)
    return result.reshape(drafts, requests, -1)


def solution(mesh):
    return jax.shard_map(
        on_device,
        mesh=mesh,
        in_specs=(
            P(None, "inst", "tp", None),
            P(None, "inst", "tp", None),
            P(None, "inst", "tp", None),
            P("inst", "tp", None, None),
            P("inst", "tp", None, None),
            P("inst"),
            P("inst"),
            P("tp", None),
        ),
        out_specs=P(None, "inst", "tp"),
        check_vma=False,
    )
```

time: 219 us -> 79.2 us (0.36); the launches traced: 216 us -> 78.9 us
  waiting for transfers between devices: 100 us -> 5.65 us
  matrix products: 32.2 us -> 0 us
  between operations: 14.3 us -> 0.06 us
  blocking collectives: 29.6 us -> 43.7 us
  Pallas kernels: 0 us -> 13.7 us
  other arithmetic: 12.7 us -> 1.18 us
  starting transfers between devices: 16.1 us -> 7.93 us
  local copies, waits for them, and re-layouts: 10.7 us -> 6.76 us
    all_to_all x3 -> x0, waiting for transfers between devices: 45 us -> none  [the longest x1 42.4 us: on_device(): lax.all_to_all(req_out.reshape(n_inst, req_dev, kv_loc, group, drafts, he...]
    all_to_all x0 -> x2, blocking collectives: none -> 43.7 us  [the longest x1 24.9 us: on_device(): asked = lax.all_to_all(payload, 'inst', 0, 0, tiled=True)]
    reduce_scatter x1 -> x0, waiting for transfers between devices: 38.4 us -> none  [on_device(): lax.psum_scatter(partial_value, 'tp', scatter_dimension=2, tiled=True)]
    dot_general x7 -> x0, matrix products: 32.2 us -> none  [the longest x1 10.2 us: on_device(): jnp.dot(flat, out_weight, preferred_element_type=jnp.float32)]
    all_gather x1 -> x0, waiting for transfers between devices: 16.2 us -> none  [on_device(): all_rows = lax.all_gather(queries, 'inst', axis=1, tiled=True)]
    all_to_all x3 -> x0, starting transfers between devices: 16 us -> none  [the longest x1 6.65 us: on_device(): lax.all_to_all(req_peak.reshape(n_inst, req_dev, kv_loc, group, drafts),...]
    all_gather x1 -> x0, blocking collectives: 15 us -> none  [on_device(): lax.all_gather(block_table, 'inst', axis=0, tiled=True)]
    unnamed x1 -> x0, blocking collectives: 14.5 us -> none
  transfers between devices with their start and end apart: 5 -> 4, of which waited for: 4 -> 2; matrix products, arithmetic and copies ran while one was open for 10% -> 0% of each run, Pallas kernels for 0% -> 2%
where the time goes in v2:
time: 79.2 us; the launch traced here: 78.9 us
  blocking collectives  43.7 us (55%)
  Pallas kernels  13.7 us (17%)
  starting transfers between devices  7.93 us (10%)
  local copies, waits for them, and re-layouts  6.76 us (9%)
  waiting for transfers between devices  5.65 us (7%)
  other arithmetic  1.18 us (1%)
    all_to_all x1, blocking collectives, on_device(): asked = lax.all_to_all(payload, 'inst', 0, 0, tiled=True)  24.9 us
    all_to_all x1, blocking collectives, on_device(): got = lax.all_to_all(answer, 'inst', 0, 0, tiled=True)  18.8 us
    unnamed x6, local copies, waits for them, and re-layouts  6.76 us
    ppermute x3, waiting for transfers between devices, on_device(): lax.ppermute((keep[n] + other[n].astype(F32)).astype(BF16), 'tp', [(i, (i...  5.64 us
    pallas_call x1, Pallas kernels, attend(): pl.pallas_call(functools.partial(attend_kernel, rows, chunk), in_specs=[s...  5.6 us
    ppermute x3, starting transfers between devices, on_device(): lax.ppermute((keep[n] + other[n].astype(F32)).astype(BF16), 'tp', [(i, (i...  4.45 us
    pallas_call x1, Pallas kernels, combine(): pl.pallas_call(functools.partial(combine_kernel, drafts), in_specs=[smem,...  3.52 us
    ppermute x1, starting transfers between devices, on_device(): other = lax.ppermute(send, 'tp', [(i, i ^ 1) for i in range(tp)])  3.48 us
  transfers between devices with their start and end apart: 4, of which 2 were waited for; matrix products, arithmetic and copies ran while one was open for 0% of the time, Pallas kernels for 2%

profile of v2, /device:TPU:1, one launch (start us, length us, event | category | flops | bytes accessed | tf_op | source)
XLA Modules:
  0.0 78.9 jit_solution(10939739074277727333)
XLA Ops:
  0.0 3.0 %prepare.1 = (bf16[16,272,128]{2,1,0:T(8,128)(2,1)S(1)}, s32[128]{0:T(128)S(1)}, f32[16,32,128]{2,1,0:T(8,128)S(1)}, f32[2,16,128]{2,1,0:T(8,128)S(1)}) custom-call(s32[128]{0:T(128)} %table_hbm.1, s32[16]{0:T(128)} %length_hbm.1, bf16[4,16,8,128]{3,2,1,0:T(8,128)(2,1)} %queries_hbm.1, bf16[64,128]{1,0:T(8,128)(2,1)} %bitcast.23, bf16[64,128]{1,0:T(8,128)(2,1)} %bitcast.24), custom_call_target="tpu_custom_call" | custom-call | bytes 67108864 | tf_op jit(solution)/shard_map/prepare/pallas_call | solution.py:105
  3.0 24.9 %all_to_all.10.q_ref = bf16[16,272,128]{2,1,0:T(8,128)(2,1)S(1)} all-to-all(bf16[16,272,128]{2,1,0:T(8,128)(2,1)S(1)} %get-tuple-element.12), channel_id=1, replica_groups=mesh['inst'=16,'tp'=8] {'inst'}, dimensions={0} | all-to-all | bytes 2228224 | tf_op jit(solution)/shard_map/all_to_all | solution.py:317
  27.9 0.3 convert_reduce_fusion.info_ref
  28.2 0.0 copy-start.1
  28.3 3.4 %copy-done.1 = bf16[128,1,256,128]{3,2,1,0:T(8,128)(2,1)S(1)} copy-done((bf16[128,1,256,128]{3,2,1,0:T(8,128)(2,1)S(1)}, bf16[128,1,256,128]{3,2,1,0:T(8,128)(2,1)}, u32[]{:S(2)}) %copy-start.1) | copy-done | bytes 8388632
  31.6 0.0 copy-start.2
  31.6 3.4 %copy-done.2 = bf16[128,1,256,128]{3,2,1,0:T(8,128)(2,1)S(1)} copy-done((bf16[128,1,256,128]{3,2,1,0:T(8,128)(2,1)S(1)}, bf16[128,1,256,128]{3,2,1,0:T(8,128)(2,1)}, u32[]{:S(2)}) %copy-start.2) | copy-done | bytes 8388632
  35.0 0.0 copy-start
  35.0 5.6 %attend.1 = bf16[16,272,128]{2,1,0:T(8,128)(2,1)S(1)} custom-call(s32[16,16]{1,0:T(8,128)S(1)} %convert_reduce_fusion.info_ref, bf16[16,272,128]{2,1,0:T(8,128)(2,1)S(1)} %all_to_all.10.q_ref, bf16[128,256,128]{2,1,0:T(8,128)(2,1)S(1)} %bitcast.21, bf16[128,256,128]{2,1,0:T(8,128)(2,1)S(1)} %bitcast.22), custom_call_target="tpu_custom_call" | custom-call | tf_op jit(solution)/shard_map/attend/pallas_call | solution.py:187
  40.6 18.8 %all_to_all.11.got_ref = bf16[16,272,128]{2,1,0:T(8,128)(2,1)S(1)} all-to-all(bf16[16,272,128]{2,1,0:T(8,128)(2,1)S(1)} %attend.1), channel_id=1, replica_groups=mesh['inst'=16,'tp'=8] {'inst'}, dimensions={0} | all-to-all | bytes 2228224 | tf_op jit(solution)/shard_map/all_to_all | solution.py:323
  59.4 0.0 copy-done
  59.4 3.5 %combine.1 = (bf16[4,64,1024]{2,1,0:T(8,128)(2,1)S(1)}, bf16[64,1024]{1,0:T(8,128)(2,1)S(1)}) custom-call(s32[128]{0:T(128)S(1)} %get-tuple-element.11.place_ref, bf16[16,272,128]{2,1,0:T(8,128)(2,1)S(1)} %all_to_all.11.got_ref, f32[16,32,128]{2,1,0:T(8,128)S(1)} %get-tuple-element.13.fresh_ref, f32[2,16,128]{2,1,0:T(8,128)S(1)} %get-tuple-element.14.stat_ref, ...), custom_call_target="tpu_custom_call" | custom-call | tf_op jit(solution)/shard_map/combine/pallas_call | solution.py:260
  62.9 3.5 %collective-permute-start = (bf16[4,64,1024]{2,1,0:T(8,128)(2,1)S(1)}, bf16[4,64,1024]{2,1,0:T(8,128)(2,1)S(1)}, u32[]{:S(2)}, u32[]{:S(2)}) collective-permute-start(bf16[4,64,1024]{2,1,0:T(8,128)(2,1)S(1)} %get-tuple-element.16), channel_id=1, source_target_pairs={{0,1},{1,0},{2,3},{3,2},{4,5},{5,4},{6,7},{7,6},{8,9},{9,8},{10,11... | collective-permute-start | bytes 1572872 | tf_op jit(solution)/shard_map/ppermute | solution.py:326
  66.4 1.6 %keep_half.1 = f32[4,64,1024]{2,1,0:T(8,128)S(1)} custom-call(bf16[64,1024]{1,0:T(8,128)(2,1)S(1)} %get-tuple-element.15.att_ref, bf16[1024,8192]{1,0:T(8,128)(2,1)S(1)} %copy-done), custom_call_target="tpu_custom_call" | custom-call | flops 536870912 | bytes 8388608 | tf_op jit(solution)/shard_map/keep_half/pallas_call | solution.py:294
  68.0 0.0 collective-permute-done
  68.0 0.1 fusion.8
  68.1 1.4 %collective-permute-start.1 = (bf16[64,1024]{1,0:T(8,128)(2,1)S(1)}, bf16[64,1024]{1,0:T(8,128)(2,1)S(1)}, u32[]{:S(2)}, u32[]{:S(2)}) collective-permute-start(bf16[64,1024]{1,0:T(8,128)(2,1)S(1)} %get-tuple-element.17), channel_id=1, source_target_pairs={{0,2},{1,3},{2,4},{3,5},{4,6},{5,7},{6,0},{7,1},{8,10},{9,11},{10,... | collective-permute-start | bytes 393224 | tf_op jit(solution)/shard_map/ppermute | solution.py:330
  69.4 1.5 %collective-permute-start.3 = (bf16[64,1024]{1,0:T(8,128)(2,1)S(1)}, bf16[64,1024]{1,0:T(8,128)(2,1)S(1)}, u32[]{:S(2)}, u32[]{:S(2)}) collective-permute-start(bf16[64,1024]{1,0:T(8,128)(2,1)S(1)} %get-tuple-element.18), channel_id=1, source_target_pairs={{0,6},{1,7},{2,0},{3,1},{4,2},{5,3},{6,4},{7,5},{8,14},{9,15},{10,... | collective-permute-start | bytes 393224 | tf_op jit(solution)/shard_map/ppermute | solution.py:330
  71.0 1.6 %collective-permute-start.2 = (bf16[64,1024]{1,0:T(8,128)(2,1)S(1)}, bf16[64,1024]{1,0:T(8,128)(2,1)S(1)}, u32[]{:S(2)}, u32[]{:S(2)}) collective-permute-start(bf16[64,1024]{1,0:T(8,128)(2,1)S(1)} %get-tuple-element.19), channel_id=1, source_target_pairs={{0,4},{1,5},{2,6},{3,7},{4,0},{5,1},{6,2},{7,3},{8,12},{9,13},{10,... | collective-permute-start | bytes 393224 | tf_op jit(solution)/shard_map/ppermute | solution.py:330
  72.5 1.7 %collective-permute-done.1 = bf16[64,1024]{1,0:T(8,128)(2,1)S(1)} collective-permute-done((bf16[64,1024]{1,0:T(8,128)(2,1)S(1)}, bf16[64,1024]{1,0:T(8,128)(2,1)S(1)}, u32[]{:S(2)}, u32[]{:S(2)}) %collective-permute-start.1) | collective-permute-done | bytes 131104 | tf_op jit(solution)/shard_map/ppermute | solution.py:330
  74.3 0.0 collective-permute-done.3
  74.3 3.9 %collective-permute-done.2 = bf16[64,1024]{1,0:T(8,128)(2,1)S(1)} collective-permute-done((bf16[64,1024]{1,0:T(8,128)(2,1)S(1)}, bf16[64,1024]{1,0:T(8,128)(2,1)S(1)}, u32[]{:S(2)}, u32[]{:S(2)}) %collective-permute-start.2) | collective-permute-done | bytes 131104 | tf_op jit(solution)/shard_map/ppermute | solution.py:330
  78.2 0.7 fusion.7
Async XLA Ops:
  28.2 3.4 %copy-start.1 = (bf16[128,1,256,128]{3,2,1,0:T(8,128)(2,1)S(1)}, bf16[128,1,256,128]{3,2,1,0:T(8,128)(2,1)}, u32[]{:S(2)}) copy-start(bf16[128,1,256,128]{3,2,1,0:T(8,128)(2,1)} %param.11) | copy-start | bytes 25165828
  31.6 3.4 %copy-start.2 = (bf16[128,1,256,128]{3,2,1,0:T(8,128)(2,1)S(1)}, bf16[128,1,256,128]{3,2,1,0:T(8,128)(2,1)}, u32[]{:S(2)}) copy-start(bf16[128,1,256,128]{3,2,1,0:T(8,128)(2,1)} %param.12) | copy-start | bytes 25165828
  35.0 24.4 %copy-start = (bf16[1024,8192]{1,0:T(8,128)(2,1)S(1)}, bf16[1024,8192]{1,0:T(8,128)(2,1)}, u32[]{:S(2)}) copy-start(bf16[1024,8192]{1,0:T(8,128)(2,1)} %w_ref.3) | copy-start | bytes 50331652
  62.9 5.1 %collective-permute-start = (bf16[4,64,1024]{2,1,0:T(8,128)(2,1)S(1)}, bf16[4,64,1024]{2,1,0:T(8,128)(2,1)S(1)}, u32[]{:S(2)}, u32[]{:S(2)}) collective-permute-start(bf16[4,64,1024]{2,1,0:T(8,128)(2,1)S(1)} %get-tuple-element.16), channel_id=1, source_target_pairs={{0,1},{1,0},{2,3},{3,2},{4,5},{5,4},{6,7},{7,6},{8,9},{9,8},{10,11... | collective-permute-start | bytes 1572872 | tf_op jit(solution)/shard_map/ppermute | solution.py:326
  68.1 6.2 %collective-permute-start.1 = (bf16[64,1024]{1,0:T(8,128)(2,1)S(1)}, bf16[64,1024]{1,0:T(8,128)(2,1)S(1)}, u32[]{:S(2)}, u32[]{:S(2)}) collective-permute-start(bf16[64,1024]{1,0:T(8,128)(2,1)S(1)} %get-tuple-element.17), channel_id=1, source_target_pairs={{0,2},{1,3},{2,4},{3,5},{4,6},{5,7},{6,0},{7,1},{8,10},{9,11},{10,... | collective-permute-start | bytes 393224 | tf_op jit(solution)/shard_map/ppermute | solution.py:330
  69.4 4.8 %collective-permute-start.3 = (bf16[64,1024]{1,0:T(8,128)(2,1)S(1)}, bf16[64,1024]{1,0:T(8,128)(2,1)S(1)}, u32[]{:S(2)}, u32[]{:S(2)}) collective-permute-start(bf16[64,1024]{1,0:T(8,128)(2,1)S(1)} %get-tuple-element.18), channel_id=1, source_target_pairs={{0,6},{1,7},{2,0},{3,1},{4,2},{5,3},{6,4},{7,5},{8,14},{9,15},{10,... | collective-permute-start | bytes 393224 | tf_op jit(solution)/shard_map/ppermute | solution.py:330
  71.0 7.2 %collective-permute-start.2 = (bf16[64,1024]{1,0:T(8,128)(2,1)S(1)}, bf16[64,1024]{1,0:T(8,128)(2,1)S(1)}, u32[]{:S(2)}, u32[]{:S(2)}) collective-permute-start(bf16[64,1024]{1,0:T(8,128)(2,1)S(1)} %get-tuple-element.19), channel_id=1, source_target_pairs={{0,4},{1,5},{2,6},{3,7},{4,0},{5,1},{6,2},{7,3},{8,12},{9,13},{10,... | collective-permute-start | bytes 393224 | tf_op jit(solution)/shard_map/ppermute | solution.py:330

commit v3 on v2

--- a/solution.py
+++ b/solution.py
@@ -125,7 +125,7 @@
         ],
         compiler_params=pltpu.CompilerParams(vmem_limit_bytes=8 * 1024 * 1024),
         cost_estimate=pl.CostEstimate(
-            flops=0, bytes_accessed=64 * 1024 * 1024, transcendentals=0
+            flops=2 * 10**10, bytes_accessed=64 * 1024 * 1024, transcendentals=10**7
         ),
         name="prepare",
     )(*(in_hbm(x) for x in (table, lengths, queries, new_keys, new_values)))

time: 79.2 us -> 72.8 us (0.919)
  local copies, waits for them, and re-layouts: 6.76 us -> 0.02 us
    unnamed x6 -> x10, local copies, waits for them, and re-layouts: 6.76 us -> 0.02 us
where the time goes in v3:
time: 72.8 us; the launch traced here: 72.7 us
  blocking collectives  43.9 us (60%)
  Pallas kernels  13.8 us (19%)
  starting transfers between devices  7.94 us (11%)
  waiting for transfers between devices  5.65 us (8%)
  other arithmetic  1.18 us (2%)
    all_to_all x1, blocking collectives, on_device(): asked = lax.all_to_all(payload, 'inst', 0, 0, tiled=True)  25.2 us
    all_to_all x1, blocking collectives, on_device(): got = lax.all_to_all(answer, 'inst', 0, 0, tiled=True)  18.8 us
    ppermute x3, waiting for transfers between devices, on_device(): lax.ppermute((keep[n] + other[n].astype(F32)).astype(BF16), 'tp', [(i, (i...  5.64 us
    pallas_call x1, Pallas kernels, attend(): pl.pallas_call(functools.partial(attend_kernel, rows, chunk), in_specs=[s...  5.6 us
    ppermute x3, starting transfers between devices, on_device(): lax.ppermute((keep[n] + other[n].astype(F32)).astype(BF16), 'tp', [(i, (i...  4.45 us
    pallas_call x1, Pallas kernels, combine(): pl.pallas_call(functools.partial(combine_kernel, drafts), in_specs=[smem,...  3.52 us
    ppermute x1, starting transfers between devices, on_device(): other = lax.ppermute(send, 'tp', [(i, i ^ 1) for i in range(tp)])  3.48 us
    pallas_call x1, Pallas kernels, prepare(): pl.pallas_call(functools.partial(prepare_kernel, shifts), in_specs=[pl.Bl...  3.15 us
  transfers between devices with their start and end apart: 4, of which 2 were waited for; matrix products, arithmetic and copies ran while one was open for 0% of the time, Pallas kernels for 2%

profile of v3, /device:TPU:1, one launch (start us, length us, event | category | flops | bytes accessed | tf_op | source)
XLA Modules:
  0.0 72.7 jit_solution(10565193381194574809)
XLA Ops:
  0.0 0.0 slice-start
  0.0 0.0 slice-start.2
  0.0 0.0 slice-start.1
  0.0 0.0 slice-start.3
  0.0 3.1 %prepare.1 = (bf16[16,272,128]{2,1,0:T(8,128)(2,1)S(1)}, s32[128]{0:T(128)S(1)}, f32[16,32,128]{2,1,0:T(8,128)S(1)}, f32[2,16,128]{2,1,0:T(8,128)S(1)}) custom-call(s32[128]{0:T(128)} %table_hbm.1, s32[16]{0:T(128)} %length_hbm.1, bf16[4,16,8,128]{3,2,1,0:T(8,128)(2,1)} %queries_hbm.1, bf16[64,128]{1,0:T(8,128)(2,1)} %bitcast.27, bf16[64,128]{1,0:T(8,128)(2,1)} %bitcast.28), custom_call_target="tpu_custom_call" | custom-call | flops 20000000000 | bytes 67108864 | tf_op jit(solution)/shard_map/prepare/pallas_call | solution.py:105
  3.2 25.2 %all_to_all.10.q_ref = bf16[16,272,128]{2,1,0:T(8,128)(2,1)S(1)} all-to-all(bf16[16,272,128]{2,1,0:T(8,128)(2,1)S(1)} %get-tuple-element.12), channel_id=1, replica_groups=mesh['inst'=16,'tp'=8] {'inst'}, dimensions={0} | all-to-all | bytes 2228224 | tf_op jit(solution)/shard_map/all_to_all | solution.py:317
  28.3 0.3 convert_reduce_fusion.info_ref
  28.7 0.0 slice-done
  28.7 0.0 slice-done.2
  28.7 0.0 slice-done.1
  28.7 0.0 slice-done.3
  28.7 0.0 copy-start
  28.8 5.6 %attend.1 = bf16[16,272,128]{2,1,0:T(8,128)(2,1)S(1)} custom-call(s32[16,16]{1,0:T(8,128)S(1)} %convert_reduce_fusion.info_ref, bf16[16,272,128]{2,1,0:T(8,128)(2,1)S(1)} %all_to_all.10.q_ref, bf16[128,256,128]{2,1,0:T(8,128)(2,1)S(1)} %bitcast.23, bf16[128,256,128]{2,1,0:T(8,128)(2,1)S(1)} %bitcast.26), custom_call_target="tpu_custom_call" | custom-call | tf_op jit(solution)/shard_map/attend/pallas_call | solution.py:187
  34.4 18.8 %all_to_all.11.got_ref = bf16[16,272,128]{2,1,0:T(8,128)(2,1)S(1)} all-to-all(bf16[16,272,128]{2,1,0:T(8,128)(2,1)S(1)} %attend.1), channel_id=1, replica_groups=mesh['inst'=16,'tp'=8] {'inst'}, dimensions={0} | all-to-all | bytes 2228224 | tf_op jit(solution)/shard_map/all_to_all | solution.py:323
  53.1 0.0 copy-done
  53.1 3.5 %combine.1 = (bf16[4,64,1024]{2,1,0:T(8,128)(2,1)S(1)}, bf16[64,1024]{1,0:T(8,128)(2,1)S(1)}) custom-call(s32[128]{0:T(128)S(1)} %get-tuple-element.11.place_ref, bf16[16,272,128]{2,1,0:T(8,128)(2,1)S(1)} %all_to_all.11.got_ref, f32[16,32,128]{2,1,0:T(8,128)S(1)} %get-tuple-element.13.fresh_ref, f32[2,16,128]{2,1,0:T(8,128)S(1)} %get-tuple-element.14.stat_ref, ...), custom_call_target="tpu_custom_call" | custom-call | tf_op jit(solution)/shard_map/combine/pallas_call | solution.py:260
  56.7 3.5 %collective-permute-start = (bf16[4,64,1024]{2,1,0:T(8,128)(2,1)S(1)}, bf16[4,64,1024]{2,1,0:T(8,128)(2,1)S(1)}, u32[]{:S(2)}, u32[]{:S(2)}) collective-permute-start(bf16[4,64,1024]{2,1,0:T(8,128)(2,1)S(1)} %get-tuple-element.16), channel_id=1, source_target_pairs={{0,1},{1,0},{2,3},{3,2},{4,5},{5,4},{6,7},{7,6},{8,9},{9,8},{10,11... | collective-permute-start | bytes 1572872 | tf_op jit(solution)/shard_map/ppermute | solution.py:326
  60.1 1.6 %keep_half.1 = f32[4,64,1024]{2,1,0:T(8,128)S(1)} custom-call(bf16[64,1024]{1,0:T(8,128)(2,1)S(1)} %get-tuple-element.15.att_ref, bf16[1024,8192]{1,0:T(8,128)(2,1)S(1)} %copy-done), custom_call_target="tpu_custom_call" | custom-call | flops 536870912 | bytes 8388608 | tf_op jit(solution)/shard_map/keep_half/pallas_call | solution.py:294
  61.7 0.0 collective-permute-done
  61.7 0.1 fusion.8
  61.8 1.4 %collective-permute-start.1 = (bf16[64,1024]{1,0:T(8,128)(2,1)S(1)}, bf16[64,1024]{1,0:T(8,128)(2,1)S(1)}, u32[]{:S(2)}, u32[]{:S(2)}) collective-permute-start(bf16[64,1024]{1,0:T(8,128)(2,1)S(1)} %get-tuple-element.17), channel_id=1, source_target_pairs={{0,2},{1,3},{2,4},{3,5},{4,6},{5,7},{6,0},{7,1},{8,10},{9,11},{10,... | collective-permute-start | bytes 393224 | tf_op jit(solution)/shard_map/ppermute | solution.py:330
  63.2 1.5 %collective-permute-start.3 = (bf16[64,1024]{1,0:T(8,128)(2,1)S(1)}, bf16[64,1024]{1,0:T(8,128)(2,1)S(1)}, u32[]{:S(2)}, u32[]{:S(2)}) collective-permute-start(bf16[64,1024]{1,0:T(8,128)(2,1)S(1)} %get-tuple-element.18), channel_id=1, source_target_pairs={{0,6},{1,7},{2,0},{3,1},{4,2},{5,3},{6,4},{7,5},{8,14},{9,15},{10,... | collective-permute-start | bytes 393224 | tf_op jit(solution)/shard_map/ppermute | solution.py:330
  64.7 1.6 %collective-permute-start.2 = (bf16[64,1024]{1,0:T(8,128)(2,1)S(1)}, bf16[64,1024]{1,0:T(8,128)(2,1)S(1)}, u32[]{:S(2)}, u32[]{:S(2)}) collective-permute-start(bf16[64,1024]{1,0:T(8,128)(2,1)S(1)} %get-tuple-element.19), channel_id=1, source_target_pairs={{0,4},{1,5},{2,6},{3,7},{4,0},{5,1},{6,2},{7,3},{8,12},{9,13},{10,... | collective-permute-start | bytes 393224 | tf_op jit(solution)/shard_map/ppermute | solution.py:330
  66.3 1.7 %collective-permute-done.1 = bf16[64,1024]{1,0:T(8,128)(2,1)S(1)} collective-permute-done((bf16[64,1024]{1,0:T(8,128)(2,1)S(1)}, bf16[64,1024]{1,0:T(8,128)(2,1)S(1)}, u32[]{:S(2)}, u32[]{:S(2)}) %collective-permute-start.1) | collective-permute-done | bytes 131104 | tf_op jit(solution)/shard_map/ppermute | solution.py:330
  68.0 0.0 collective-permute-done.3
  68.0 3.9 %collective-permute-done.2 = bf16[64,1024]{1,0:T(8,128)(2,1)S(1)} collective-permute-done((bf16[64,1024]{1,0:T(8,128)(2,1)S(1)}, bf16[64,1024]{1,0:T(8,128)(2,1)S(1)}, u32[]{:S(2)}, u32[]{:S(2)}) %collective-permute-start.2) | collective-permute-done | bytes 131104 | tf_op jit(solution)/shard_map/ppermute | solution.py:330
  71.9 0.7 %fusion.7 = bf16[64,1024]{1,0:T(8,128)(2,1)} fusion(f32[4,64,1024]{2,1,0:T(8,128)S(1)} %keep_half.1, bf16[64,1024]{1,0:T(8,128)(2,1)S(1)} %collective-permute-done.3, bf16[64,1024]{1,0:T(8,128)(2,1)S(1)} %collective-permute-done.2, bf16[64,1024]{1,0:T(8,128)(2,1)S(1)} %collective-permute-done.1, bf16[4,64,1024]{2,1,0:T(8,128)(2,1)S(1)} %collective-permute-done), kind=kLoop, calls=%fused_computation.11 | loop fusion | flops 589824 | bytes 917504 | tf_op jit(solution)/shard_map/convert_element_type | solution.py:340
  (2 shorter events, 0.0 us)
Async XLA Ops:
  0.0 28.7 %slice-start = ((s8[8388608]{0:T(1024)(128)(4,1)}), s8[4194304]{0:T(1024)(128)(4,1)S(1)}, s32[]{:S(2)}) async-start(s8[8388608]{0:T(1024)(128)(4,1)} %bitcast.21), calls=%async_computation.2 | async-start | bytes 8388608
  0.0 28.7 %slice-start.2 = ((s8[8388608]{0:T(1024)(128)(4,1)}), s8[4194304]{0:T(1024)(128)(4,1)S(1)}, s32[]{:S(2)}) async-start(s8[8388608]{0:T(1024)(128)(4,1)} %bitcast.24), calls=%async_computation.4 | async-start | bytes 8388608
  0.0 28.7 %slice-start.1 = ((s8[8388608]{0:T(1024)(128)(4,1)}), s8[4194304]{0:T(1024)(128)(4,1)S(1)}, s32[]{:S(2)}) async-start(s8[8388608]{0:T(1024)(128)(4,1)} %bitcast.21), calls=%async_computation.3 | async-start | bytes 8388608
  0.0 28.7 %slice-start.3 = ((s8[8388608]{0:T(1024)(128)(4,1)}), s8[4194304]{0:T(1024)(128)(4,1)S(1)}, s32[]{:S(2)}) async-start(s8[8388608]{0:T(1024)(128)(4,1)} %bitcast.24), calls=%async_computation.5 | async-start | bytes 8388608
  28.7 24.4 %copy-start = (bf16[1024,8192]{1,0:T(8,128)(2,1)S(1)}, bf16[1024,8192]{1,0:T(8,128)(2,1)}, u32[]{:S(2)}) copy-start(bf16[1024,8192]{1,0:T(8,128)(2,1)} %w_ref.3) | copy-start | bytes 50331652
  56.7 5.1 %collective-permute-start = (bf16[4,64,1024]{2,1,0:T(8,128)(2,1)S(1)}, bf16[4,64,1024]{2,1,0:T(8,128)(2,1)S(1)}, u32[]{:S(2)}, u32[]{:S(2)}) collective-permute-start(bf16[4,64,1024]{2,1,0:T(8,128)(2,1)S(1)} %get-tuple-element.16), channel_id=1, source_target_pairs={{0,1},{1,0},{2,3},{3,2},{4,5},{5,4},{6,7},{7,6},{8,9},{9,8},{10,11... | collective-permute-start | bytes 1572872 | tf_op jit(solution)/shard_map/ppermute | solution.py:326
  61.8 6.2 %collective-permute-start.1 = (bf16[64,1024]{1,0:T(8,128)(2,1)S(1)}, bf16[64,1024]{1,0:T(8,128)(2,1)S(1)}, u32[]{:S(2)}, u32[]{:S(2)}) collective-permute-start(bf16[64,1024]{1,0:T(8,128)(2,1)S(1)} %get-tuple-element.17), channel_id=1, source_target_pairs={{0,2},{1,3},{2,4},{3,5},{4,6},{5,7},{6,0},{7,1},{8,10},{9,11},{10,... | collective-permute-start | bytes 393224 | tf_op jit(solution)/shard_map/ppermute | solution.py:330
  63.2 4.8 %collective-permute-start.3 = (bf16[64,1024]{1,0:T(8,128)(2,1)S(1)}, bf16[64,1024]{1,0:T(8,128)(2,1)S(1)}, u32[]{:S(2)}, u32[]{:S(2)}) collective-permute-start(bf16[64,1024]{1,0:T(8,128)(2,1)S(1)} %get-tuple-element.18), channel_id=1, source_target_pairs={{0,6},{1,7},{2,0},{3,1},{4,2},{5,3},{6,4},{7,5},{8,14},{9,15},{10,... | collective-permute-start | bytes 393224 | tf_op jit(solution)/shard_map/ppermute | solution.py:330
  64.7 7.2 %collective-permute-start.2 = (bf16[64,1024]{1,0:T(8,128)(2,1)S(1)}, bf16[64,1024]{1,0:T(8,128)(2,1)S(1)}, u32[]{:S(2)}, u32[]{:S(2)}) collective-permute-start(bf16[64,1024]{1,0:T(8,128)(2,1)S(1)} %get-tuple-element.19), channel_id=1, source_target_pairs={{0,4},{1,5},{2,6},{3,7},{4,0},{5,1},{6,2},{7,3},{8,12},{9,13},{10,... | collective-permute-start | bytes 393224 | tf_op jit(solution)/shard_map/ppermute | solution.py:330

commit v4 on v3

--- a/solution.py
+++ b/solution.py
@@ -1,4 +1,5 @@
 import functools
+import math
 
 import jax
 import jax.numpy as jnp
@@ -89,7 +90,7 @@
         meta_ref[lender, pl.ds(each + j, 1), :] = jnp.full(lanes, limit.astype(F32), F32)
         return 0
 
-    lax.fori_loop(0, entries, one, 0, unroll=8)
+    lax.fori_loop(0, entries, one, 0, unroll=True)
     out_ref[:, each * rows :, :] = meta_ref[...].astype(BF16)
     draft_block(drafts, q_ref[...], k_ref, v_ref, fresh_ref, stat_ref)
 
@@ -131,43 +132,63 @@
     )(*(in_hbm(x) for x in (table, lengths, queries, new_keys, new_values)))
 
 
-def attend_kernel(rows, chunk, info_ref, q_ref, k_ref, v_ref, out_ref, stat_ref):
+def attend_kernel(
+    rows, ahead, behind, q_ref, k_ref, v_ref, out_ref, number_ref, info_ref, sem
+):
     block, head = k_ref.shape[1:]
     lenders = out_ref.shape[0]
     each = (out_ref.shape[1] - META) // rows
+    entries = lenders * each
     scale = head ** (-0.5)
-    lane = lax.broadcasted_iota(jnp.int32, (rows, block), 1)
+    fast = scale * math.log2(math.e)
+
+    lane = lax.broadcasted_iota(jnp.int32, (META, head), 1)
+    row = lax.broadcasted_iota(jnp.int32, (META, head), 0)
+    for n in range(lenders):
+        meta = jnp.where(lane == row, q_ref[n, each * rows :, :].astype(F32), 0.0)
+        number_ref[n : n + 1, :] = jnp.sum(meta, axis=0, keepdims=True).astype(jnp.int32)
+    copy = pltpu.make_async_copy(number_ref, info_ref, sem)
+    copy.start()
+    copy.wait()
+
+    token = lax.broadcasted_iota(jnp.int32, (8, block), 1)
     column = lax.broadcasted_iota(jnp.int32, (rows, head), 1)
-    near = chunk // each
-
-    def some(step, _):
-        of = [(step * near + i // each, i % each) for i in range(chunk)]
-        slot = [info_ref[n, j] for n, j in of]
-        limit = [info_ref[n, each + j] for n, j in of]
-        scores = [
-            lax.dot_general(
-                q_ref[n, j * rows : (j + 1) * rows, :],
-                k_ref[slot[i]],
+    slot = [info_ref[i // each, i % each] for i in range(entries)]
+    limit = [info_ref[i // each, each + i % each] for i in range(entries)]
+
+    def here(i):
+        return i // each, pl.ds(i % each * rows, rows), slice(None)
+
+    scores, soft, outs = {}, {}, {}
+    peaks = jnp.zeros((rows, head), F32)
+    totals = jnp.ones((rows, head), F32)
+    for i in range(-ahead, entries + 2 * behind):
+        if i + ahead < entries:
+            n = i + ahead
+            scores[n] = lax.dot_general(
+                q_ref[here(n)],
+                k_ref[slot[n]],
                 (((1,), (1,)), ((), ())),
                 preferred_element_type=F32,
             )
-            for i, (n, j) in enumerate(of)
-        ]
-        stat = stat_ref[...]
-        for i, (n, j) in enumerate(of):
-            s = jnp.where(lane < limit[i], scores[i] * scale, NEG)
+        if 0 <= i < entries:
+            bias = jnp.where(token < limit[i], 0.0, NEG)
+            s = scores.pop(i).reshape(rows // 8, 8, block) + bias[None]
+            s = s.reshape(rows, block)
             peak = jnp.max(s, axis=1, keepdims=True)
-            weight = jnp.exp(s - peak)
-            total = jnp.sum(weight, axis=1, keepdims=True)
-            summed = jnp.dot(weight.astype(BF16), v_ref[slot[i]], preferred_element_type=F32)
-            out_ref[n, j * rows : (j + 1) * rows, :] = (summed * (1.0 / total)).astype(BF16)
-            lse = jnp.where(limit[i] > 0, peak + jnp.log(total), NEG)
-            stat = jnp.where(column == step * chunk + i, lse, stat)
-        stat_ref[...] = stat
-        return 0
-
-    lax.fori_loop(0, lenders * each // chunk, some, 0)
-    x = stat_ref[...]
+            weight = jnp.exp2((s - peak) * fast)
+            soft[i] = peak, jnp.sum(weight, axis=1, keepdims=True), weight.astype(BF16)
+        if 0 <= i - behind < entries:
+            n = i - behind
+            outs[n] = jnp.dot(soft[n][2], v_ref[slot[n]], preferred_element_type=F32)
+        if 0 <= i - 2 * behind < entries:
+            n = i - 2 * behind
+            peak, total, _ = soft.pop(n)
+            out_ref[here(n)] = (outs.pop(n) * (1.0 / total)).astype(BF16)
+            peaks = jnp.where(column == n, peak, peaks)
+            totals = jnp.where(column == n, total, totals)
+
+    x = peaks * scale + jnp.log(totals)
     hi = x.astype(BF16).astype(F32)
     rest = x - hi
     mid = rest.astype(BF16).astype(F32)
@@ -181,18 +202,23 @@
         out_ref[i, each * rows :, :] = part.astype(BF16)
 
 
-def attend(info, q, keys, values, rows, chunk):
-    pool, block, head = keys.shape
-    vmem, smem = pl.BlockSpec(memory_space=pltpu.VMEM), pl.BlockSpec(memory_space=pltpu.SMEM)
+def attend(q, keys, values, rows):
+    lenders = q.shape[0]
+    head = q.shape[2]
+    vmem = pl.BlockSpec(memory_space=pltpu.VMEM)
     return pl.pallas_call(
-        functools.partial(attend_kernel, rows, chunk),
-        in_specs=[smem, vmem, vmem, vmem],
+        functools.partial(attend_kernel, rows, 8, 4),
+        in_specs=[vmem, vmem, vmem],
         out_specs=vmem,
         out_shape=jax.ShapeDtypeStruct(q.shape, BF16),
-        scratch_shapes=[pltpu.VMEM((rows, pool), F32)],
+        scratch_shapes=[
+            pltpu.VMEM((lenders, head), jnp.int32),
+            pltpu.SMEM((lenders, head), jnp.int32),
+            pltpu.SemaphoreType.DMA,
+        ],
         compiler_params=pltpu.CompilerParams(vmem_limit_bytes=16 * 1024 * 1024),
         name="attend",
-    )(info, q, keys, values)
+    )(q, keys, values)
 
 
 def combine_kernel(
@@ -219,20 +245,42 @@
     weight = jnp.exp(lse - top[:, None])
     fresh_weight = jnp.exp(fresh_peak - top)
     part = 1.0 / (jnp.sum(weight, axis=1) + stat_ref[1] * fresh_weight)
-    weight = (weight * part[:, None]).reshape(entries, head).T
+    lane = lax.broadcasted_iota(jnp.int32, (entries, head), 1)
+    weight = jnp.where(lane < rows, (weight * part[:, None]).reshape(entries, head), 0.0)
     fresh_weight = fresh_weight * part
     fresh_weight = jnp.concatenate(
         [fresh_weight, jnp.zeros((head - requests, head), F32)], axis=0
     ).T
+    beside = head // rows
+    rows_bits = rows.bit_length() - 1
+    spread = weight
+    for n in range(1, beside):
+        spread = spread + pltpu.roll(weight, n * rows, 1)
+    lane = lax.broadcasted_iota(jnp.int32, (blocks, head), 1)
+    near = lax.broadcasted_iota(jnp.int32, (blocks, head), 0) - lax.shift_right_logical(
+        lane, rows_bits
+    )
+    diagonal = lax.broadcasted_iota(jnp.int32, (rows, head), 0) == (
+        lax.broadcasted_iota(jnp.int32, (rows, head), 1) & (rows - 1)
+    )
     for r in range(requests):
-        acc = fresh_ref[r] * fresh_weight[:rows, r : r + 1]
+        mine = spread[r * blocks : (r + 1) * blocks]
+        high, low, parts = [], [], []
+        for n in range(0, blocks, beside):
+            line = jnp.sum(jnp.where(near == n, mine, 0.0), axis=0, keepdims=True)
+            square = jnp.where(diagonal, line, 0.0)
+            high.append(square.astype(BF16))
+            low.append((square - high[-1].astype(F32)).astype(BF16))
         for b in range(blocks):
-            e = r * blocks + b
-            place = place_ref[e]
+            place = place_ref[r * blocks + b]
             lender = lax.shift_right_logical(place, each_bits)
             start = pl.multiple_of((place & (each - 1)) * rows, rows)
-            block_out = got_ref[lender, pl.ds(start, rows), :]
-            acc += block_out.astype(F32) * weight[:rows, e : e + 1]
+            parts.append(got_ref[lender, pl.ds(start, rows), :])
+        left = jnp.concatenate(
+            [jnp.concatenate(high, axis=1), jnp.concatenate(low, axis=1)], axis=0
+        )
+        both = jnp.dot(left, jnp.concatenate(parts, axis=0), preferred_element_type=F32)
+        acc = both[:rows] + both[rows:] + fresh_ref[r] * fresh_weight[:rows, r : r + 1]
         for d in range(drafts):
             rows_ref[pl.ds((d * requests + r) * group, group), :] = acc[
                 d * group : (d + 1) * group
@@ -315,10 +363,8 @@
         block_table, context_len, queries, new_keys.reshape(-1, head), new_values.reshape(-1, head), block
     )
     asked = lax.all_to_all(payload, "inst", 0, 0, tiled=True)
-    each = pool // asked.shape[0]
-    info = asked[:, each * rows :, 0].astype(jnp.int32)
     answer = attend(
-        info, asked, key_pool.reshape(pool, block, head), value_pool.reshape(pool, block, head), rows, 32
+        asked, key_pool.reshape(pool, block, head), value_pool.reshape(pool, block, head), rows
     )
     got = lax.all_to_all(answer, "inst", 0, 0, tiled=True)
 
@@ -332,7 +378,7 @@
             "tp",
             [(i, (i + 2 * n) % tp) for i in range(tp)],
         )
-        for n in range(1, ring)
+        for n in (2, 1, 3)
     ]
     total = keep[0] + other[0].astype(F32)
     for part in parts:

time: 72.8 us -> 69.9 us (0.960)
  Pallas kernels: 13.8 us -> 11.8 us
    pallas_call x1, Pallas kernels: 5.6 us -> 4.53 us  [attend(): pl.pallas_call(functools.partial(attend_kernel, rows, 8, 4), in_specs=[vm...]
where the time goes in v4:
time: 69.9 us; the launch traced here: 69.8 us
  blocking collectives  44.1 us (63%)
  Pallas kernels  11.8 us (17%)
  starting transfers between devices  7.94 us (11%)
  waiting for transfers between devices  5.04 us (7%)
  other arithmetic  0.83 us (1%)
    all_to_all x1, blocking collectives, on_device(): asked = lax.all_to_all(payload, 'inst', 0, 0, tiled=True)  25.2 us
    all_to_all x1, blocking collectives, on_device(): got = lax.all_to_all(answer, 'inst', 0, 0, tiled=True)  18.9 us
    ppermute x3, waiting for transfers between devices, on_device(): lax.ppermute((keep[n] + other[n].astype(F32)).astype(BF16), 'tp', [(i, (i...  5.04 us
    pallas_call x1, Pallas kernels, attend(): pl.pallas_call(functools.partial(attend_kernel, rows, 8, 4), in_specs=[vm...  4.53 us
    ppermute x3, starting transfers between devices, on_device(): lax.ppermute((keep[n] + other[n].astype(F32)).astype(BF16), 'tp', [(i, (i...  4.46 us
    ppermute x1, starting transfers between devices, on_device(): other = lax.ppermute(send, 'tp', [(i, i ^ 1) for i in range(tp)])  3.48 us
    pallas_call x1, Pallas kernels, prepare(): pl.pallas_call(functools.partial(prepare_kernel, shifts), in_specs=[pl.Bl...  2.87 us
    pallas_call x1, Pallas kernels, combine(): pl.pallas_call(functools.partial(combine_kernel, drafts), in_specs=[smem,...  2.81 us
  transfers between devices with their start and end apart: 4, of which 2 were waited for; matrix products, arithmetic and copies ran while one was open for 0% of the time, Pallas kernels for 2%

profile of v4, /device:TPU:1, one launch (start us, length us, event | category | flops | bytes accessed | tf_op | source)
XLA Modules:
  0.0 69.8 jit_solution(9320835590019534365)
XLA Ops:
  0.0 0.0 slice-start
  0.0 0.0 slice-start.2
  0.0 0.0 slice-start.1
  0.0 0.0 slice-start.3
  0.0 2.9 %prepare.1 = (bf16[16,272,128]{2,1,0:T(8,128)(2,1)S(1)}, s32[128]{0:T(128)S(1)}, f32[16,32,128]{2,1,0:T(8,128)S(1)}, f32[2,16,128]{2,1,0:T(8,128)S(1)}) custom-call(s32[128]{0:T(128)} %table_hbm.1, s32[16]{0:T(128)} %length_hbm.1, bf16[4,16,8,128]{3,2,1,0:T(8,128)(2,1)} %queries_hbm.1, bf16[64,128]{1,0:T(8,128)(2,1)} %bitcast.27, bf16[64,128]{1,0:T(8,128)(2,1)} %bitcast.28), custom_call_target="tpu_custom_call" | custom-call | flops 20000000000 | bytes 67108864 | tf_op jit(solution)/shard_map/prepare/pallas_call | solution.py:106
  2.9 25.2 %all_to_all.10.q_ref = bf16[16,272,128]{2,1,0:T(8,128)(2,1)S(1)} all-to-all(bf16[16,272,128]{2,1,0:T(8,128)(2,1)S(1)} %get-tuple-element.12), channel_id=1, replica_groups=mesh['inst'=16,'tp'=8] {'inst'}, dimensions={0} | all-to-all | bytes 2228224 | tf_op jit(solution)/shard_map/all_to_all | solution.py:365
  28.1 0.0 slice-done
  28.1 0.0 slice-done.2
  28.1 0.0 slice-done.1
  28.1 0.0 slice-done.3
  28.1 0.0 copy-start
  28.1 4.5 %attend.1 = bf16[16,272,128]{2,1,0:T(8,128)(2,1)S(1)} custom-call(bf16[16,272,128]{2,1,0:T(8,128)(2,1)S(1)} %all_to_all.10.q_ref, bf16[128,256,128]{2,1,0:T(8,128)(2,1)S(1)} %bitcast.23, bf16[128,256,128]{2,1,0:T(8,128)(2,1)S(1)} %bitcast.26), custom_call_target="tpu_custom_call" | custom-call | tf_op jit(solution)/shard_map/attend/pallas_call | solution.py:209
  32.6 18.9 %all_to_all.11.got_ref = bf16[16,272,128]{2,1,0:T(8,128)(2,1)S(1)} all-to-all(bf16[16,272,128]{2,1,0:T(8,128)(2,1)S(1)} %attend.1), channel_id=1, replica_groups=mesh['inst'=16,'tp'=8] {'inst'}, dimensions={0} | all-to-all | bytes 2228224 | tf_op jit(solution)/shard_map/all_to_all | solution.py:369
  51.6 0.0 copy-done
  51.6 2.8 %combine.1 = (bf16[4,64,1024]{2,1,0:T(8,128)(2,1)S(1)}, bf16[64,1024]{1,0:T(8,128)(2,1)S(1)}) custom-call(s32[128]{0:T(128)S(1)} %get-tuple-element.11.place_ref, bf16[16,272,128]{2,1,0:T(8,128)(2,1)S(1)} %all_to_all.11.got_ref, f32[16,32,128]{2,1,0:T(8,128)S(1)} %get-tuple-element.13.fresh_ref, f32[2,16,128]{2,1,0:T(8,128)S(1)} %get-tuple-element.14.stat_ref, ...), custom_call_target="tpu_custom_call" | custom-call | tf_op jit(solution)/shard_map/combine/pallas_call | solution.py:308
  54.4 3.5 %collective-permute-start = (bf16[4,64,1024]{2,1,0:T(8,128)(2,1)S(1)}, bf16[4,64,1024]{2,1,0:T(8,128)(2,1)S(1)}, u32[]{:S(2)}, u32[]{:S(2)}) collective-permute-start(bf16[4,64,1024]{2,1,0:T(8,128)(2,1)S(1)} %get-tuple-element.16), channel_id=1, source_target_pairs={{0,1},{1,0},{2,3},{3,2},{4,5},{5,4},{6,7},{7,6},{8,9},{9,8},{10,11... | collective-permute-start | bytes 1572872 | tf_op jit(solution)/shard_map/ppermute | solution.py:372
  57.9 1.6 %keep_half.1 = f32[4,64,1024]{2,1,0:T(8,128)S(1)} custom-call(bf16[64,1024]{1,0:T(8,128)(2,1)S(1)} %get-tuple-element.15.att_ref, bf16[1024,8192]{1,0:T(8,128)(2,1)S(1)} %copy-done), custom_call_target="tpu_custom_call" | custom-call | flops 536870912 | bytes 8388608 | tf_op jit(solution)/shard_map/keep_half/pallas_call | solution.py:342
  59.4 0.0 collective-permute-done
  59.4 0.1 fusion.8
  59.5 3.0 %collective-permute-start.1 = (bf16[64,1024]{1,0:T(8,128)(2,1)S(1)}, bf16[64,1024]{1,0:T(8,128)(2,1)S(1)}, u32[]{:S(2)}, u32[]{:S(2)}) collective-permute-start(bf16[64,1024]{1,0:T(8,128)(2,1)S(1)} %get-tuple-element.17), channel_id=1, source_target_pairs={{0,4},{1,5},{2,6},{3,7},{4,0},{5,1},{6,2},{7,3},{8,12},{9,13},{10,... | collective-permute-start | bytes 393224 | tf_op jit(solution)/shard_map/ppermute | solution.py:376
  62.5 0.8 %collective-permute-start.3 = (bf16[64,1024]{1,0:T(8,128)(2,1)S(1)}, bf16[64,1024]{1,0:T(8,128)(2,1)S(1)}, u32[]{:S(2)}, u32[]{:S(2)}) collective-permute-start(bf16[64,1024]{1,0:T(8,128)(2,1)S(1)} %get-tuple-element.18), channel_id=1, source_target_pairs={{0,6},{1,7},{2,0},{3,1},{4,2},{5,3},{6,4},{7,5},{8,14},{9,15},{10,... | collective-permute-start | bytes 393224 | tf_op jit(solution)/shard_map/ppermute | solution.py:376
  63.3 0.7 collective-permute-start.2
  64.0 1.9 %collective-permute-done.1 = bf16[64,1024]{1,0:T(8,128)(2,1)S(1)} collective-permute-done((bf16[64,1024]{1,0:T(8,128)(2,1)S(1)}, bf16[64,1024]{1,0:T(8,128)(2,1)S(1)}, u32[]{:S(2)}, u32[]{:S(2)}) %collective-permute-start.1) | collective-permute-done | bytes 131104 | tf_op jit(solution)/shard_map/ppermute | solution.py:376
  65.9 3.1 %collective-permute-done.3 = bf16[64,1024]{1,0:T(8,128)(2,1)S(1)} collective-permute-done((bf16[64,1024]{1,0:T(8,128)(2,1)S(1)}, bf16[64,1024]{1,0:T(8,128)(2,1)S(1)}, u32[]{:S(2)}, u32[]{:S(2)}) %collective-permute-start.3) | collective-permute-done | bytes 131104 | tf_op jit(solution)/shard_map/ppermute | solution.py:376
  69.0 0.0 collective-permute-done.2
  69.0 0.7 %fusion.7 = bf16[64,1024]{1,0:T(8,128)(2,1)} fusion(f32[4,64,1024]{2,1,0:T(8,128)S(1)} %keep_half.1, bf16[64,1024]{1,0:T(8,128)(2,1)S(1)} %collective-permute-done.3, bf16[64,1024]{1,0:T(8,128)(2,1)S(1)} %collective-permute-done.2, bf16[64,1024]{1,0:T(8,128)(2,1)S(1)} %collective-permute-done.1, bf16[4,64,1024]{2,1,0:T(8,128)(2,1)S(1)} %collective-permute-done), kind=kLoop, calls=%fused_computation.11 | loop fusion | flops 589824 | bytes 917504 | tf_op jit(solution)/shard_map/convert_element_type | solution.py:386
  (2 shorter events, 0.0 us)
Async XLA Ops:
  0.0 28.1 %slice-start = ((s8[8388608]{0:T(1024)(128)(4,1)}), s8[4194304]{0:T(1024)(128)(4,1)S(1)}, s32[]{:S(2)}) async-start(s8[8388608]{0:T(1024)(128)(4,1)} %bitcast.21), calls=%async_computation.2 | async-start | bytes 8388608
  0.0 28.1 %slice-start.2 = ((s8[8388608]{0:T(1024)(128)(4,1)}), s8[4194304]{0:T(1024)(128)(4,1)S(1)}, s32[]{:S(2)}) async-start(s8[8388608]{0:T(1024)(128)(4,1)} %bitcast.24), calls=%async_computation.4 | async-start | bytes 8388608
  0.0 28.1 %slice-start.1 = ((s8[8388608]{0:T(1024)(128)(4,1)}), s8[4194304]{0:T(1024)(128)(4,1)S(1)}, s32[]{:S(2)}) async-start(s8[8388608]{0:T(1024)(128)(4,1)} %bitcast.21), calls=%async_computation.3 | async-start | bytes 8388608
  0.0 28.1 %slice-start.3 = ((s8[8388608]{0:T(1024)(128)(4,1)}), s8[4194304]{0:T(1024)(128)(4,1)S(1)}, s32[]{:S(2)}) async-start(s8[8388608]{0:T(1024)(128)(4,1)} %bitcast.24), calls=%async_computation.5 | async-start | bytes 8388608
  28.1 23.5 %copy-start = (bf16[1024,8192]{1,0:T(8,128)(2,1)S(1)}, bf16[1024,8192]{1,0:T(8,128)(2,1)}, u32[]{:S(2)}) copy-start(bf16[1024,8192]{1,0:T(8,128)(2,1)} %w_ref.3) | copy-start | bytes 50331652
  54.4 5.1 %collective-permute-start = (bf16[4,64,1024]{2,1,0:T(8,128)(2,1)S(1)}, bf16[4,64,1024]{2,1,0:T(8,128)(2,1)S(1)}, u32[]{:S(2)}, u32[]{:S(2)}) collective-permute-start(bf16[4,64,1024]{2,1,0:T(8,128)(2,1)S(1)} %get-tuple-element.16), channel_id=1, source_target_pairs={{0,1},{1,0},{2,3},{3,2},{4,5},{5,4},{6,7},{7,6},{8,9},{9,8},{10,11... | collective-permute-start | bytes 1572872 | tf_op jit(solution)/shard_map/ppermute | solution.py:372
  59.5 6.3 %collective-permute-start.1 = (bf16[64,1024]{1,0:T(8,128)(2,1)S(1)}, bf16[64,1024]{1,0:T(8,128)(2,1)S(1)}, u32[]{:S(2)}, u32[]{:S(2)}) collective-permute-start(bf16[64,1024]{1,0:T(8,128)(2,1)S(1)} %get-tuple-element.17), channel_id=1, source_target_pairs={{0,4},{1,5},{2,6},{3,7},{4,0},{5,1},{6,2},{7,3},{8,12},{9,13},{10,... | collective-permute-start | bytes 393224 | tf_op jit(solution)/shard_map/ppermute | solution.py:376
  62.5 6.5 %collective-permute-start.3 = (bf16[64,1024]{1,0:T(8,128)(2,1)S(1)}, bf16[64,1024]{1,0:T(8,128)(2,1)S(1)}, u32[]{:S(2)}, u32[]{:S(2)}) collective-permute-start(bf16[64,1024]{1,0:T(8,128)(2,1)S(1)} %get-tuple-element.18), channel_id=1, source_target_pairs={{0,6},{1,7},{2,0},{3,1},{4,2},{5,3},{6,4},{7,5},{8,14},{9,15},{10,... | collective-permute-start | bytes 393224 | tf_op jit(solution)/shard_map/ppermute | solution.py:376
  63.3 5.7 %collective-permute-start.2 = (bf16[64,1024]{1,0:T(8,128)(2,1)S(1)}, bf16[64,1024]{1,0:T(8,128)(2,1)S(1)}, u32[]{:S(2)}, u32[]{:S(2)}) collective-permute-start(bf16[64,1024]{1,0:T(8,128)(2,1)S(1)} %get-tuple-element.19), channel_id=1, source_target_pairs={{0,2},{1,3},{2,4},{3,5},{4,6},{5,7},{6,0},{7,1},{8,10},{9,11},{10,... | collective-permute-start | bytes 393224 | tf_op jit(solution)/shard_map/ppermute | solution.py:376

commit v5 on v4

--- a/solution.py
+++ b/solution.py
@@ -11,7 +11,8 @@
 NEG = -1e30
 F32 = jnp.float32
 BF16 = jnp.bfloat16
-META = 16
+META = 8
+EARLY = 512
 
 
 def in_hbm(x):
@@ -48,94 +49,103 @@
             stat_ref[n, r : r + 1, :] = piece
 
 
+def weight_copy(w_hbm, w_ref, start, stop, sem):
+    here = pl.ds(start, stop - start)
+    return pltpu.make_async_copy(w_hbm.at[here], w_ref.at[here], sem)
+
+
 def prepare_kernel(
-    shifts, table_hbm, length_hbm, queries_hbm, k_hbm, v_hbm,
-    out_ref, place_ref, fresh_ref, stat_ref,
-    table_ref, length_ref, queries_ref, k_ref, v_ref, q_ref, meta_ref, count_ref, sems,
+    shifts, table_hbm, length_hbm, queries_hbm, w_hbm,
+    out_ref, place_ref, q_ref, w_ref,
+    table_ref, length_ref, queries_ref, meta_ref, count_ref, sems, w_sem,
 ):
-    pairs = (
-        (table_hbm, table_ref), (length_hbm, length_ref), (queries_hbm, queries_ref),
-        (k_hbm, k_ref), (v_hbm, v_ref),
-    )
-    copies = [pltpu.make_async_copy(a, b, sems.at[i]) for i, (a, b) in enumerate(pairs)]
-    for copy in copies:
-        copy.start()
     drafts, requests, group, head = queries_ref.shape
     lenders = out_ref.shape[0]
     rows = drafts * group
     entries = table_ref.shape[0]
     each = entries // lenders
-    pool_bits, blocks_bits, block_bits = shifts
-
+    blocks = entries // requests
+    pool_bits, each_bits, block_bits = shifts
+    pairs = ((table_hbm, table_ref), (length_hbm, length_ref), (queries_hbm, queries_ref))
+    copies = [pltpu.make_async_copy(a, b, sems.at[i]) for i, (a, b) in enumerate(pairs)]
+    for copy in copies:
+        copy.start()
     for i in range(lenders):
         count_ref[i] = 0
-    for copy in copies:
-        copy.wait()
-    for r in range(requests):
-        q_ref[r] = jnp.concatenate([queries_ref[d, r] for d in range(drafts)], axis=0)
-
-    def one(e, _):
+    first_half = lax.broadcasted_iota(jnp.int32, (1, head), 1) < head // 2
+    copies[0].wait()
+    copies[1].wait()
+    for e in range(entries):
         slot = table_ref[e]
         lender = lax.shift_right_logical(slot, pool_bits)
         j = count_ref[lender]
         count_ref[lender] = j + 1
         place_ref[e] = lender * each + j
-        r = lax.shift_right_logical(e, blocks_bits)
-        start = lax.shift_left(e & ((1 << blocks_bits) - 1), block_bits)
-        limit = jnp.clip(length_ref[r] - start, 0, 1 << block_bits)
-        out_ref[lender, pl.ds(pl.multiple_of(j * rows, rows), rows), :] = q_ref[r]
-        lanes = (1, head)
+        limit = jnp.clip(length_ref[e // blocks] - (e % blocks << block_bits), 0, 1 << block_bits)
         inner = slot & ((1 << pool_bits) - 1)
-        meta_ref[lender, pl.ds(j, 1), :] = jnp.full(lanes, inner.astype(F32), F32)
-        meta_ref[lender, pl.ds(each + j, 1), :] = jnp.full(lanes, limit.astype(F32), F32)
-        return 0
-
-    lax.fori_loop(0, entries, one, 0, unroll=True)
+        meta_ref[lender, pl.ds(j, 1), :] = jnp.where(first_half, inner, limit).astype(F32)
+    copies[2].wait()
+    for r in range(requests):
+        q = jnp.concatenate([queries_ref[d, r] for d in range(drafts)], axis=0)
+        q_ref[r] = q
+        for b in range(blocks):
+            place = place_ref[r * blocks + b]
+            lender = lax.shift_right_logical(place, each_bits)
+            start = pl.multiple_of((place & (each - 1)) * rows, rows)
+            out_ref[lender, pl.ds(start, rows), :] = q
     out_ref[:, each * rows :, :] = meta_ref[...].astype(BF16)
-    draft_block(drafts, q_ref[...], k_ref, v_ref, fresh_ref, stat_ref)
-
-
-def prepare(table, lengths, queries, new_keys, new_values, block):
+
+    @pl.when(lax.axis_index("tp") & 1 == 0)
+    def _():
+        copy = weight_copy(w_hbm, w_ref, 0, EARLY, w_sem)
+        copy.start()
+        copy.wait()
+
+
+def prepare(table, lengths, queries, w, block):
     drafts, requests, group, head = queries.shape
     rows = drafts * group
     entries = table.shape[0]
     lenders = lax.axis_size("inst")
     each = entries // lenders
-    shifts = tuple(n.bit_length() - 1 for n in (entries, entries // requests, block))
+    shifts = tuple(n.bit_length() - 1 for n in (entries, each, block))
     vmem, smem = pl.BlockSpec(memory_space=pltpu.VMEM), pl.BlockSpec(memory_space=pltpu.SMEM)
     return pl.pallas_call(
         functools.partial(prepare_kernel, shifts),
-        in_specs=[pl.BlockSpec(memory_space=pltpu.HBM)] * 5,
+        in_specs=[pl.BlockSpec(memory_space=pltpu.HBM)] * 4,
         out_specs=[vmem, smem, vmem, vmem],
         out_shape=[
             jax.ShapeDtypeStruct((lenders, each * rows + META, head), BF16),
             jax.ShapeDtypeStruct((entries,), jnp.int32),
-            jax.ShapeDtypeStruct((requests, rows, head), F32),
-            jax.ShapeDtypeStruct((2, requests, head), F32),
+            jax.ShapeDtypeStruct((requests, rows, head), BF16),
+            pltpu.VMEM(w.shape, BF16),
         ],
         scratch_shapes=[
             pltpu.SMEM(table.shape, jnp.int32),
             pltpu.SMEM(lengths.shape, jnp.int32),
             pltpu.VMEM(queries.shape, BF16),
-            pltpu.VMEM(new_keys.shape, BF16),
-            pltpu.VMEM(new_values.shape, BF16),
-            pltpu.VMEM((requests, rows, head), BF16),
             pltpu.VMEM((lenders, META, head), F32),
             pltpu.SMEM((lenders,), jnp.int32),
-            pltpu.SemaphoreType.DMA((5,)),
+            pltpu.SemaphoreType.DMA((3,)),
+            pltpu.SemaphoreType.DMA,
         ],
         compiler_params=pltpu.CompilerParams(vmem_limit_bytes=8 * 1024 * 1024),
         cost_estimate=pl.CostEstimate(
             flops=2 * 10**10, bytes_accessed=64 * 1024 * 1024, transcendentals=10**7
         ),
         name="prepare",
-    )(*(in_hbm(x) for x in (table, lengths, queries, new_keys, new_values)))
+    )(*(in_hbm(x) for x in (table, lengths, queries, w)))
 
 
 def attend_kernel(
-    rows, ahead, behind, q_ref, k_ref, v_ref, out_ref, number_ref, info_ref, sem
+    drafts, ahead, behind, q_ref, k_ref, v_ref, own_ref, new_k_ref, new_v_ref, w_hbm, w_in,
+    out_ref, fresh_ref, stat_ref, w_ref, number_ref, info_ref, sem, w_sem,
 ):
+    others = weight_copy(w_hbm, w_ref, EARLY, w_ref.shape[0], w_sem)
+    others.start()
+
     block, head = k_ref.shape[1:]
+    rows = own_ref.shape[1]
     lenders = out_ref.shape[0]
     each = (out_ref.shape[1] - META) // rows
     entries = lenders * each
@@ -145,7 +155,7 @@
     lane = lax.broadcasted_iota(jnp.int32, (META, head), 1)
     row = lax.broadcasted_iota(jnp.int32, (META, head), 0)
     for n in range(lenders):
-        meta = jnp.where(lane == row, q_ref[n, each * rows :, :].astype(F32), 0.0)
+        meta = jnp.where(lane & (head // 2 - 1) == row, q_ref[n, each * rows :, :].astype(F32), 0.0)
         number_ref[n : n + 1, :] = jnp.sum(meta, axis=0, keepdims=True).astype(jnp.int32)
     copy = pltpu.make_async_copy(number_ref, info_ref, sem)
     copy.start()
@@ -154,7 +164,7 @@
     token = lax.broadcasted_iota(jnp.int32, (8, block), 1)
     column = lax.broadcasted_iota(jnp.int32, (rows, head), 1)
     slot = [info_ref[i // each, i % each] for i in range(entries)]
-    limit = [info_ref[i // each, each + i % each] for i in range(entries)]
+    limit = [info_ref[i // each, head // 2 + i % each] for i in range(entries)]
 
     def here(i):
         return i // each, pl.ds(i % each * rows, rows), slice(None)
@@ -163,6 +173,8 @@
     peaks = jnp.zeros((rows, head), F32)
     totals = jnp.ones((rows, head), F32)
     for i in range(-ahead, entries + 2 * behind):
+        if i == 32:
+            draft_block(drafts, own_ref[...], new_k_ref, new_v_ref, fresh_ref, stat_ref)
         if i + ahead < entries:
             n = i + ahead
             scores[n] = lax.dot_general(
@@ -196,35 +208,46 @@
     stack = jnp.concatenate([hi, mid, low, jnp.zeros((head - 3 * rows, head), F32)], axis=0)
     turned = stack.T
     for i in range(lenders):
-        part = jnp.concatenate(
-            [turned[i * each : (i + 1) * each], jnp.zeros((META - each, head), F32)], axis=0
-        )
-        out_ref[i, each * rows :, :] = part.astype(BF16)
-
-
-def attend(q, keys, values, rows):
+        out_ref[i, each * rows :, :] = turned[i * each : (i + 1) * each].astype(BF16)
+    others.wait()
+
+
+def attend(q, keys, values, own, new_keys, new_values, w, w_part, drafts):
     lenders = q.shape[0]
-    head = q.shape[2]
+    requests, rows, head = own.shape
     vmem = pl.BlockSpec(memory_space=pltpu.VMEM)
     return pl.pallas_call(
-        functools.partial(attend_kernel, rows, 8, 4),
-        in_specs=[vmem, vmem, vmem],
-        out_specs=vmem,
-        out_shape=jax.ShapeDtypeStruct(q.shape, BF16),
+        functools.partial(attend_kernel, drafts, 8, 4),
+        in_specs=[vmem] * 6 + [pl.BlockSpec(memory_space=pltpu.HBM), vmem],
+        out_specs=[vmem] * 4,
+        out_shape=[
+            jax.ShapeDtypeStruct(q.shape, BF16),
+            jax.ShapeDtypeStruct((requests, rows, head), F32),
+            jax.ShapeDtypeStruct((2, requests, head), F32),
+            pltpu.VMEM(w.shape, BF16),
+        ],
         scratch_shapes=[
             pltpu.VMEM((lenders, head), jnp.int32),
             pltpu.SMEM((lenders, head), jnp.int32),
             pltpu.SemaphoreType.DMA,
-        ],
-        compiler_params=pltpu.CompilerParams(vmem_limit_bytes=16 * 1024 * 1024),
+            pltpu.SemaphoreType.DMA,
+        ],
+        input_output_aliases={7: 3},
+        compiler_params=pltpu.CompilerParams(vmem_limit_bytes=8 * 1024 * 1024),
         name="attend",
-    )(q, keys, values)
+    )(q, keys, values, own, new_keys, new_values, in_hbm(w), w_part)
 
 
 def combine_kernel(
-    drafts, place_ref, got_ref, fresh_ref, stat_ref, w_ref,
-    send_ref, att_ref, arrived_ref, own_ref, rows_ref,
+    drafts, place_ref, got_ref, fresh_ref, stat_ref, w_hbm, w_in,
+    send_ref, att_ref, w_ref, arrived_ref, own_ref, rows_ref, w_sem,
 ):
+    first = weight_copy(w_hbm, w_ref, 0, EARLY, w_sem)
+
+    @pl.when(lax.axis_index("tp") & 1 == 1)
+    def _():
+        first.start()
+
     requests, rows, head = fresh_ref.shape
     lenders = got_ref.shape[0]
     entries = place_ref.shape[0]
@@ -234,7 +257,7 @@
     group = rows // drafts
 
     for i in range(lenders):
-        arrived_ref[i * each : (i + 1) * each, :] = got_ref[i, each * rows :, :].astype(F32)[:each]
+        arrived_ref[i * each : (i + 1) * each, :] = got_ref[i, each * rows :, :].astype(F32)
     for e in range(entries):
         own_ref[e : e + 1, :] = arrived_ref[pl.ds(place_ref[e], 1), :]
     x = own_ref[...]
@@ -289,6 +312,11 @@
         [rows_ref[pl.ds(g, drafts * requests, stride=group), :] for g in range(group)], axis=1
     ).astype(BF16)
     att_ref[...] = att
+
+    @pl.when(lax.axis_index("tp") & 1 == 1)
+    def _():
+        first.wait()
+
     tile = send_ref.shape[2]
     place_tp = lax.axis_index("tp")
     core = place_tp & 1
@@ -299,7 +327,7 @@
         send_ref[i] = jnp.dot(att, w_ref[:, here], preferred_element_type=F32).astype(BF16)
 
 
-def combine(place, got, fresh, stat, w, drafts, tp):
+def combine(place, got, fresh, stat, w, w_part, drafts, tp):
     requests, rows, head = fresh.shape
     deep, wide = w.shape
     tile = wide // tp
@@ -307,20 +335,23 @@
     vmem, smem = pl.BlockSpec(memory_space=pltpu.VMEM), pl.BlockSpec(memory_space=pltpu.SMEM)
     return pl.pallas_call(
         functools.partial(combine_kernel, drafts),
-        in_specs=[smem, vmem, vmem, vmem, vmem],
-        out_specs=[vmem, vmem],
+        in_specs=[smem, vmem, vmem, vmem, pl.BlockSpec(memory_space=pltpu.HBM), vmem],
+        out_specs=[vmem] * 3,
         out_shape=[
             jax.ShapeDtypeStruct((tp // 2, tall, tile), BF16),
             jax.ShapeDtypeStruct((tall, deep), BF16),
+            pltpu.VMEM(w.shape, BF16),
         ],
         scratch_shapes=[
             pltpu.VMEM((place.shape[0], head), F32),
             pltpu.VMEM((place.shape[0], head), F32),
             pltpu.VMEM((requests * rows, head), F32),
-        ],
-        compiler_params=pltpu.CompilerParams(vmem_limit_bytes=16 * 1024 * 1024),
+            pltpu.SemaphoreType.DMA,
+        ],
+        input_output_aliases={5: 2},
+        compiler_params=pltpu.CompilerParams(vmem_limit_bytes=8 * 1024 * 1024),
         name="combine",
-    )(place, got, fresh, stat, w)
+    )(place, got, fresh, stat, in_hbm(w), w_part)
 
 
 def keep_kernel(att_ref, w_ref, keep_ref):
@@ -344,7 +375,7 @@
         in_specs=[vmem, vmem],
         out_specs=vmem,
         out_shape=jax.ShapeDtypeStruct((tp // 2, tall, tile), F32),
-        compiler_params=pltpu.CompilerParams(vmem_limit_bytes=16 * 1024 * 1024),
+        compiler_params=pltpu.CompilerParams(vmem_limit_bytes=8 * 1024 * 1024),
         cost_estimate=pl.CostEstimate(
             flops=tall * deep * wide, bytes_accessed=deep * wide, transcendentals=0
         ),
@@ -358,19 +389,24 @@
     drafts, requests, heads, head = queries.shape
     pool, _, block, _ = key_pool.shape
     tp = lax.axis_size("tp")
-    rows = drafts * heads
-    payload, place, fresh, stat = prepare(
-        block_table, context_len, queries, new_keys.reshape(-1, head), new_values.reshape(-1, head), block
-    )
+    payload, place, own, weight = prepare(block_table, context_len, queries, out_weight, block)
     asked = lax.all_to_all(payload, "inst", 0, 0, tiled=True)
-    answer = attend(
-        asked, key_pool.reshape(pool, block, head), value_pool.reshape(pool, block, head), rows
+    answer, fresh, stat, weight = attend(
+        asked,
+        key_pool.reshape(pool, block, head),
+        value_pool.reshape(pool, block, head),
+        own,
+        new_keys.reshape(-1, head),
+        new_values.reshape(-1, head),
+        out_weight,
+        weight,
+        drafts,
     )
     got = lax.all_to_all(answer, "inst", 0, 0, tiled=True)
 
-    send, att = combine(place, got, fresh, stat, out_weight, drafts, tp)
+    send, att, weight = combine(place, got, fresh, stat, out_weight, weight, drafts, tp)
     other = lax.ppermute(send, "tp", [(i, i ^ 1) for i in range(tp)])
-    keep = keep_half(att, out_weight, tp)
+    keep = keep_half(att, weight, tp)
     ring = tp // 2
     parts = [
         lax.ppermute(

time: 69.9 us -> 65.7 us (0.940)
  blocking collectives: 44.1 us -> 36.2 us
  Pallas kernels: 11.8 us -> 14.9 us
    all_to_all x1, blocking collectives: 25.2 us -> 20.9 us  [on_device(): asked = lax.all_to_all(payload, 'inst', 0, 0, tiled=True)]
    all_to_all x1, blocking collectives: 18.9 us -> 15.2 us  [on_device(): got = lax.all_to_all(answer, 'inst', 0, 0, tiled=True)]
    pallas_call x1, Pallas kernels: 2.81 us -> 6.1 us  [combine(): pl.pallas_call(functools.partial(combine_kernel, drafts), in_specs=[smem,...]
where the time goes in v5:
time: 65.7 us; the launch traced here: 65.5 us
  blocking collectives  36.2 us (55%)
  Pallas kernels  14.9 us (23%)
  starting transfers between devices  8.54 us (13%)
  waiting for transfers between devices  5.04 us (8%)
  other arithmetic  0.83 us (1%)
    all_to_all x1, blocking collectives, on_device(): asked = lax.all_to_all(payload, 'inst', 0, 0, tiled=True)  20.9 us
    all_to_all x1, blocking collectives, on_device(): got = lax.all_to_all(answer, 'inst', 0, 0, tiled=True)  15.2 us
    pallas_call x1, Pallas kernels, combine(): pl.pallas_call(functools.partial(combine_kernel, drafts), in_specs=[smem,...  6.1 us
    ppermute x3, waiting for transfers between devices, on_device(): lax.ppermute((keep[n] + other[n].astype(F32)).astype(BF16), 'tp', [(i, (i...  5.04 us
    pallas_call x1, Pallas kernels, attend(): pl.pallas_call(functools.partial(attend_kernel, drafts, 8, 4), in_specs=[...  4.85 us
    ppermute x3, starting transfers between devices, on_device(): lax.ppermute((keep[n] + other[n].astype(F32)).astype(BF16), 'tp', [(i, (i...  4.46 us
    ppermute x1, starting transfers between devices, on_device(): other = lax.ppermute(send, 'tp', [(i, i ^ 1) for i in range(tp)])  4.08 us
    pallas_call x1, Pallas kernels, prepare(): pl.pallas_call(functools.partial(prepare_kernel, shifts), in_specs=[pl.Bl...  2.35 us
  transfers between devices with their start and end apart: 4, of which 2 were waited for; matrix products, arithmetic and copies ran while one was open for 0% of the time, Pallas kernels for 2%

profile of v5, /device:TPU:1, one launch (start us, length us, event | category | flops | bytes accessed | tf_op | source)
XLA Modules:
  0.0 65.5 jit_solution(8256597767478857909)
XLA Ops:
  0.0 0.0 copy-start.1
  0.0 0.0 copy-start
  0.0 0.0 copy-start.3
  0.0 0.0 copy-start.2
  0.0 2.4 %prepare.1 = (bf16[16,264,128]{2,1,0:T(8,128)(2,1)S(1)}, s32[128]{0:T(128)S(1)}, bf16[16,32,128]{2,1,0:T(8,128)(2,1)S(1)}, bf16[1024,8192]{1,0:T(8,128)(2,1)S(1)}) custom-call(s32[128]{0:T(128)} %table_hbm.1, s32[16]{0:T(128)} %length_hbm.1, bf16[4,16,8,128]{3,2,1,0:T(8,128)(2,1)} %queries_hbm.1, bf16[1024,8192]{1,0:T(8,128)(2,1)} %w_hbm.5), custom_call_target="tpu_custom_call" | custom-call | flops 20000000000 | bytes 67108864 | tf_op jit(solution)/shard_map/prepare/pallas_call | solution.py:113
  2.4 20.9 %all_to_all.10.q_ref = bf16[16,264,128]{2,1,0:T(8,128)(2,1)S(1)} all-to-all(bf16[16,264,128]{2,1,0:T(8,128)(2,1)S(1)} %get-tuple-element.17), channel_id=1, replica_groups=mesh['inst'=16,'tp'=8] {'inst'}, dimensions={0} | all-to-all | bytes 2162688 | tf_op jit(solution)/shard_map/all_to_all | solution.py:393
  23.3 0.0 copy-done.1
  23.3 0.0 copy-done
  23.3 0.0 copy-done.3
  23.3 0.0 copy-done.2
  23.3 4.9 %attend.1 = (bf16[16,264,128]{2,1,0:T(8,128)(2,1)S(1)}, f32[16,32,128]{2,1,0:T(8,128)S(1)}, f32[2,16,128]{2,1,0:T(8,128)S(1)}, bf16[1024,8192]{1,0:T(8,128)(2,1)S(1)}) custom-call(bf16[16,264,128]{2,1,0:T(8,128)(2,1)S(1)} %all_to_all.10.q_ref, bf16[128,256,128]{2,1,0:T(8,128)(2,1)S(1)} %bitcast.21, ...), custom_call_target="tpu_custom_call", output_to_operand_aliasing={{3}: (7, {})} | custom-call | tf_op jit(solution)/shard_map/attend/pallas_call | solution.py:219
  28.2 15.2 %all_to_all.11.got_ref = bf16[16,264,128]{2,1,0:T(8,128)(2,1)S(1)} all-to-all(bf16[16,264,128]{2,1,0:T(8,128)(2,1)S(1)} %get-tuple-element.20), channel_id=1, replica_groups=mesh['inst'=16,'tp'=8] {'inst'}, dimensions={0} | all-to-all | bytes 2162688 | tf_op jit(solution)/shard_map/all_to_all | solution.py:405
  43.4 6.1 %combine.1 = (bf16[4,64,1024]{2,1,0:T(8,128)(2,1)S(1)}, bf16[64,1024]{1,0:T(8,128)(2,1)S(1)}, bf16[1024,8192]{1,0:T(8,128)(2,1)S(1)}) custom-call(s32[128]{0:T(128)S(1)} %get-tuple-element.16.place_ref, bf16[16,264,128]{2,1,0:T(8,128)(2,1)S(1)} %all_to_all.11.got_ref, ...), custom_call_target="tpu_custom_call", output_to_operand_aliasing={{2}: (5, {})} | custom-call | tf_op jit(solution)/shard_map/combine/pallas_call | solution.py:336
  49.5 4.1 %collective-permute-start = (bf16[4,64,1024]{2,1,0:T(8,128)(2,1)S(1)}, bf16[4,64,1024]{2,1,0:T(8,128)(2,1)S(1)}, u32[]{:S(2)}, u32[]{:S(2)}) collective-permute-start(bf16[4,64,1024]{2,1,0:T(8,128)(2,1)S(1)} %get-tuple-element.26), channel_id=1, source_target_pairs={{0,1},{1,0},{2,3},{3,2},{4,5},{5,4},{6,7},{7,6},{8,9},{9,8},{10,11... | collective-permute-start | bytes 1572872 | tf_op jit(solution)/shard_map/ppermute | solution.py:408
  53.6 1.6 %keep_half.1 = f32[4,64,1024]{2,1,0:T(8,128)S(1)} custom-call(bf16[64,1024]{1,0:T(8,128)(2,1)S(1)} %get-tuple-element.24.att_ref, bf16[1024,8192]{1,0:T(8,128)(2,1)S(1)} %get-tuple-element.25.w_ref), custom_call_target="tpu_custom_call" | custom-call | flops 536870912 | bytes 8388608 | tf_op jit(solution)/shard_map/keep_half/pallas_call | solution.py:373
  55.2 0.0 collective-permute-done
  55.2 0.1 fusion.8
  55.3 3.0 %collective-permute-start.1 = (bf16[64,1024]{1,0:T(8,128)(2,1)S(1)}, bf16[64,1024]{1,0:T(8,128)(2,1)S(1)}, u32[]{:S(2)}, u32[]{:S(2)}) collective-permute-start(bf16[64,1024]{1,0:T(8,128)(2,1)S(1)} %get-tuple-element.27), channel_id=1, source_target_pairs={{0,4},{1,5},{2,6},{3,7},{4,0},{5,1},{6,2},{7,3},{8,12},{9,13},{10,... | collective-permute-start | bytes 393224 | tf_op jit(solution)/shard_map/ppermute | solution.py:412
  58.3 0.8 %collective-permute-start.3 = (bf16[64,1024]{1,0:T(8,128)(2,1)S(1)}, bf16[64,1024]{1,0:T(8,128)(2,1)S(1)}, u32[]{:S(2)}, u32[]{:S(2)}) collective-permute-start(bf16[64,1024]{1,0:T(8,128)(2,1)S(1)} %get-tuple-element.28), channel_id=1, source_target_pairs={{0,6},{1,7},{2,0},{3,1},{4,2},{5,3},{6,4},{7,5},{8,14},{9,15},{10,... | collective-permute-start | bytes 393224 | tf_op jit(solution)/shard_map/ppermute | solution.py:412
  59.1 0.7 %collective-permute-start.2 = (bf16[64,1024]{1,0:T(8,128)(2,1)S(1)}, bf16[64,1024]{1,0:T(8,128)(2,1)S(1)}, u32[]{:S(2)}, u32[]{:S(2)}) collective-permute-start(bf16[64,1024]{1,0:T(8,128)(2,1)S(1)} %get-tuple-element.29), channel_id=1, source_target_pairs={{0,2},{1,3},{2,4},{3,5},{4,6},{5,7},{6,0},{7,1},{8,10},{9,11},{10,... | collective-permute-start | bytes 393224 | tf_op jit(solution)/shard_map/ppermute | solution.py:412
  59.8 1.9 %collective-permute-done.1 = bf16[64,1024]{1,0:T(8,128)(2,1)S(1)} collective-permute-done((bf16[64,1024]{1,0:T(8,128)(2,1)S(1)}, bf16[64,1024]{1,0:T(8,128)(2,1)S(1)}, u32[]{:S(2)}, u32[]{:S(2)}) %collective-permute-start.1) | collective-permute-done | bytes 131104 | tf_op jit(solution)/shard_map/ppermute | solution.py:412
  61.6 3.2 %collective-permute-done.3 = bf16[64,1024]{1,0:T(8,128)(2,1)S(1)} collective-permute-done((bf16[64,1024]{1,0:T(8,128)(2,1)S(1)}, bf16[64,1024]{1,0:T(8,128)(2,1)S(1)}, u32[]{:S(2)}, u32[]{:S(2)}) %collective-permute-start.3) | collective-permute-done | bytes 131104 | tf_op jit(solution)/shard_map/ppermute | solution.py:412
  64.8 0.0 collective-permute-done.2
  64.8 0.7 %fusion.7 = bf16[64,1024]{1,0:T(8,128)(2,1)} fusion(f32[4,64,1024]{2,1,0:T(8,128)S(1)} %keep_half.1, bf16[64,1024]{1,0:T(8,128)(2,1)S(1)} %collective-permute-done.3, bf16[64,1024]{1,0:T(8,128)(2,1)S(1)} %collective-permute-done.2, bf16[64,1024]{1,0:T(8,128)(2,1)S(1)} %collective-permute-done.1, bf16[4,64,1024]{2,1,0:T(8,128)(2,1)S(1)} %collective-permute-done), kind=kLoop, calls=%fused_computation.11 | loop fusion | flops 589824 | bytes 917504 | tf_op jit(solution)/shard_map/convert_element_type | solution.py:422
Async XLA Ops:
  0.0 23.3 %copy-start.1 = (bf16[128,1,256,128]{3,2,1,0:T(8,128)(2,1)S(1)}, bf16[128,1,256,128]{3,2,1,0:T(8,128)(2,1)}, u32[]{:S(2)}) copy-start(bf16[128,1,256,128]{3,2,1,0:T(8,128)(2,1)} %param.12) | copy-start | bytes 25165828
  0.0 23.3 %copy-start = (bf16[128,1,256,128]{3,2,1,0:T(8,128)(2,1)S(1)}, bf16[128,1,256,128]{3,2,1,0:T(8,128)(2,1)}, u32[]{:S(2)}) copy-start(bf16[128,1,256,128]{3,2,1,0:T(8,128)(2,1)} %param.11) | copy-start | bytes 25165828
  0.0 23.3 %copy-start.3 = (bf16[4,16,1,128]{3,1,2,0:T(8,128)(2,1)S(1)}, bf16[4,16,1,128]{3,1,2,0:T(8,128)(2,1)}, u32[]{:S(2)}) copy-start(bf16[4,16,1,128]{3,1,2,0:T(8,128)(2,1)} %param.10) | copy-start | bytes 49156
  0.0 23.3 %copy-start.2 = (bf16[4,16,1,128]{3,1,2,0:T(8,128)(2,1)S(1)}, bf16[4,16,1,128]{3,1,2,0:T(8,128)(2,1)}, u32[]{:S(2)}) copy-start(bf16[4,16,1,128]{3,1,2,0:T(8,128)(2,1)} %param.9) | copy-start | bytes 49156
  49.5 5.7 %collective-permute-start = (bf16[4,64,1024]{2,1,0:T(8,128)(2,1)S(1)}, bf16[4,64,1024]{2,1,0:T(8,128)(2,1)S(1)}, u32[]{:S(2)}, u32[]{:S(2)}) collective-permute-start(bf16[4,64,1024]{2,1,0:T(8,128)(2,1)S(1)} %get-tuple-element.26), channel_id=1, source_target_pairs={{0,1},{1,0},{2,3},{3,2},{4,5},{5,4},{6,7},{7,6},{8,9},{9,8},{10,11... | collective-permute-start | bytes 1572872 | tf_op jit(solution)/shard_map/ppermute | solution.py:408
  55.3 6.3 %collective-permute-start.1 = (bf16[64,1024]{1,0:T(8,128)(2,1)S(1)}, bf16[64,1024]{1,0:T(8,128)(2,1)S(1)}, u32[]{:S(2)}, u32[]{:S(2)}) collective-permute-start(bf16[64,1024]{1,0:T(8,128)(2,1)S(1)} %get-tuple-element.27), channel_id=1, source_target_pairs={{0,4},{1,5},{2,6},{3,7},{4,0},{5,1},{6,2},{7,3},{8,12},{9,13},{10,... | collective-permute-start | bytes 393224 | tf_op jit(solution)/shard_map/ppermute | solution.py:412
  58.3 6.5 %collective-permute-start.3 = (bf16[64,1024]{1,0:T(8,128)(2,1)S(1)}, bf16[64,1024]{1,0:T(8,128)(2,1)S(1)}, u32[]{:S(2)}, u32[]{:S(2)}) collective-permute-start(bf16[64,1024]{1,0:T(8,128)(2,1)S(1)} %get-tuple-element.28), channel_id=1, source_target_pairs={{0,6},{1,7},{2,0},{3,1},{4,2},{5,3},{6,4},{7,5},{8,14},{9,15},{10,... | collective-permute-start | bytes 393224 | tf_op jit(solution)/shard_map/ppermute | solution.py:412
  59.1 5.7 %collective-permute-start.2 = (bf16[64,1024]{1,0:T(8,128)(2,1)S(1)}, bf16[64,1024]{1,0:T(8,128)(2,1)S(1)}, u32[]{:S(2)}, u32[]{:S(2)}) collective-permute-start(bf16[64,1024]{1,0:T(8,128)(2,1)S(1)} %get-tuple-element.29), channel_id=1, source_target_pairs={{0,2},{1,3},{2,4},{3,5},{4,6},{5,7},{6,0},{7,1},{8,10},{9,11},{10,... | collective-permute-start | bytes 393224 | tf_op jit(solution)/shard_map/ppermute | solution.py:412

commit v6 on v5

--- a/solution.py
+++ b/solution.py
@@ -11,6 +11,8 @@
 NEG = -1e30
 F32 = jnp.float32
 BF16 = jnp.bfloat16
+FAR = 2
+REST = (1, 3, 0)
 META = 8
 EARLY = 512
 
@@ -34,12 +36,15 @@
     drafted = lax.shift_right_logical(row & (rows - 1), group_bits)
     valid = own & (lax.shift_right_logical(key, request_bits) <= drafted)
     s = jnp.where(valid, s * head ** (-0.5), NEG)
+    yield
     peak = jnp.max(s, axis=0, keepdims=True)
     weight = jnp.exp(s - peak)
     total = jnp.sum(weight, axis=0, keepdims=True)
+    yield
     out_ref[...] = lax.dot_general(
         weight.astype(BF16), v_ref[...], (((0,), (0,)), ((), ())), preferred_element_type=F32
     ).reshape(requests, rows, head)
+    yield
     for r in range(requests):
         start = r * rows // head * head
         for n, x in enumerate((peak, total)):
@@ -47,6 +52,7 @@
             if r * rows > start:
                 piece = pltpu.roll(piece, head - (r * rows - start), 1)
             stat_ref[n, r : r + 1, :] = piece
+    yield
 
 
 def weight_copy(w_hbm, w_ref, start, stop, sem):
@@ -56,8 +62,8 @@
 
 def prepare_kernel(
     shifts, table_hbm, length_hbm, queries_hbm, w_hbm,
-    out_ref, place_ref, q_ref, w_ref,
-    table_ref, length_ref, queries_ref, meta_ref, count_ref, sems, w_sem,
+    out_ref, place_hbm, q_ref, w_ref,
+    table_ref, length_ref, queries_ref, place_ref, meta_ref, count_ref, sems, w_sem,
 ):
     drafts, requests, group, head = queries_ref.shape
     lenders = out_ref.shape[0]
@@ -84,6 +90,8 @@
         limit = jnp.clip(length_ref[e // blocks] - (e % blocks << block_bits), 0, 1 << block_bits)
         inner = slot & ((1 << pool_bits) - 1)
         meta_ref[lender, pl.ds(j, 1), :] = jnp.where(first_half, inner, limit).astype(F32)
+    places = pltpu.make_async_copy(place_ref, place_hbm, sems.at[3])
+    places.start()
     copies[2].wait()
     for r in range(requests):
         q = jnp.concatenate([queries_ref[d, r] for d in range(drafts)], axis=0)
@@ -94,6 +102,7 @@
             start = pl.multiple_of((place & (each - 1)) * rows, rows)
             out_ref[lender, pl.ds(start, rows), :] = q
     out_ref[:, each * rows :, :] = meta_ref[...].astype(BF16)
+    places.wait()
 
     @pl.when(lax.axis_index("tp") & 1 == 0)
     def _():
@@ -109,14 +118,14 @@
     lenders = lax.axis_size("inst")
     each = entries // lenders
     shifts = tuple(n.bit_length() - 1 for n in (entries, each, block))
-    vmem, smem = pl.BlockSpec(memory_space=pltpu.VMEM), pl.BlockSpec(memory_space=pltpu.SMEM)
+    vmem = pl.BlockSpec(memory_space=pltpu.VMEM)
     return pl.pallas_call(
         functools.partial(prepare_kernel, shifts),
         in_specs=[pl.BlockSpec(memory_space=pltpu.HBM)] * 4,
-        out_specs=[vmem, smem, vmem, vmem],
+        out_specs=[vmem, pl.BlockSpec(memory_space=pltpu.HBM), vmem, vmem],
         out_shape=[
             jax.ShapeDtypeStruct((lenders, each * rows + META, head), BF16),
-            jax.ShapeDtypeStruct((entries,), jnp.int32),
+            pltpu.HBM((entries,), jnp.int32),
             jax.ShapeDtypeStruct((requests, rows, head), BF16),
             pltpu.VMEM(w.shape, BF16),
         ],
@@ -124,9 +133,10 @@
             pltpu.SMEM(table.shape, jnp.int32),
             pltpu.SMEM(lengths.shape, jnp.int32),
             pltpu.VMEM(queries.shape, BF16),
+            pltpu.SMEM((entries,), jnp.int32),
             pltpu.VMEM((lenders, META, head), F32),
             pltpu.SMEM((lenders,), jnp.int32),
-            pltpu.SemaphoreType.DMA((3,)),
+            pltpu.SemaphoreType.DMA((4,)),
             pltpu.SemaphoreType.DMA,
         ],
         compiler_params=pltpu.CompilerParams(vmem_limit_bytes=8 * 1024 * 1024),
@@ -169,12 +179,13 @@
     def here(i):
         return i // each, pl.ds(i % each * rows, rows), slice(None)
 
+    draft = draft_block(drafts, own_ref[...], new_k_ref, new_v_ref, fresh_ref, stat_ref)
     scores, soft, outs = {}, {}, {}
     peaks = jnp.zeros((rows, head), F32)
     totals = jnp.ones((rows, head), F32)
     for i in range(-ahead, entries + 2 * behind):
-        if i == 32:
-            draft_block(drafts, own_ref[...], new_k_ref, new_v_ref, fresh_ref, stat_ref)
+        if i in (16, 28, 40, 52):
+            next(draft)
         if i + ahead < entries:
             n = i + ahead
             scores[n] = lax.dot_general(
@@ -238,9 +249,21 @@
     )(q, keys, values, own, new_keys, new_values, in_hbm(w), w_part)
 
 
+def project_to(steps, other, att_ref, w_ref, out_ref):
+    place = lax.axis_index("tp")
+    core = 1 - (place & 1) if other else place & 1
+    tile = out_ref.shape[2]
+    ring = w_ref.shape[1] // tile // 2
+    for i, step in enumerate(steps):
+        to = ((place >> 1) + step) & (ring - 1)
+        here = pl.ds(pl.multiple_of((2 * to + core) * tile, tile), tile)
+        out = jnp.dot(att_ref[...], w_ref[:, here], preferred_element_type=F32)
+        out_ref[i] = out.astype(out_ref.dtype)
+
+
 def combine_kernel(
     drafts, place_ref, got_ref, fresh_ref, stat_ref, w_hbm, w_in,
-    send_ref, att_ref, w_ref, arrived_ref, own_ref, rows_ref, w_sem,
+    far_ref, send_ref, att_ref, w_ref, arrived_ref, own_ref, rows_ref, w_sem,
 ):
     first = weight_copy(w_hbm, w_ref, 0, EARLY, w_sem)
 
@@ -317,14 +340,8 @@
     def _():
         first.wait()
 
-    tile = send_ref.shape[2]
-    place_tp = lax.axis_index("tp")
-    core = place_tp & 1
-    ring = send_ref.shape[0]
-    for i in range(send_ref.shape[0]):
-        to = ((place_tp >> 1) + i) & (ring - 1)
-        here = pl.ds(pl.multiple_of((2 * to + 1 - core) * tile, tile), tile)
-        send_ref[i] = jnp.dot(att, w_ref[:, here], preferred_element_type=F32).astype(BF16)
+    project_to((FAR,), True, att_ref, w_ref, far_ref)
+    project_to(REST, True, att_ref, w_ref, send_ref)
 
 
 def combine(place, got, fresh, stat, w, w_part, drafts, tp):
@@ -336,9 +353,10 @@
     return pl.pallas_call(
         functools.partial(combine_kernel, drafts),
         in_specs=[smem, vmem, vmem, vmem, pl.BlockSpec(memory_space=pltpu.HBM), vmem],
-        out_specs=[vmem] * 3,
+        out_specs=[vmem] * 4,
         out_shape=[
-            jax.ShapeDtypeStruct((tp // 2, tall, tile), BF16),
+            jax.ShapeDtypeStruct((1, tall, tile), BF16),
+            jax.ShapeDtypeStruct((len(REST), tall, tile), BF16),
             jax.ShapeDtypeStruct((tall, deep), BF16),
             pltpu.VMEM(w.shape, BF16),
         ],
@@ -348,38 +366,29 @@
             pltpu.VMEM((requests * rows, head), F32),
             pltpu.SemaphoreType.DMA,
         ],
-        input_output_aliases={5: 2},
+        input_output_aliases={5: 3},
         compiler_params=pltpu.CompilerParams(vmem_limit_bytes=8 * 1024 * 1024),
         name="combine",
     )(place, got, fresh, stat, in_hbm(w), w_part)
 
 
-def keep_kernel(att_ref, w_ref, keep_ref):
-    tile = keep_ref.shape[2]
-    place_tp = lax.axis_index("tp")
-    core = place_tp & 1
-    ring = keep_ref.shape[0]
-    for i in range(ring):
-        to = ((place_tp >> 1) + i) & (ring - 1)
-        here = pl.ds(pl.multiple_of((2 * to + core) * tile, tile), tile)
-        keep_ref[i] = jnp.dot(att_ref[...], w_ref[:, here], preferred_element_type=F32)
-
-
-def keep_half(att, w, tp):
+def keep(steps, att, w, tp):
     deep, wide = w.shape
     tile = wide // tp
     tall = att.shape[0]
-    vmem, smem = pl.BlockSpec(memory_space=pltpu.VMEM), pl.BlockSpec(memory_space=pltpu.SMEM)
+    vmem = pl.BlockSpec(memory_space=pltpu.VMEM)
     return pl.pallas_call(
-        keep_kernel,
+        functools.partial(project_to, steps, False),
         in_specs=[vmem, vmem],
         out_specs=vmem,
-        out_shape=jax.ShapeDtypeStruct((tp // 2, tall, tile), F32),
+        out_shape=jax.ShapeDtypeStruct((len(steps), tall, tile), F32),
         compiler_params=pltpu.CompilerParams(vmem_limit_bytes=8 * 1024 * 1024),
         cost_estimate=pl.CostEstimate(
-            flops=tall * deep * wide, bytes_accessed=deep * wide, transcendentals=0
+            flops=2 * tall * deep * tile * len(steps),
+            bytes_accessed=2 * deep * tile * len(steps),
+            transcendentals=0,
         ),
-        name="keep_half",
+        name="keep",
     )(att, w)
 
 
@@ -404,19 +413,21 @@
     )
     got = lax.all_to_all(answer, "inst", 0, 0, tiled=True)
 
-    send, att, weight = combine(place, got, fresh, stat, out_weight, weight, drafts, tp)
-    other = lax.ppermute(send, "tp", [(i, i ^ 1) for i in range(tp)])
-    keep = keep_half(att, weight, tp)
-    ring = tp // 2
-    parts = [
-        lax.ppermute(
-            (keep[n] + other[n].astype(F32)).astype(BF16),
-            "tp",
-            [(i, (i + 2 * n) % tp) for i in range(tp)],
-        )
-        for n in (2, 1, 3)
-    ]
-    total = keep[0] + other[0].astype(F32)
+    far, send, att, weight = combine(place, got, fresh, stat, out_weight, weight, drafts, tp)
+    swap = [(i, i ^ 1) for i in range(tp)]
+
+    def along(pair, step):
+        return lax.ppermute(pair.astype(BF16), "tp", [(i, (i + 2 * step) % tp) for i in range(tp)])
+
+    other_far = lax.ppermute(far, "tp", swap)
+    other = lax.ppermute(send, "tp", swap)
+    pair = keep((FAR,), att, weight, tp)[0] + other_far[0].astype(F32)
+    parts = [along(pair, FAR)]
+    att, _ = lax.optimization_barrier((att, pair))
+    kept = keep(REST, att, weight, tp)
+    pairs = [kept[n] + other[n].astype(F32) for n in range(len(REST))]
+    parts += [along(pairs[n], REST[n]) for n in range(2)]
+    total = pairs[2]
     for part in parts:
         total = total + part.astype(F32)
     result = total.astype(BF16)

time: 65.7 us -> 65.1 us (level)
  waiting for transfers between devices: 5.04 us -> 3.34 us
  starting transfers between devices: 8.54 us -> 10.1 us
    ppermute x4 -> x5, waiting for transfers between devices: 5.04 us -> 3.34 us  [the longest x3 2.93 us: along(): lax.ppermute(pair.astype(BF16), 'tp', [(i, (i + 2 * step) % tp) for i in...]
    ppermute x4 -> x5, starting transfers between devices: 8.54 us -> 10.1 us  [the longest x3 5.74 us: along(): lax.ppermute(pair.astype(BF16), 'tp', [(i, (i + 2 * step) % tp) for i in...]
    pallas_call x1 -> x2, Pallas kernels: 1.57 us -> 1.68 us  [keep(): pl.pallas_call(functools.partial(project_to, steps, False), in_specs=[vme...]
  transfers between devices with their start and end apart: 4 -> 5, of which waited for: 2 -> 2; matrix products, arithmetic and copies ran while one was open for 0% -> 0% of each run, Pallas kernels for 2% -> 3%
where the time goes in v6:
time: 65.1 us; the launch traced here: 64.8 us
  blocking collectives  36 us (55%)
  Pallas kernels  14.5 us (22%)
  starting transfers between devices  10.1 us (16%)
  waiting for transfers between devices  3.34 us (5%)
  other arithmetic  0.82 us (1%)
    all_to_all x1, blocking collectives, on_device(): asked = lax.all_to_all(payload, 'inst', 0, 0, tiled=True)  20.8 us
    all_to_all x1, blocking collectives, on_device(): got = lax.all_to_all(answer, 'inst', 0, 0, tiled=True)  15.1 us
    pallas_call x1, Pallas kernels, combine(): pl.pallas_call(functools.partial(combine_kernel, drafts), in_specs=[smem,...  6.12 us
    ppermute x3, starting transfers between devices, along(): lax.ppermute(pair.astype(BF16), 'tp', [(i, (i + 2 * step) % tp) for i in...  5.74 us
    pallas_call x1, Pallas kernels, attend(): pl.pallas_call(functools.partial(attend_kernel, drafts, 8, 4), in_specs=[...  4.67 us
    ppermute x1, starting transfers between devices, on_device(): other_far = lax.ppermute(far, 'tp', swap)  4.29 us
    ppermute x3, waiting for transfers between devices, along(): lax.ppermute(pair.astype(BF16), 'tp', [(i, (i + 2 * step) % tp) for i in...  2.93 us
    pallas_call x1, Pallas kernels, prepare(): pl.pallas_call(functools.partial(prepare_kernel, shifts), in_specs=[pl.Bl...  1.98 us
  transfers between devices with their start and end apart: 5, of which 2 were waited for; matrix products, arithmetic and copies ran while one was open for 0% of the time, Pallas kernels for 3%

profile of v6, /device:TPU:1, one launch (start us, length us, event | category | flops | bytes accessed | tf_op | source)
XLA Modules:
  0.0 64.8 jit_solution(6365297612253406465)
XLA Ops:
  0.0 0.0 copy-start.1
  0.0 0.0 copy-start
  0.0 0.0 copy-start.3
  0.0 0.0 copy-start.2
  0.0 2.0 %prepare.1 = (bf16[16,264,128]{2,1,0:T(8,128)(2,1)S(1)}, s32[128]{0:T(128)}, bf16[16,32,128]{2,1,0:T(8,128)(2,1)S(1)}, bf16[1024,8192]{1,0:T(8,128)(2,1)S(1)}) custom-call(s32[128]{0:T(128)} %table_hbm.1, s32[16]{0:T(128)} %length_hbm.1, bf16[4,16,8,128]{3,2,1,0:T(8,128)(2,1)} %queries_hbm.1, bf16[1024,8192]{1,0:T(8,128)(2,1)} %w_hbm.5), custom_call_target="tpu_custom_call" | custom-call | flops 20000000000 | bytes 67108864 | tf_op jit(solution)/shard_map/prepare/pallas_call | solution.py:122
  2.0 20.8 %all_to_all.10.q_ref = bf16[16,264,128]{2,1,0:T(8,128)(2,1)S(1)} all-to-all(bf16[16,264,128]{2,1,0:T(8,128)(2,1)S(1)} %get-tuple-element.19), channel_id=1, replica_groups=mesh['inst'=16,'tp'=8] {'inst'}, dimensions={0} | all-to-all | bytes 2162688 | tf_op jit(solution)/shard_map/all_to_all | solution.py:402
  22.8 0.0 copy-done.1
  22.8 0.0 copy-done
  22.8 0.0 copy-done.3
  22.8 0.0 copy-done.2
  22.9 0.0 copy-start.4
  22.9 4.7 %attend.1 = (bf16[16,264,128]{2,1,0:T(8,128)(2,1)S(1)}, f32[16,32,128]{2,1,0:T(8,128)S(1)}, f32[2,16,128]{2,1,0:T(8,128)S(1)}, bf16[1024,8192]{1,0:T(8,128)(2,1)S(1)}) custom-call(bf16[16,264,128]{2,1,0:T(8,128)(2,1)S(1)} %all_to_all.10.q_ref, bf16[128,256,128]{2,1,0:T(8,128)(2,1)S(1)} %bitcast.21, ...), custom_call_target="tpu_custom_call", output_to_operand_aliasing={{3}: (7, {})} | custom-call | tf_op jit(solution)/shard_map/attend/pallas_call | solution.py:230
  27.5 15.1 %all_to_all.11.got_ref = bf16[16,264,128]{2,1,0:T(8,128)(2,1)S(1)} all-to-all(bf16[16,264,128]{2,1,0:T(8,128)(2,1)S(1)} %get-tuple-element.22), channel_id=1, replica_groups=mesh['inst'=16,'tp'=8] {'inst'}, dimensions={0} | all-to-all | bytes 2162688 | tf_op jit(solution)/shard_map/all_to_all | solution.py:414
  42.7 0.0 copy-done.4
  42.7 6.1 %combine.1 = (bf16[1,64,1024]{2,1,0:T(8,128)(2,1)S(1)}, bf16[3,64,1024]{2,1,0:T(8,128)(2,1)S(1)}, bf16[64,1024]{1,0:T(8,128)(2,1)S(1)}, bf16[1024,8192]{1,0:T(8,128)(2,1)S(1)}) custom-call(s32[128]{0:T(128)S(1)} %copy-done.4, bf16[16,264,128]{2,1,0:T(8,128)(2,1)S(1)} %all_to_all.11.got_ref, ...), custom_call_target="tpu_custom_call", output_to_operand_aliasing={{3}: (5, {})} | custom-call | tf_op jit(solution)/shard_map/combine/pallas_call | solution.py:353
  48.8 4.3 %collective-permute-start = (bf16[1,64,1024]{2,1,0:T(8,128)(2,1)S(1)}, bf16[1,64,1024]{2,1,0:T(8,128)(2,1)S(1)}, u32[]{:S(2)}, u32[]{:S(2)}) collective-permute-start(bf16[1,64,1024]{2,1,0:T(8,128)(2,1)S(1)} %get-tuple-element.28), channel_id=1, source_target_pairs={{0,1},{1,0},{2,3},{3,2},{4,5},{5,4},{6,7},{7,6},{8,9},{9,8},{10,11... | collective-permute-start | bytes 393224 | tf_op jit(solution)/shard_map/ppermute | solution.py:422
  53.1 0.1 collective-permute-start.1
  53.2 0.5 keep.2
  53.7 0.4 collective-permute-done
  54.1 3.0 %collective-permute-start.2 = (bf16[64,1024]{1,0:T(8,128)(2,1)S(1)}, bf16[64,1024]{1,0:T(8,128)(2,1)S(1)}, u32[]{:S(2)}, u32[]{:S(2)}) collective-permute-start(bf16[64,1024]{1,0:T(8,128)(2,1)S(1)} %add_bitcast_fusion), channel_id=1, source_target_pairs={{0,4},{1,5},{2,6},{3,7},{4,0},{5,1},{6,2},{7,3},{8,12},{9,13},{10,... | collective-permute-start | bytes 393224 | tf_op jit(solution)/shard_map/ppermute | solution.py:420
  57.1 1.2 %keep.3 = f32[3,64,1024]{2,1,0:T(8,128)S(1)} custom-call(bf16[64,1024]{1,0:T(8,128)(2,1)S(1)} %get-tuple-element.29.att_ref, bf16[1024,8192]{1,0:T(8,128)(2,1)S(1)} %get-tuple-element.27.w_ref), custom_call_target="tpu_custom_call" | custom-call | flops 402653184 | bytes 6291456 | tf_op jit(solution)/shard_map/keep/pallas_call | solution.py:380
  58.3 0.0 collective-permute-done.1
  58.3 0.1 fusion.7
  58.4 0.5 collective-permute-start.3
  58.9 2.3 %collective-permute-start.4 = (bf16[64,1024]{1,0:T(8,128)(2,1)S(1)}, bf16[64,1024]{1,0:T(8,128)(2,1)S(1)}, u32[]{:S(2)}, u32[]{:S(2)}) collective-permute-start(bf16[64,1024]{1,0:T(8,128)(2,1)S(1)} %get-tuple-element.32), channel_id=1, source_target_pairs={{0,6},{1,7},{2,0},{3,1},{4,2},{5,3},{6,4},{7,5},{8,14},{9,15},{10,... | collective-permute-start | bytes 393224 | tf_op jit(solution)/shard_map/ppermute | solution.py:420
  61.2 0.0 collective-permute-done.2
  61.2 2.9 %collective-permute-done.3 = bf16[64,1024]{1,0:T(8,128)(2,1)S(1)} collective-permute-done((bf16[64,1024]{1,0:T(8,128)(2,1)S(1)}, bf16[64,1024]{1,0:T(8,128)(2,1)S(1)}, u32[]{:S(2)}, u32[]{:S(2)}) %collective-permute-start.3) | collective-permute-done | bytes 131104 | tf_op jit(solution)/shard_map/ppermute | solution.py:420
  64.1 0.0 collective-permute-done.4
  64.1 0.7 %fusion.6 = bf16[64,1024]{1,0:T(8,128)(2,1)} fusion(f32[3,64,1024]{2,1,0:T(8,128)S(1)} %keep.3, bf16[64,1024]{1,0:T(8,128)(2,1)S(1)} %collective-permute-done.4, bf16[64,1024]{1,0:T(8,128)(2,1)S(1)} %collective-permute-done.3, bf16[64,1024]{1,0:T(8,128)(2,1)S(1)} %collective-permute-done.2, bf16[3,64,1024]{2,1,0:T(8,128)(2,1)S(1)} %collective-permute-done.1), kind=kLoop, calls=%fused_computation.9 | loop fusion | flops 589824 | bytes 917504 | tf_op jit(solution)/shard_map/convert_element_type | solution.py:433
  (1 shorter events, 0.0 us)
Async XLA Ops:
  0.0 22.8 %copy-start.1 = (bf16[128,1,256,128]{3,2,1,0:T(8,128)(2,1)S(1)}, bf16[128,1,256,128]{3,2,1,0:T(8,128)(2,1)}, u32[]{:S(2)}) copy-start(bf16[128,1,256,128]{3,2,1,0:T(8,128)(2,1)} %param.12) | copy-start | bytes 25165828
  0.0 22.8 %copy-start = (bf16[128,1,256,128]{3,2,1,0:T(8,128)(2,1)S(1)}, bf16[128,1,256,128]{3,2,1,0:T(8,128)(2,1)}, u32[]{:S(2)}) copy-start(bf16[128,1,256,128]{3,2,1,0:T(8,128)(2,1)} %param.11) | copy-start | bytes 25165828
  0.0 22.8 %copy-start.3 = (bf16[4,16,1,128]{3,1,2,0:T(8,128)(2,1)S(1)}, bf16[4,16,1,128]{3,1,2,0:T(8,128)(2,1)}, u32[]{:S(2)}) copy-start(bf16[4,16,1,128]{3,1,2,0:T(8,128)(2,1)} %param.10) | copy-start | bytes 49156
  0.0 22.8 %copy-start.2 = (bf16[4,16,1,128]{3,1,2,0:T(8,128)(2,1)S(1)}, bf16[4,16,1,128]{3,1,2,0:T(8,128)(2,1)}, u32[]{:S(2)}) copy-start(bf16[4,16,1,128]{3,1,2,0:T(8,128)(2,1)} %param.9) | copy-start | bytes 49156
  22.9 19.8 %copy-start.4 = (s32[128]{0:T(128)S(1)}, s32[128]{0:T(128)}, u32[]{:S(2)}) copy-start(s32[128]{0:T(128)} %get-tuple-element.18.place_ref) | copy-start | bytes 1540
  48.8 5.3 %collective-permute-start = (bf16[1,64,1024]{2,1,0:T(8,128)(2,1)S(1)}, bf16[1,64,1024]{2,1,0:T(8,128)(2,1)S(1)}, u32[]{:S(2)}, u32[]{:S(2)}) collective-permute-start(bf16[1,64,1024]{2,1,0:T(8,128)(2,1)S(1)} %get-tuple-element.28), channel_id=1, source_target_pairs={{0,1},{1,0},{2,3},{3,2},{4,5},{5,4},{6,7},{7,6},{8,9},{9,8},{10,11... | collective-permute-start | bytes 393224 | tf_op jit(solution)/shard_map/ppermute | solution.py:422
  53.1 5.2 %collective-permute-start.1 = (bf16[3,64,1024]{2,1,0:T(8,128)(2,1)S(1)}, bf16[3,64,1024]{2,1,0:T(8,128)(2,1)S(1)}, u32[]{:S(2)}, u32[]{:S(2)}) collective-permute-start(bf16[3,64,1024]{2,1,0:T(8,128)(2,1)S(1)} %get-tuple-element.30), channel_id=1, source_target_pairs={{0,1},{1,0},{2,3},{3,2},{4,5},{5,4},{6,7},{7,6},{8,9},{9,8},{10,11... | collective-permute-start | bytes 1179656 | tf_op jit(solution)/shard_map/ppermute | solution.py:423
  54.1 7.0 %collective-permute-start.2 = (bf16[64,1024]{1,0:T(8,128)(2,1)S(1)}, bf16[64,1024]{1,0:T(8,128)(2,1)S(1)}, u32[]{:S(2)}, u32[]{:S(2)}) collective-permute-start(bf16[64,1024]{1,0:T(8,128)(2,1)S(1)} %add_bitcast_fusion), channel_id=1, source_target_pairs={{0,4},{1,5},{2,6},{3,7},{4,0},{5,1},{6,2},{7,3},{8,12},{9,13},{10,... | collective-permute-start | bytes 393224 | tf_op jit(solution)/shard_map/ppermute | solution.py:420
  58.4 5.7 %collective-permute-start.3 = (bf16[64,1024]{1,0:T(8,128)(2,1)S(1)}, bf16[64,1024]{1,0:T(8,128)(2,1)S(1)}, u32[]{:S(2)}, u32[]{:S(2)}) collective-permute-start(bf16[64,1024]{1,0:T(8,128)(2,1)S(1)} %get-tuple-element.31), channel_id=1, source_target_pairs={{0,2},{1,3},{2,4},{3,5},{4,6},{5,7},{6,0},{7,1},{8,10},{9,11},{10,... | collective-permute-start | bytes 393224 | tf_op jit(solution)/shard_map/ppermute | solution.py:420
  58.9 5.2 %collective-permute-start.4 = (bf16[64,1024]{1,0:T(8,128)(2,1)S(1)}, bf16[64,1024]{1,0:T(8,128)(2,1)S(1)}, u32[]{:S(2)}, u32[]{:S(2)}) collective-permute-start(bf16[64,1024]{1,0:T(8,128)(2,1)S(1)} %get-tuple-element.32), channel_id=1, source_target_pairs={{0,6},{1,7},{2,0},{3,1},{4,2},{5,3},{6,4},{7,5},{8,14},{9,15},{10,... | collective-permute-start | bytes 393224 | tf_op jit(solution)/shard_map/ppermute | solution.py:420

commit v7 on v6

--- a/solution.py
+++ b/solution.py
@@ -61,8 +61,8 @@
 
 
 def prepare_kernel(
-    shifts, table_hbm, length_hbm, queries_hbm, w_hbm,
-    out_ref, place_hbm, q_ref, w_ref,
+    shifts, table_hbm, length_hbm, queries_hbm, k_hbm, v_hbm, w_hbm,
+    out_ref, place_hbm, q_ref, w_ref, fresh_ref, stat_ref, k_ref, v_ref,
     table_ref, length_ref, queries_ref, place_ref, meta_ref, count_ref, sems, w_sem,
 ):
     drafts, requests, group, head = queries_ref.shape
@@ -108,10 +108,20 @@
     def _():
         copy = weight_copy(w_hbm, w_ref, 0, EARLY, w_sem)
         copy.start()
+        news = [
+            pltpu.make_async_copy(k_hbm, k_ref, sems.at[4]),
+            pltpu.make_async_copy(v_hbm, v_ref, sems.at[5]),
+        ]
+        for new in news:
+            new.start()
+        for new in news:
+            new.wait()
+        for _ in draft_block(drafts, q_ref[...], k_ref, v_ref, fresh_ref, stat_ref):
+            pass
         copy.wait()
 
 
-def prepare(table, lengths, queries, w, block):
+def prepare(table, lengths, queries, new_keys, new_values, w, block):
     drafts, requests, group, head = queries.shape
     rows = drafts * group
     entries = table.shape[0]
@@ -121,22 +131,26 @@
     vmem = pl.BlockSpec(memory_space=pltpu.VMEM)
     return pl.pallas_call(
         functools.partial(prepare_kernel, shifts),
-        in_specs=[pl.BlockSpec(memory_space=pltpu.HBM)] * 4,
-        out_specs=[vmem, pl.BlockSpec(memory_space=pltpu.HBM), vmem, vmem],
+        in_specs=[pl.BlockSpec(memory_space=pltpu.HBM)] * 6,
+        out_specs=[vmem, pl.BlockSpec(memory_space=pltpu.HBM)] + [vmem] * 4,
         out_shape=[
             jax.ShapeDtypeStruct((lenders, each * rows + META, head), BF16),
             pltpu.HBM((entries,), jnp.int32),
             jax.ShapeDtypeStruct((requests, rows, head), BF16),
             pltpu.VMEM(w.shape, BF16),
+            pltpu.VMEM((requests, rows, head), F32),
+            pltpu.VMEM((2, requests, head), F32),
         ],
         scratch_shapes=[
+            pltpu.VMEM(new_keys.shape, BF16),
+            pltpu.VMEM(new_values.shape, BF16),
             pltpu.SMEM(table.shape, jnp.int32),
             pltpu.SMEM(lengths.shape, jnp.int32),
             pltpu.VMEM(queries.shape, BF16),
             pltpu.SMEM((entries,), jnp.int32),
             pltpu.VMEM((lenders, META, head), F32),
             pltpu.SMEM((lenders,), jnp.int32),
-            pltpu.SemaphoreType.DMA((4,)),
+            pltpu.SemaphoreType.DMA((6,)),
             pltpu.SemaphoreType.DMA,
         ],
         compiler_params=pltpu.CompilerParams(vmem_limit_bytes=8 * 1024 * 1024),
@@ -144,18 +158,17 @@
             flops=2 * 10**10, bytes_accessed=64 * 1024 * 1024, transcendentals=10**7
         ),
         name="prepare",
-    )(*(in_hbm(x) for x in (table, lengths, queries, w)))
+    )(*(in_hbm(x) for x in (table, lengths, queries, new_keys, new_values, w)))
 
 
 def attend_kernel(
-    drafts, ahead, behind, q_ref, k_ref, v_ref, own_ref, new_k_ref, new_v_ref, w_hbm, w_in,
-    out_ref, fresh_ref, stat_ref, w_ref, number_ref, info_ref, sem, w_sem,
+    rows, ahead, behind, q_ref, k_ref, v_ref, w_hbm, w_in,
+    out_ref, w_ref, number_ref, info_ref, sem, w_sem,
 ):
     others = weight_copy(w_hbm, w_ref, EARLY, w_ref.shape[0], w_sem)
     others.start()
 
     block, head = k_ref.shape[1:]
-    rows = own_ref.shape[1]
     lenders = out_ref.shape[0]
     each = (out_ref.shape[1] - META) // rows
     entries = lenders * each
@@ -179,13 +192,10 @@
     def here(i):
         return i // each, pl.ds(i % each * rows, rows), slice(None)
 
-    draft = draft_block(drafts, own_ref[...], new_k_ref, new_v_ref, fresh_ref, stat_ref)
     scores, soft, outs = {}, {}, {}
     peaks = jnp.zeros((rows, head), F32)
     totals = jnp.ones((rows, head), F32)
     for i in range(-ahead, entries + 2 * behind):
-        if i in (16, 28, 40, 52):
-            next(draft)
         if i + ahead < entries:
             n = i + ahead
             scores[n] = lax.dot_general(
@@ -223,18 +233,15 @@
     others.wait()
 
 
-def attend(q, keys, values, own, new_keys, new_values, w, w_part, drafts):
-    lenders = q.shape[0]
-    requests, rows, head = own.shape
+def attend(q, keys, values, w, w_part, rows):
+    lenders, _, head = q.shape
     vmem = pl.BlockSpec(memory_space=pltpu.VMEM)
     return pl.pallas_call(
-        functools.partial(attend_kernel, drafts, 8, 4),
-        in_specs=[vmem] * 6 + [pl.BlockSpec(memory_space=pltpu.HBM), vmem],
-        out_specs=[vmem] * 4,
+        functools.partial(attend_kernel, rows, 8, 4),
+        in_specs=[vmem] * 3 + [pl.BlockSpec(memory_space=pltpu.HBM), vmem],
+        out_specs=[vmem] * 2,
         out_shape=[
             jax.ShapeDtypeStruct(q.shape, BF16),
-            jax.ShapeDtypeStruct((requests, rows, head), F32),
-            jax.ShapeDtypeStruct((2, requests, head), F32),
             pltpu.VMEM(w.shape, BF16),
         ],
         scratch_shapes=[
@@ -243,10 +250,10 @@
             pltpu.SemaphoreType.DMA,
             pltpu.SemaphoreType.DMA,
         ],
-        input_output_aliases={7: 3},
+        input_output_aliases={4: 1},
         compiler_params=pltpu.CompilerParams(vmem_limit_bytes=8 * 1024 * 1024),
         name="attend",
-    )(q, keys, values, own, new_keys, new_values, in_hbm(w), w_part)
+    )(q, keys, values, in_hbm(w), w_part)
 
 
 def project_to(steps, other, att_ref, w_ref, out_ref):
@@ -262,14 +269,16 @@
 
 
 def combine_kernel(
-    drafts, place_ref, got_ref, fresh_ref, stat_ref, w_hbm, w_in,
-    far_ref, send_ref, att_ref, w_ref, arrived_ref, own_ref, rows_ref, w_sem,
+    drafts, place_ref, got_ref, fresh_in, stat_in, w_hbm, w_in, q_ref, k_ref, v_ref,
+    far_ref, send_ref, att_ref, w_ref, fresh_ref, stat_ref, arrived_ref, own_ref, rows_ref, w_sem,
 ):
     first = weight_copy(w_hbm, w_ref, 0, EARLY, w_sem)
 
     @pl.when(lax.axis_index("tp") & 1 == 1)
     def _():
         first.start()
+        for _ in draft_block(drafts, q_ref[...], k_ref, v_ref, fresh_ref, stat_ref):
+            pass
 
     requests, rows, head = fresh_ref.shape
     lenders = got_ref.shape[0]
@@ -344,7 +353,7 @@
     project_to(REST, True, att_ref, w_ref, send_ref)
 
 
-def combine(place, got, fresh, stat, w, w_part, drafts, tp):
+def combine(place, got, fresh, stat, w, w_part, own, new_keys, new_values, drafts, tp):
     requests, rows, head = fresh.shape
     deep, wide = w.shape
     tile = wide // tp
@@ -352,13 +361,15 @@
     vmem, smem = pl.BlockSpec(memory_space=pltpu.VMEM), pl.BlockSpec(memory_space=pltpu.SMEM)
     return pl.pallas_call(
         functools.partial(combine_kernel, drafts),
-        in_specs=[smem, vmem, vmem, vmem, pl.BlockSpec(memory_space=pltpu.HBM), vmem],
-        out_specs=[vmem] * 4,
+        in_specs=[smem, vmem, vmem, vmem, pl.BlockSpec(memory_space=pltpu.HBM)] + [vmem] * 4,
+        out_specs=[vmem] * 6,
         out_shape=[
             jax.ShapeDtypeStruct((1, tall, tile), BF16),
             jax.ShapeDtypeStruct((len(REST), tall, tile), BF16),
             jax.ShapeDtypeStruct((tall, deep), BF16),
             pltpu.VMEM(w.shape, BF16),
+            pltpu.VMEM(fresh.shape, F32),
+            pltpu.VMEM(stat.shape, F32),
         ],
         scratch_shapes=[
             pltpu.VMEM((place.shape[0], head), F32),
@@ -366,10 +377,10 @@
             pltpu.VMEM((requests * rows, head), F32),
             pltpu.SemaphoreType.DMA,
         ],
-        input_output_aliases={5: 3},
+        input_output_aliases={5: 3, 2: 4, 3: 5},
         compiler_params=pltpu.CompilerParams(vmem_limit_bytes=8 * 1024 * 1024),
         name="combine",
-    )(place, got, fresh, stat, in_hbm(w), w_part)
+    )(place, got, fresh, stat, in_hbm(w), w_part, own, new_keys, new_values)
 
 
 def keep(steps, att, w, tp):
@@ -398,22 +409,24 @@
     drafts, requests, heads, head = queries.shape
     pool, _, block, _ = key_pool.shape
     tp = lax.axis_size("tp")
-    payload, place, own, weight = prepare(block_table, context_len, queries, out_weight, block)
+    new_keys, new_values = new_keys.reshape(-1, head), new_values.reshape(-1, head)
+    payload, place, own, weight, fresh, stat = prepare(
+        block_table, context_len, queries, new_keys, new_values, out_weight, block
+    )
     asked = lax.all_to_all(payload, "inst", 0, 0, tiled=True)
-    answer, fresh, stat, weight = attend(
+    answer, weight = attend(
         asked,
         key_pool.reshape(pool, block, head),
         value_pool.reshape(pool, block, head),
-        own,
-        new_keys.reshape(-1, head),
-        new_values.reshape(-1, head),
         out_weight,
         weight,
-        drafts,
+        drafts * heads,
     )
     got = lax.all_to_all(answer, "inst", 0, 0, tiled=True)
 
-    far, send, att, weight = combine(place, got, fresh, stat, out_weight, weight, drafts, tp)
+    far, send, att, weight, _, _ = combine(
+        place, got, fresh, stat, out_weight, weight, own, new_keys, new_values, drafts, tp
+    )
     swap = [(i, i ^ 1) for i in range(tp)]
 
     def along(pair, step):

time: 65.1 us -> 65.1 us (level)
  Pallas kernels: 14.5 us -> 13.7 us
  starting transfers between devices: 10.1 us -> 10.9 us
    ppermute x1, starting transfers between devices: 4.29 us -> 5.07 us  [on_device(): other_far = lax.ppermute(far, 'tp', swap)]
where the time goes in v7:
time: 65.1 us; the launch traced here: 64.7 us
  blocking collectives  35.8 us (55%)
  Pallas kernels  13.7 us (21%)
  starting transfers between devices  10.9 us (17%)
  waiting for transfers between devices  3.35 us (5%)
  other arithmetic  0.82 us (1%)
    all_to_all x1, blocking collectives, on_device(): asked = lax.all_to_all(payload, 'inst', 0, 0, tiled=True)  20.8 us
    all_to_all x1, blocking collectives, on_device(): got = lax.all_to_all(answer, 'inst', 0, 0, tiled=True)  15 us
    ppermute x3, starting transfers between devices, along(): lax.ppermute(pair.astype(BF16), 'tp', [(i, (i + 2 * step) % tp) for i in...  5.74 us
    pallas_call x1, Pallas kernels, combine(): pl.pallas_call(functools.partial(combine_kernel, drafts), in_specs=[smem,...  5.52 us
    ppermute x1, starting transfers between devices, on_device(): other_far = lax.ppermute(far, 'tp', swap)  5.07 us
    pallas_call x1, Pallas kernels, attend(): pl.pallas_call(functools.partial(attend_kernel, rows, 8, 4), in_specs=[vm...  4.54 us
    ppermute x3, waiting for transfers between devices, along(): lax.ppermute(pair.astype(BF16), 'tp', [(i, (i + 2 * step) % tp) for i in...  2.94 us
    pallas_call x1, Pallas kernels, prepare(): pl.pallas_call(functools.partial(prepare_kernel, shifts), in_specs=[pl.Bl...  2 us
  transfers between devices with their start and end apart: 5, of which 2 were waited for; matrix products, arithmetic and copies ran while one was open for 0% of the time, Pallas kernels for 3%

profile of v7, /device:TPU:1, one launch (start us, length us, event | category | flops | bytes accessed | tf_op | source)
XLA Modules:
  0.0 64.7 jit_solution(2545023620564237783)
XLA Ops:
  0.0 0.0 copy-start
  0.0 0.0 copy-start.1
  0.0 2.0 %prepare.1 = (bf16[16,264,128]{2,1,0:T(8,128)(2,1)S(1)}, s32[128]{0:T(128)}, bf16[16,32,128]{2,1,0:T(8,128)(2,1)S(1)}, bf16[1024,8192]{1,0:T(8,128)(2,1)S(1)}, f...) custom-call(s32[128]{0:T(128)} %table_hbm.1, s32[16]{0:T(128)} %length_hbm.1, bf16[4,16,8,128]{3,2,1,0:T(8,128)(2,1)} %queries_hbm.1, ...), custom_call_target="tpu_custom_call" | custom-call | flops 20000000000 | bytes 67108864 | tf_op jit(solution)/shard_map/prepare/pallas_call | solution.py:132
  2.0 20.8 %all_to_all.10.q_ref = bf16[16,264,128]{2,1,0:T(8,128)(2,1)S(1)} all-to-all(bf16[16,264,128]{2,1,0:T(8,128)(2,1)S(1)} %get-tuple-element.19), channel_id=1, replica_groups=mesh['inst'=16,'tp'=8] {'inst'}, dimensions={0} | all-to-all | bytes 2162688 | tf_op jit(solution)/shard_map/all_to_all | solution.py:416
  22.8 0.0 copy-done
  22.8 0.0 copy-done.1
  22.8 0.0 copy-start.2
  22.8 0.0 copy-start.3
  22.8 0.0 copy-start.4
  22.8 4.5 %attend.1 = (bf16[16,264,128]{2,1,0:T(8,128)(2,1)S(1)}, bf16[1024,8192]{1,0:T(8,128)(2,1)S(1)}) custom-call(bf16[16,264,128]{2,1,0:T(8,128)(2,1)S(1)} %all_to_all.10.q_ref, bf16[128,256,128]{2,1,0:T(8,128)(2,1)S(1)} %bitcast.21, bf16[128,256,128]{2,1,0:T(8,128)(2,1)S(1)} %bitcast.22, bf16[1024,8192]{1,0:T(8,128)(2,1)} %w_hbm.5, ...), custom_call_target="tpu_custom_call", output_to_operand_aliasing={{1}: (4, {})} | custom-call | tf_op jit(solution)/shard_map/attend/pallas_call | solution.py:239
  27.4 15.0 %all_to_all.11.got_ref = bf16[16,264,128]{2,1,0:T(8,128)(2,1)S(1)} all-to-all(bf16[16,264,128]{2,1,0:T(8,128)(2,1)S(1)} %get-tuple-element.21), channel_id=1, replica_groups=mesh['inst'=16,'tp'=8] {'inst'}, dimensions={0} | all-to-all | bytes 2162688 | tf_op jit(solution)/shard_map/all_to_all | solution.py:425
  42.4 0.0 copy-done.2
  42.4 0.0 copy-done.3
  42.4 0.0 copy-done.4
  42.4 5.5 %combine.1 = (bf16[1,64,1024]{2,1,0:T(8,128)(2,1)S(1)}, bf16[3,64,1024]{2,1,0:T(8,128)(2,1)S(1)}, bf16[64,1024]{1,0:T(8,128)(2,1)S(1)}, bf16[1024,8192]{1,0:T(8,...) custom-call(s32[128]{0:T(128)S(1)} %copy-done.4, ...), custom_call_target="tpu_custom_call", output_to_operand_aliasing={{3}: (5, {}), {4}: (2, {}), {5}: (3, {})} | custom-call | tf_op jit(solution)/shard_map/combine/pallas_call | solution.py:362
  47.9 5.1 %collective-permute-start = (bf16[1,64,1024]{2,1,0:T(8,128)(2,1)S(1)}, bf16[1,64,1024]{2,1,0:T(8,128)(2,1)S(1)}, u32[]{:S(2)}, u32[]{:S(2)}) collective-permute-start(bf16[1,64,1024]{2,1,0:T(8,128)(2,1)S(1)} %get-tuple-element.28), channel_id=1, source_target_pairs={{0,1},{1,0},{2,3},{3,2},{4,5},{5,4},{6,7},{7,6},{8,9},{9,8},{10,11... | collective-permute-start | bytes 393224 | tf_op jit(solution)/shard_map/ppermute | solution.py:435
  53.0 0.1 collective-permute-start.1
  53.1 0.5 keep.2
  53.6 0.4 collective-permute-done
  54.0 3.0 %collective-permute-start.2 = (bf16[64,1024]{1,0:T(8,128)(2,1)S(1)}, bf16[64,1024]{1,0:T(8,128)(2,1)S(1)}, u32[]{:S(2)}, u32[]{:S(2)}) collective-permute-start(bf16[64,1024]{1,0:T(8,128)(2,1)S(1)} %add_bitcast_fusion), channel_id=1, source_target_pairs={{0,4},{1,5},{2,6},{3,7},{4,0},{5,1},{6,2},{7,3},{8,12},{9,13},{10,... | collective-permute-start | bytes 393224 | tf_op jit(solution)/shard_map/ppermute | solution.py:433
  57.0 1.2 %keep.3 = f32[3,64,1024]{2,1,0:T(8,128)S(1)} custom-call(bf16[64,1024]{1,0:T(8,128)(2,1)S(1)} %get-tuple-element.29.att_ref, bf16[1024,8192]{1,0:T(8,128)(2,1)S(1)} %get-tuple-element.27.w_ref), custom_call_target="tpu_custom_call" | custom-call | flops 402653184 | bytes 6291456 | tf_op jit(solution)/shard_map/keep/pallas_call | solution.py:391
  58.2 0.0 collective-permute-done.1
  58.2 0.1 fusion.7
  58.3 0.5 collective-permute-start.3
  58.8 2.3 %collective-permute-start.4 = (bf16[64,1024]{1,0:T(8,128)(2,1)S(1)}, bf16[64,1024]{1,0:T(8,128)(2,1)S(1)}, u32[]{:S(2)}, u32[]{:S(2)}) collective-permute-start(bf16[64,1024]{1,0:T(8,128)(2,1)S(1)} %get-tuple-element.32), channel_id=1, source_target_pairs={{0,6},{1,7},{2,0},{3,1},{4,2},{5,3},{6,4},{7,5},{8,14},{9,15},{10,... | collective-permute-start | bytes 393224 | tf_op jit(solution)/shard_map/ppermute | solution.py:433
  61.0 0.0 collective-permute-done.2
  61.0 2.9 %collective-permute-done.3 = bf16[64,1024]{1,0:T(8,128)(2,1)S(1)} collective-permute-done((bf16[64,1024]{1,0:T(8,128)(2,1)S(1)}, bf16[64,1024]{1,0:T(8,128)(2,1)S(1)}, u32[]{:S(2)}, u32[]{:S(2)}) %collective-permute-start.3) | collective-permute-done | bytes 131104 | tf_op jit(solution)/shard_map/ppermute | solution.py:433
  64.0 0.0 collective-permute-done.4
  64.0 0.7 %fusion.6 = bf16[64,1024]{1,0:T(8,128)(2,1)} fusion(f32[3,64,1024]{2,1,0:T(8,128)S(1)} %keep.3, bf16[64,1024]{1,0:T(8,128)(2,1)S(1)} %collective-permute-done.4, bf16[64,1024]{1,0:T(8,128)(2,1)S(1)} %collective-permute-done.3, bf16[64,1024]{1,0:T(8,128)(2,1)S(1)} %collective-permute-done.2, bf16[3,64,1024]{2,1,0:T(8,128)(2,1)S(1)} %collective-permute-done.1), kind=kLoop, calls=%fused_computation.9 | loop fusion | flops 589824 | bytes 917504 | tf_op jit(solution)/shard_map/convert_element_type | solution.py:446
  (1 shorter events, 0.0 us)
Async XLA Ops:
  0.0 22.8 %copy-start = (bf16[128,1,256,128]{3,2,1,0:T(8,128)(2,1)S(1)}, bf16[128,1,256,128]{3,2,1,0:T(8,128)(2,1)}, u32[]{:S(2)}) copy-start(bf16[128,1,256,128]{3,2,1,0:T(8,128)(2,1)} %param.11) | copy-start | bytes 25165828
  0.0 22.8 %copy-start.1 = (bf16[128,1,256,128]{3,2,1,0:T(8,128)(2,1)S(1)}, bf16[128,1,256,128]{3,2,1,0:T(8,128)(2,1)}, u32[]{:S(2)}) copy-start(bf16[128,1,256,128]{3,2,1,0:T(8,128)(2,1)} %param.12) | copy-start | bytes 25165828
  22.8 19.6 %copy-start.2 = (bf16[4,16,1,128]{3,1,2,0:T(8,128)(2,1)S(1)}, bf16[4,16,1,128]{3,1,2,0:T(8,128)(2,1)}, u32[]{:S(2)}) copy-start(bf16[4,16,1,128]{3,1,2,0:T(8,128)(2,1)} %param.9) | copy-start | bytes 49156
  22.8 19.6 %copy-start.3 = (bf16[4,16,1,128]{3,1,2,0:T(8,128)(2,1)S(1)}, bf16[4,16,1,128]{3,1,2,0:T(8,128)(2,1)}, u32[]{:S(2)}) copy-start(bf16[4,16,1,128]{3,1,2,0:T(8,128)(2,1)} %param.10) | copy-start | bytes 49156
  22.8 19.6 %copy-start.4 = (s32[128]{0:T(128)S(1)}, s32[128]{0:T(128)}, u32[]{:S(2)}) copy-start(s32[128]{0:T(128)} %get-tuple-element.18.place_ref) | copy-start | bytes 1540
  47.9 6.1 %collective-permute-start = (bf16[1,64,1024]{2,1,0:T(8,128)(2,1)S(1)}, bf16[1,64,1024]{2,1,0:T(8,128)(2,1)S(1)}, u32[]{:S(2)}, u32[]{:S(2)}) collective-permute-start(bf16[1,64,1024]{2,1,0:T(8,128)(2,1)S(1)} %get-tuple-element.28), channel_id=1, source_target_pairs={{0,1},{1,0},{2,3},{3,2},{4,5},{5,4},{6,7},{7,6},{8,9},{9,8},{10,11... | collective-permute-start | bytes 393224 | tf_op jit(solution)/shard_map/ppermute | solution.py:435
  53.0 5.2 %collective-permute-start.1 = (bf16[3,64,1024]{2,1,0:T(8,128)(2,1)S(1)}, bf16[3,64,1024]{2,1,0:T(8,128)(2,1)S(1)}, u32[]{:S(2)}, u32[]{:S(2)}) collective-permute-start(bf16[3,64,1024]{2,1,0:T(8,128)(2,1)S(1)} %get-tuple-element.30), channel_id=1, source_target_pairs={{0,1},{1,0},{2,3},{3,2},{4,5},{5,4},{6,7},{7,6},{8,9},{9,8},{10,11... | collective-permute-start | bytes 1179656 | tf_op jit(solution)/shard_map/ppermute | solution.py:436
  54.0 7.0 %collective-permute-start.2 = (bf16[64,1024]{1,0:T(8,128)(2,1)S(1)}, bf16[64,1024]{1,0:T(8,128)(2,1)S(1)}, u32[]{:S(2)}, u32[]{:S(2)}) collective-permute-start(bf16[64,1024]{1,0:T(8,128)(2,1)S(1)} %add_bitcast_fusion), channel_id=1, source_target_pairs={{0,4},{1,5},{2,6},{3,7},{4,0},{5,1},{6,2},{7,3},{8,12},{9,13},{10,... | collective-permute-start | bytes 393224 | tf_op jit(solution)/shard_map/ppermute | solution.py:433
  58.3 5.7 %collective-permute-start.3 = (bf16[64,1024]{1,0:T(8,128)(2,1)S(1)}, bf16[64,1024]{1,0:T(8,128)(2,1)S(1)}, u32[]{:S(2)}, u32[]{:S(2)}) collective-permute-start(bf16[64,1024]{1,0:T(8,128)(2,1)S(1)} %get-tuple-element.31), channel_id=1, source_target_pairs={{0,2},{1,3},{2,4},{3,5},{4,6},{5,7},{6,0},{7,1},{8,10},{9,11},{10,... | collective-permute-start | bytes 393224 | tf_op jit(solution)/shard_map/ppermute | solution.py:433
  58.8 5.2 %collective-permute-start.4 = (bf16[64,1024]{1,0:T(8,128)(2,1)S(1)}, bf16[64,1024]{1,0:T(8,128)(2,1)S(1)}, u32[]{:S(2)}, u32[]{:S(2)}) collective-permute-start(bf16[64,1024]{1,0:T(8,128)(2,1)S(1)} %get-tuple-element.32), channel_id=1, source_target_pairs={{0,6},{1,7},{2,0},{3,1},{4,2},{5,3},{6,4},{7,5},{8,14},{9,15},{10,... | collective-permute-start | bytes 393224 | tf_op jit(solution)/shard_map/ppermute | solution.py:433
